TPU v7x, 128 devices: a whole 4x4x4 slice. The times are simulated.
128 devices in a mesh: expert: 2 (over z_lo), rep: 4 (over y), seq: 16 (over z_hi, x, core).
Axes of the slice: x: 4, y: 4, z: 4 (z_hi: 2, z_lo: 2; z = z_hi * 2 + z_lo), core: 2. Of those that a mesh axis runs over, the one named last changes fastest.
Arguments:
- query_in: bfloat16 [2, 8, 2048, 4096], P('expert', 'rep', 'seq'), may hold values from -64 to 64
- key_in: bfloat16 [2, 8, 2048, 4096], P('expert', 'rep', 'seq'), may hold values from -64 to 64
- value_in: bfloat16 [2, 8, 2048, 4096], P('expert', 'rep', 'seq'), may hold values from -12 to 12
- sample_noise: bfloat16 [2, 8, 2048, 4096], P('expert', 'rep', 'seq'), may hold values from -12 to 12
- old_velocity: bfloat16 [2, 8, 2048, 4096], P('expert', 'rep', 'seq'), may hold values from -12 to 12
- gate_scale: bfloat16 [2, 8, 4096], P('expert', 'rep'), may hold values from 0.5 to 1.5
- rewards: float32 [2, 8], P(None, 'rep'), may hold values from -12 to 12
- group_ids: int32 [2, 8], P(None, 'rep'), may hold values from 0 to 3
- timesteps: int32 [2, 8], P(None, 'rep'), may hold values from 150 to 899, as said below
- counts: int32 [2, 4], P(None, 'rep'), may hold values from 0 to 2, as said below
Outputs:
- grad_query: bfloat16 [2, 8, 2048, 4096], P('expert', 'rep', 'seq')
- grad_key: bfloat16 [2, 8, 2048, 4096], P('expert', 'rep', 'seq')
- grad_value: bfloat16 [2, 8, 2048, 4096], P('expert', 'rep', 'seq')
- grad_gate: bfloat16 [2, 8, 4096], P('expert', 'rep')
- log_ratio: bfloat16 [2, 8], P('expert', 'rep')
Inputs may be any that keep to these rules, and one draw needn't show every extreme that they name: Steps of expert set 0 have timesteps of 875 or more, steps of set 1 below 875. `counts`: every replica of one expert set, chosen from the seed, keeps all 2 slots; some replica of the other set keeps none.
All inputs are finite; a program needn't handle non-finite values.
Results may differ from a plain program's by a relative error of at most 0.012.
The roundings to bfloat16 on the way count: a program that leaves them out, or rounds other values in their place, can miss the bound.
Values may be sent and summed in bfloat16 or wider, within the bound.
No kernel may reach another device: no remote copies, remote signals or barrier semaphores. Data moves between devices by JAX's collectives and lax.ppermute only.
A program may use at most 256 MiB of HBM per device.

v0:
```python
import jax
import jax.numpy as jnp
from jax import lax
from jax.sharding import PartitionSpec as P

HD = 128
GROUPS = 4


def step_coef(timesteps):
    fraction = timesteps.astype(jnp.float32) / 1000.0
    sigma_level = 0.7 * jnp.sqrt(fraction / (1.0 - fraction))
    return jnp.sqrt(jnp.float32(0.1)) / sigma_level


def to_heads(matrix, groups):
    return matrix.reshape(matrix.shape[0], groups, matrix.shape[1] // groups)


def attention_forward(heads_query, heads_key, heads_value):
    length, heads_here, head_size = heads_query.shape
    block_rows = min(512, length)
    scale_factor = head_size ** (-0.5)

    def one_block(start):
        rows_query = lax.dynamic_slice_in_dim(heads_query, start, block_rows, 0)
        scores = (
            jnp.einsum("qhd,khd->hqk", rows_query, heads_key, preferred_element_type=jnp.float32)
            * scale_factor
        )
        row_max = jnp.max(scores, axis=2, keepdims=True)
        weights = jnp.exp(scores - row_max)
        probabilities = (weights / jnp.sum(weights, axis=2, keepdims=True)).astype(jnp.bfloat16)
        attended = jnp.einsum(
            "hqk,khd->qhd", probabilities, heads_value, preferred_element_type=jnp.float32
        ).astype(jnp.bfloat16)
        return (probabilities, attended)

    starts = jnp.arange(length // block_rows, dtype=jnp.int32) * block_rows
    probabilities, attended = lax.map(one_block, starts)
    return (probabilities, attended.reshape(length, heads_here, head_size))


def attention_backward(heads_query, heads_key, heads_value, probabilities, attended, grad_attended):
    length, heads_here, head_size = heads_query.shape
    block_rows = probabilities.shape[2]
    scale_factor = head_size ** (-0.5)

    def one_block(totals, block_items):
        block_probs, start = block_items
        rows_query = lax.dynamic_slice_in_dim(heads_query, start, block_rows, 0)
        rows_out = lax.dynamic_slice_in_dim(attended, start, block_rows, 0)
        rows_grad = lax.dynamic_slice_in_dim(grad_attended, start, block_rows, 0)
        row_dot = jnp.sum(rows_grad.astype(jnp.float32) * rows_out.astype(jnp.float32), axis=2)
        grad_probs = jnp.einsum(
            "qhd,khd->hqk", rows_grad, heads_value, preferred_element_type=jnp.float32
        )
        grad_scores = (
            block_probs.astype(jnp.float32) * (grad_probs - row_dot.T[:, :, None])
        ).astype(jnp.bfloat16)
        grad_rows = (
            jnp.einsum("hqk,khd->qhd", grad_scores, heads_key, preferred_element_type=jnp.float32)
            * scale_factor
        ).astype(jnp.bfloat16)
        key_total = totals[0] + jnp.einsum(
            "hqk,qhd->khd", grad_scores, rows_query, preferred_element_type=jnp.float32
        )
        value_total = totals[1] + jnp.einsum(
            "hqk,qhd->khd", block_probs, rows_grad, preferred_element_type=jnp.float32
        )
        return ((key_total, value_total), grad_rows)

    zero_field = jnp.zeros((length, heads_here, head_size), jnp.float32)
    starts = jnp.arange(length // block_rows, dtype=jnp.int32) * block_rows
    (key_total, value_total), grad_rows = lax.scan(
        one_block, (zero_field, zero_field), (probabilities, starts)
    )
    grad_query = grad_rows.reshape(length, heads_here, head_size)
    return (
        grad_query,
        (key_total * scale_factor).astype(jnp.bfloat16),
        value_total.astype(jnp.bfloat16),
    )


def log_ratio(coefficient, noise_rows, velocity_gap, entries):
    partial_sum = jnp.sum(
        2.0 * coefficient * noise_rows * velocity_gap
        + coefficient * coefficient * velocity_gap * velocity_gap
    )
    return -lax.psum(partial_sum, "seq") / (2.0 * entries)


def one_step(
    query_in, key_in, value_in, sample_noise, old_velocity, gate_scale, coefficient, weight
):
    groups = lax.axis_size("seq")
    tokens_here, full_width = query_in.shape
    length = tokens_here * groups
    piece_width = full_width // groups
    heads_here = piece_width // HD
    gate_full = gate_scale.astype(jnp.float32)
    arrived = (
        lax.all_to_all(to_heads(query_in, groups), "seq", split_axis=1, concat_axis=0, tiled=True),
        lax.all_to_all(to_heads(key_in, groups), "seq", split_axis=1, concat_axis=0, tiled=True),
        lax.all_to_all(to_heads(value_in, groups), "seq", split_axis=1, concat_axis=0, tiled=True),
    )
    heads_query = arrived[0].reshape(length, heads_here, HD)
    heads_key = arrived[1].reshape(length, heads_here, HD)
    heads_value = arrived[2].reshape(length, heads_here, HD)
    probabilities, attended = attention_forward(heads_query, heads_key, heads_value)
    mixed_back = lax.all_to_all(
        attended.reshape(length, 1, piece_width), "seq", split_axis=0, concat_axis=1, tiled=True
    )
    mixed_rows = mixed_back.reshape(tokens_here, full_width).astype(jnp.float32)
    noise_rows = sample_noise.astype(jnp.float32)
    velocity_gap = gate_full[None, :] * mixed_rows - old_velocity.astype(jnp.float32)
    ratio_log = log_ratio(coefficient, noise_rows, velocity_gap, length * full_width)
    grad_gap = (
        weight
        * jnp.exp(ratio_log)
        * (coefficient * noise_rows + coefficient * coefficient * velocity_gap)
    )
    grad_gate = lax.psum(jnp.sum(grad_gap * mixed_rows, axis=0), "seq").astype(jnp.bfloat16)
    grad_out = (grad_gap * gate_full[None, :]).astype(jnp.bfloat16)
    grad_attended = lax.all_to_all(
        to_heads(grad_out, groups), "seq", split_axis=1, concat_axis=0, tiled=True
    ).reshape(length, heads_here, HD)
    grad_query, grad_key, grad_value = attention_backward(
        heads_query, heads_key, heads_value, probabilities, attended, grad_attended
    )
    returned = (
        lax.all_to_all(
            grad_query.reshape(length, 1, piece_width),
            "seq",
            split_axis=0,
            concat_axis=1,
            tiled=True,
        ),
        lax.all_to_all(
            grad_key.reshape(length, 1, piece_width), "seq", split_axis=0, concat_axis=1, tiled=True
        ),
        lax.all_to_all(
            grad_value.reshape(length, 1, piece_width),
            "seq",
            split_axis=0,
            concat_axis=1,
            tiled=True,
        ),
    )
    return (
        returned[0].reshape(tokens_here, full_width),
        returned[1].reshape(tokens_here, full_width),
        returned[2].reshape(tokens_here, full_width),
        grad_gate,
        ratio_log.astype(jnp.bfloat16),
    )


def store(results, slot_index, computed):
    return tuple(
        (
            lax.dynamic_update_index_in_dim(buffer, fresh_item, slot_index, 0)
            for buffer, fresh_item in zip(results, computed)
        )
    )


def masked_ratio(computed, kept_value):
    return computed[:4] + ((computed[4].astype(jnp.float32) * kept_value).astype(jnp.bfloat16),)


def local(
    query_in,
    key_in,
    value_in,
    sample_noise,
    old_velocity,
    gate_scale,
    rewards,
    group_ids,
    timesteps,
    counts,
):
    slot_count = query_in.shape[1]
    tokens_here = query_in.shape[2]
    full_width = query_in.shape[3]
    expert_at = lax.axis_index("expert")
    set_counts = counts[:, 0]
    kept_mask = (jnp.arange(slot_count, dtype=jnp.int32)[None, :] < set_counts[:, None]).astype(
        jnp.float32
    )
    choose = (group_ids[..., None] == jnp.arange(GROUPS, dtype=jnp.int32)).astype(jnp.float32)
    live_mask = choose * kept_mask[..., None]
    number, reward_sum, square = lax.psum(
        (
            jnp.sum(live_mask, axis=(0, 1)),
            jnp.sum(live_mask * rewards[..., None], axis=(0, 1)),
            jnp.sum(live_mask * (rewards * rewards)[..., None], axis=(0, 1)),
        ),
        "rep",
    )
    group_mean = reward_sum / jnp.maximum(number, 1.0)
    spread = square / jnp.maximum(number, 1.0) - group_mean * group_mean
    centre = jnp.sum(choose * group_mean, axis=-1)
    group_scale = jnp.sum(choose * jnp.sqrt(jnp.maximum(spread, 1.0)), axis=-1)
    advantage = (rewards - centre) / group_scale
    weight_all = kept_mask * advantage
    coefficient = step_coef(timesteps)

    def run_slot(slot_index, results):

        def pick_slot(stacked):
            return lax.dynamic_index_in_dim(stacked[0], slot_index, 0, keepdims=False)

        computed = one_step(
            pick_slot(query_in),
            pick_slot(key_in),
            pick_slot(value_in),
            pick_slot(sample_noise),
            pick_slot(old_velocity),
            pick_slot(gate_scale),
            coefficient[expert_at, slot_index],
            weight_all[expert_at, slot_index],
        )
        return store(results, slot_index, masked_ratio(computed, kept_mask[expert_at, slot_index]))

    blank_results = (
        jnp.zeros((slot_count, tokens_here, full_width), jnp.bfloat16),
        jnp.zeros((slot_count, tokens_here, full_width), jnp.bfloat16),
        jnp.zeros((slot_count, tokens_here, full_width), jnp.bfloat16),
        jnp.zeros((slot_count, full_width), jnp.bfloat16),
        jnp.zeros((slot_count,), jnp.bfloat16),
    )
    results = lax.fori_loop(0, slot_count, run_slot, blank_results)
    return (
        results[0][None],
        results[1][None],
        results[2][None],
        results[3][None],
        results[4][None],
    )


def solution(mesh):
    placed = (
        P("expert", "rep", "seq", None),
        P("expert", "rep", "seq", None),
        P("expert", "rep", "seq", None),
        P("expert", "rep", "seq", None),
        P("expert", "rep", "seq", None),
        P("expert", "rep", None),
        P(None, "rep"),
        P(None, "rep"),
        P(None, "rep"),
        P(None, "rep"),
    )
    return jax.shard_map(
        local,
        mesh=mesh,
        in_specs=placed,
        out_specs=(
            P("expert", "rep", "seq", None),
            P("expert", "rep", "seq", None),
            P("expert", "rep", "seq", None),
            P("expert", "rep", None),
            P("expert", "rep"),
        ),
        check_vma=False,
    )
```

profile of v0, /device:TPU:0, one launch (start us, length us, event | category | flops | bytes accessed | tf_op | source)
XLA Modules:
  0.0 1037.9 jit_solution(17344902583222337583)
XLA Ops:
  2.9 10.8 %all-reduce = (f32[4]{0:T(128)S(1)}, f32[4]{0:T(128)S(1)}, f32[4]{0:T(128)S(1)}) all-reduce(f32[4]{0:T(128)S(1)} %get-tuple-element.687, f32[4]{0:T(128)S(1)} %get-tuple-element.686, f32[4]{0:T(128)S(1)} %get-tuple-element.685), channel_id=1, replica_groups=mesh['expert'=2,'rep'=4,'seq'=16] {'rep'}, use_global_device_ids=true, to_apply=%region_1.0 | all-reduce | flops 12 | bytes 96 | tf_op jit(solution)/shard_map/psum | solution.py:195
  15.4 1021.9 %while.106 = (s32[]{:T(128)}, bf16[2,128,4096]{2,1,0:T(8,128)(2,1)}, bf16[2,128,4096]{2,1,0:T(8,128)(2,1)}, bf16[2,128,4096]{2,1,0:T(8,128)(2,1)}, bf16[2,4096]{...) while((s32[]{:T(128)}, bf16[2,128,4096]{2,1,0:T(8,128)(2,1)}, ...), condition=%wide.region_20.21_spmd, body=%wide.region_8.20_spmd.sunk | while | flops 3260421120 | bytes 331632448 | solution.py:235
  18.0 7.7 all-to-all-start.1
  28.3 15.4 %all-to-all-done.1 = bf16[128,16,256]{0,2,1:T(8,128)(2,1)S(1)} async-done(((bf16[128,16,256]{0,2,1:T(8,128)(2,1)}), bf16[128,16,256]{0,2,1:T(8,128)(2,1)S(1)}, u32[]{:S(2)}, u32[]{:S(2)}) %all-to-all-start.1) | async-done | bytes 1048608 | tf_op jit(solution)/shard_map/while/body/eval_jaxpr/all_to_all | solution.py:105
  52.3 13.0 %all-to-all-done.2 = bf16[128,16,256]{0,2,1:T(8,128)(2,1)S(1)} async-done(((bf16[128,16,256]{0,2,1:T(8,128)(2,1)}), bf16[128,16,256]{0,2,1:T(8,128)(2,1)S(1)}, u32[]{:S(2)}, u32[]{:S(2)}) %all-to-all-start.2) | async-done | bytes 1048608 | tf_op jit(solution)/shard_map/while/body/eval_jaxpr/all_to_all | solution.py:106
  92.9 67.5 %while.107 = (s32[]{:T(128)}, bf16[4,2,512,2048]{3,2,1,0:T(8,128)(2,1)}, bf16[4,512,2,128]{3,1,2,0:T(8,128)(2,1)}, s32[4]{0:T(128)S(1)}, bf16[2048,2,128]{0,2,1:...) while((s32[]{:T(128)}, ...), condition=%wide.region_12.12_spmd, body=%wide.region_9.11_spmd.sunk | while | flops 1084360704 | bytes 31990936 | solution.py:40
  95.1 7.2 fusion.102
  128.9 7.2 fusion.102
  164.1 7.4 reshape.306
  172.0 12.6 %reduce.15 = bf16[2048,256]{1,0:T(8,128)(2,1)} reduce(bf16[2048,1,256]{2,1,0:T(2,128)(2,1)} %reshape.306, bf16[]{:T(256)} %broadcast.205), dimensions={1}, to_apply=%reshape.268.reduce_sub_computation | reduce | bytes 2097154 | tf_op jit(solution)/shard_map/while/body/eval_jaxpr/reshape;while/body/eval_jaxpr/reshape | solution.py:113
  199.0 10.2 all-to-all-done.3
  221.6 33.9 %psum.52 = f32[]{:T(128)} all-reduce(f32[]{:T(128)} %fusion.95), channel_id=1, replica_groups=mesh['expert'=2,'rep'=4,'seq'=16] {'seq'}, use_global_device_ids=true, to_apply=%region_14.14 | all-reduce | flops 1 | bytes 8 | tf_op jit(solution)/shard_map/while/body/eval_jaxpr/psum | solution.py:91
  267.6 15.7 %all-to-all-done.4 = bf16[128,16,256]{2,0,1:T(8,128)(2,1)} async-done(((bf16[128,16,256]{2,0,1:T(8,128)(2,1)}), bf16[128,16,256]{2,0,1:T(8,128)(2,1)}, u32[]{:S(2)}, u32[]{:S(2)}) %all-to-all-start.4) | async-done | bytes 1048608 | tf_op jit(solution)/shard_map/while/body/eval_jaxpr/all_to_all | solution.py:126
  285.5 85.8 %while.108 = (s32[]{:T(128)}, f32[2048,2,128]{0,2,1:T(8,128)}, f32[2048,2,128]{0,2,1:T(8,128)S(1)}, bf16[4,512,2,128]{3,2,1,0:T(2,128)(2,1)}, s32[4]{0:T(128)S(1...) while((s32[]{:T(128)}, f32[2048,2,128]{0,2,1:T(8,128)}, ...), condition=%wide.region_17.17_spmd.clone, body=%wide.region_15.16_spmd.clone.sunk | while | flops 2158754816 | bytes 50865384 | solution.py:75
  383.2 14.2 %all-to-all-done.6 = bf16[16,2,16384]{2,1,0:T(2,128)(2,1)} async-done(((bf16[16,2,16384]{2,1,0:T(2,128)(2,1)}), bf16[16,2,16384]{2,1,0:T(2,128)(2,1)}, u32[]{:S(2)}, u32[]{:S(2)}) %all-to-all-start.6) | async-done | bytes 1048608 | tf_op jit(solution)/shard_map/while/body/eval_jaxpr/all_to_all | solution.py:143
  402.8 11.6 %reduce.16 = bf16[2048,256]{1,0:T(8,128)(2,1)} reduce(bf16[2048,1,256]{2,1,0:T(2,128)(2,1)S(1)} %reshape.311, bf16[]{:T(256)} %broadcast.207), dimensions={1}, to_apply=%reshape.270.reduce_sub_computation | reduce | bytes 2097154 | tf_op jit(solution)/shard_map/while/body/eval_jaxpr/reshape;while/body/eval_jaxpr/reshape | solution.py:134
  427.8 71.3 %psum.53 = bf16[4096]{0:T(1024)(128)(2,1)S(1)} all-reduce(f32[4096]{0:T(1024)S(1)} %fusion.97), channel_id=1, replica_groups=mesh['expert'=2,'rep'=4,'seq'=16] {'seq'}, use_global_device_ids=true, to_apply=%region_19.19 | all-reduce | flops 4096 | bytes 24576 | tf_op jit(solution)/shard_map/while/body/eval_jaxpr/psum | solution.py:124
  537.6 15.4 %all-to-all-done.1 = bf16[128,16,256]{0,2,1:T(8,128)(2,1)S(1)} async-done(((bf16[128,16,256]{0,2,1:T(8,128)(2,1)}), bf16[128,16,256]{0,2,1:T(8,128)(2,1)S(1)}, u32[]{:S(2)}, u32[]{:S(2)}) %all-to-all-start.1) | async-done | bytes 1048608 | tf_op jit(solution)/shard_map/while/body/eval_jaxpr/all_to_all | solution.py:105
  561.6 13.0 %all-to-all-done.2 = bf16[128,16,256]{0,2,1:T(8,128)(2,1)S(1)} async-done(((bf16[128,16,256]{0,2,1:T(8,128)(2,1)}), bf16[128,16,256]{0,2,1:T(8,128)(2,1)S(1)}, u32[]{:S(2)}, u32[]{:S(2)}) %all-to-all-start.2) | async-done | bytes 1048608 | tf_op jit(solution)/shard_map/while/body/eval_jaxpr/all_to_all | solution.py:106
  602.2 67.5 %while.107 = (s32[]{:T(128)}, bf16[4,2,512,2048]{3,2,1,0:T(8,128)(2,1)}, bf16[4,512,2,128]{3,1,2,0:T(8,128)(2,1)}, s32[4]{0:T(128)S(1)}, bf16[2048,2,128]{0,2,1:...) while((s32[]{:T(128)}, ...), condition=%wide.region_12.12_spmd, body=%wide.region_9.11_spmd.sunk | while | flops 1084360704 | bytes 31990936 | solution.py:40
  604.4 7.2 fusion.102
  621.3 7.2 fusion.102
  638.2 7.2 fusion.102
  673.4 7.4 reshape.306
  681.3 12.6 %reduce.15 = bf16[2048,256]{1,0:T(8,128)(2,1)} reduce(bf16[2048,1,256]{2,1,0:T(2,128)(2,1)} %reshape.306, bf16[]{:T(256)} %broadcast.205), dimensions={1}, to_apply=%reshape.268.reduce_sub_computation | reduce | bytes 2097154 | tf_op jit(solution)/shard_map/while/body/eval_jaxpr/reshape;while/body/eval_jaxpr/reshape | solution.py:113
  708.3 10.2 all-to-all-done.3
  730.8 33.9 %psum.52 = f32[]{:T(128)} all-reduce(f32[]{:T(128)} %fusion.95), channel_id=1, replica_groups=mesh['expert'=2,'rep'=4,'seq'=16] {'seq'}, use_global_device_ids=true, to_apply=%region_14.14 | all-reduce | flops 1 | bytes 8 | tf_op jit(solution)/shard_map/while/body/eval_jaxpr/psum | solution.py:91
  776.9 15.7 %all-to-all-done.4 = bf16[128,16,256]{2,0,1:T(8,128)(2,1)} async-done(((bf16[128,16,256]{2,0,1:T(8,128)(2,1)}), bf16[128,16,256]{2,0,1:T(8,128)(2,1)}, u32[]{:S(2)}, u32[]{:S(2)}) %all-to-all-start.4) | async-done | bytes 1048608 | tf_op jit(solution)/shard_map/while/body/eval_jaxpr/all_to_all | solution.py:126
  794.8 85.8 %while.108 = (s32[]{:T(128)}, f32[2048,2,128]{0,2,1:T(8,128)}, f32[2048,2,128]{0,2,1:T(8,128)S(1)}, bf16[4,512,2,128]{3,2,1,0:T(2,128)(2,1)}, s32[4]{0:T(128)S(1...) while((s32[]{:T(128)}, f32[2048,2,128]{0,2,1:T(8,128)}, ...), condition=%wide.region_17.17_spmd.clone, body=%wide.region_15.16_spmd.clone.sunk | while | flops 2158754816 | bytes 50865384 | solution.py:75
  892.5 14.2 %all-to-all-done.6 = bf16[16,2,16384]{2,1,0:T(2,128)(2,1)} async-done(((bf16[16,2,16384]{2,1,0:T(2,128)(2,1)}), bf16[16,2,16384]{2,1,0:T(2,128)(2,1)}, u32[]{:S(2)}, u32[]{:S(2)}) %all-to-all-start.6) | async-done | bytes 1048608 | tf_op jit(solution)/shard_map/while/body/eval_jaxpr/all_to_all | solution.py:143
  912.1 11.6 %reduce.16 = bf16[2048,256]{1,0:T(8,128)(2,1)} reduce(bf16[2048,1,256]{2,1,0:T(2,128)(2,1)S(1)} %reshape.311, bf16[]{:T(256)} %broadcast.207), dimensions={1}, to_apply=%reshape.270.reduce_sub_computation | reduce | bytes 2097154 | tf_op jit(solution)/shard_map/while/body/eval_jaxpr/reshape;while/body/eval_jaxpr/reshape | solution.py:134
  937.1 71.3 %psum.53 = bf16[4096]{0:T(1024)(128)(2,1)S(1)} all-reduce(f32[4096]{0:T(1024)S(1)} %fusion.97), channel_id=1, replica_groups=mesh['expert'=2,'rep'=4,'seq'=16] {'seq'}, use_global_device_ids=true, to_apply=%region_19.19 | all-reduce | flops 4096 | bytes 24576 | tf_op jit(solution)/shard_map/while/body/eval_jaxpr/psum | solution.py:124
  (359 shorter events, 534.3 us)
Async XLA Ops:
  18.0 25.7 %all-to-all-start.1 = ((bf16[128,16,256]{0,2,1:T(8,128)(2,1)}), bf16[128,16,256]{0,2,1:T(8,128)(2,1)S(1)}, u32[]{:S(2)}, u32[]{:S(2)}) async-start(bf16[128,16,256]{0,2,1:T(8,128)(2,1)} %bitcast.210), calls=%async_computation.1 | async-start | bytes 2097152 | tf_op jit(solution)/shard_map/while/body/eval_jaxpr/all_to_all | solution.py:105
  43.7 21.6 %all-to-all-start.2 = ((bf16[128,16,256]{0,2,1:T(8,128)(2,1)}), bf16[128,16,256]{0,2,1:T(8,128)(2,1)S(1)}, u32[]{:S(2)}, u32[]{:S(2)}) async-start(bf16[128,16,256]{0,2,1:T(8,128)(2,1)} %bitcast.212), calls=%async_computation.2 | async-start | bytes 2097152 | tf_op jit(solution)/shard_map/while/body/eval_jaxpr/all_to_all | solution.py:106
  65.3 5.7 copy-start.10
  65.3 22.3 %all-to-all-start = ((bf16[128,16,256]{0,2,1:T(8,128)(2,1)}), bf16[128,16,256]{0,2,1:T(8,128)(2,1)}, u32[]{:S(2)}, u32[]{:S(2)}) async-start(bf16[128,16,256]{0,2,1:T(8,128)(2,1)} %bitcast.208), calls=%async_computation | async-start | bytes 2097152 | tf_op jit(solution)/shard_map/while/body/eval_jaxpr/all_to_all | solution.py:104
  74.3 121.9 %copy-start.5 = (bf16[1,1,128,4096]{2,3,1,0:T(8,128)(2,1)}, bf16[1,1,128,4096]{2,3,1,0:T(8,128)(2,1)S(1)}, u32[]{:S(2)}) copy-start(bf16[1,1,128,4096]{2,3,1,0:T(8,128)(2,1)S(1)} %copy.233) | copy-start | bytes 3145732 | tf_op jit(solution)/shard_map/while
  160.4 11.1 %copy-start.2 = (bf16[2048,2,128]{2,0,1:T(8,128)(2,1)}, bf16[2048,2,128]{2,0,1:T(8,128)(2,1)S(1)}, u32[]{:S(2)}) copy-start(bf16[2048,2,128]{2,0,1:T(8,128)(2,1)S(1)} %get-tuple-element.1209) | copy-start | bytes 3145732 | tf_op jit(solution)/shard_map/while
  184.6 6.6 copy-start.7
  186.8 22.3 %all-to-all-start.3 = ((bf16[16,2,16384]{2,1,0:T(2,128)(2,1)}), bf16[16,2,16384]{2,1,0:T(2,128)(2,1)}, u32[]{:S(2)}, u32[]{:S(2)}) async-start(bf16[16,2,16384]{2,1,0:T(2,128)(2,1)} %reshape.307), calls=%async_computation.3 | async-start | bytes 2097152 | tf_op jit(solution)/shard_map/while/body/eval_jaxpr/all_to_all | solution.py:112
  260.8 22.5 %all-to-all-start.4 = ((bf16[128,16,256]{2,0,1:T(8,128)(2,1)}), bf16[128,16,256]{2,0,1:T(8,128)(2,1)}, u32[]{:S(2)}, u32[]{:S(2)}) async-start(bf16[128,16,256]{2,0,1:T(8,128)(2,1)} %fusion.96), calls=%async_computation.4 | async-start | bytes 2097152 | tf_op jit(solution)/shard_map/while/body/eval_jaxpr/all_to_all | solution.py:126
  375.1 22.3 %all-to-all-start.6 = ((bf16[16,2,16384]{2,1,0:T(2,128)(2,1)}), bf16[16,2,16384]{2,1,0:T(2,128)(2,1)}, u32[]{:S(2)}, u32[]{:S(2)}) async-start(bf16[16,2,16384]{2,1,0:T(2,128)(2,1)} %reshape.314), calls=%async_computation.6 | async-start | bytes 2097152 | tf_op jit(solution)/shard_map/while/body/eval_jaxpr/all_to_all | solution.py:143
  382.1 19.7 %copy-start.12 = (bf16[4,512,2,128]{3,2,1,0:T(2,128)(2,1)S(1)}, bf16[4,512,2,128]{3,2,1,0:T(2,128)(2,1)}, u32[]{:S(2)}) copy-start(bf16[4,512,2,128]{3,2,1,0:T(2,128)(2,1)} %get-tuple-element.1017) | copy-start | bytes 3145732 | tf_op jit(solution)/shard_map/while
  397.4 22.3 %all-to-all-start.7 = ((bf16[16,2,16384]{2,1,0:T(2,128)(2,1)}), bf16[16,2,16384]{2,1,0:T(2,128)(2,1)}, u32[]{:S(2)}, u32[]{:S(2)}) async-start(bf16[16,2,16384]{2,1,0:T(2,128)(2,1)} %reshape.316), calls=%async_computation.7 | async-start | bytes 2097152 | tf_op jit(solution)/shard_map/while/body/eval_jaxpr/all_to_all | solution.py:140
  414.4 9.7 copy-start.15
  414.4 10.4 %copy-start.4 = (f32[128,16,1,256]{0,3,1,2:T(8,128)S(1)}, f32[128,16,1,256]{0,3,1,2:T(8,128)}, u32[]{:S(2)}) copy-start(f32[128,16,1,256]{0,3,1,2:T(8,128)} %copy-done.3) | copy-start | bytes 6291460 | tf_op jit(solution)/shard_map/while
  414.4 10.4 %copy-start.6 = (bf16[1,1,128,4096]{2,3,1,0:T(8,128)(2,1)S(1)}, bf16[1,1,128,4096]{2,3,1,0:T(8,128)(2,1)}, u32[]{:S(2)}) copy-start(bf16[1,1,128,4096]{2,3,1,0:T(8,128)(2,1)} %copy-done.5) | copy-start | bytes 3145732 | tf_op jit(solution)/shard_map/while
  419.7 94.4 %all-to-all-start.5 = ((bf16[16,2,16384]{2,1,0:T(2,128)(2,1)}), bf16[16,2,16384]{2,1,0:T(2,128)(2,1)}, u32[]{:S(2)}, u32[]{:S(2)}) async-start(bf16[16,2,16384]{2,1,0:T(2,128)(2,1)} %reshape.312), calls=%async_computation.5 | async-start | bytes 2097152 | tf_op jit(solution)/shard_map/while/body/eval_jaxpr/all_to_all | solution.py:133
  530.6 22.4 %all-to-all-start.1 = ((bf16[128,16,256]{0,2,1:T(8,128)(2,1)}), bf16[128,16,256]{0,2,1:T(8,128)(2,1)S(1)}, u32[]{:S(2)}, u32[]{:S(2)}) async-start(bf16[128,16,256]{0,2,1:T(8,128)(2,1)} %bitcast.210), calls=%async_computation.1 | async-start | bytes 2097152 | tf_op jit(solution)/shard_map/while/body/eval_jaxpr/all_to_all | solution.py:105
  553.0 21.6 %all-to-all-start.2 = ((bf16[128,16,256]{0,2,1:T(8,128)(2,1)}), bf16[128,16,256]{0,2,1:T(8,128)(2,1)S(1)}, u32[]{:S(2)}, u32[]{:S(2)}) async-start(bf16[128,16,256]{0,2,1:T(8,128)(2,1)} %bitcast.212), calls=%async_computation.2 | async-start | bytes 2097152 | tf_op jit(solution)/shard_map/while/body/eval_jaxpr/all_to_all | solution.py:106
  574.6 5.7 copy-start.10
  574.6 22.3 %all-to-all-start = ((bf16[128,16,256]{0,2,1:T(8,128)(2,1)}), bf16[128,16,256]{0,2,1:T(8,128)(2,1)}, u32[]{:S(2)}, u32[]{:S(2)}) async-start(bf16[128,16,256]{0,2,1:T(8,128)(2,1)} %bitcast.208), calls=%async_computation | async-start | bytes 2097152 | tf_op jit(solution)/shard_map/while/body/eval_jaxpr/all_to_all | solution.py:104
  583.5 121.9 %copy-start.5 = (bf16[1,1,128,4096]{2,3,1,0:T(8,128)(2,1)}, bf16[1,1,128,4096]{2,3,1,0:T(8,128)(2,1)S(1)}, u32[]{:S(2)}) copy-start(bf16[1,1,128,4096]{2,3,1,0:T(8,128)(2,1)S(1)} %copy.233) | copy-start | bytes 3145732 | tf_op jit(solution)/shard_map/while
  669.7 11.1 %copy-start.2 = (bf16[2048,2,128]{2,0,1:T(8,128)(2,1)}, bf16[2048,2,128]{2,0,1:T(8,128)(2,1)S(1)}, u32[]{:S(2)}) copy-start(bf16[2048,2,128]{2,0,1:T(8,128)(2,1)S(1)} %get-tuple-element.1209) | copy-start | bytes 3145732 | tf_op jit(solution)/shard_map/while
  693.9 6.6 copy-start.7
  696.1 22.3 %all-to-all-start.3 = ((bf16[16,2,16384]{2,1,0:T(2,128)(2,1)}), bf16[16,2,16384]{2,1,0:T(2,128)(2,1)}, u32[]{:S(2)}, u32[]{:S(2)}) async-start(bf16[16,2,16384]{2,1,0:T(2,128)(2,1)} %reshape.307), calls=%async_computation.3 | async-start | bytes 2097152 | tf_op jit(solution)/shard_map/while/body/eval_jaxpr/all_to_all | solution.py:112
  770.1 22.5 %all-to-all-start.4 = ((bf16[128,16,256]{2,0,1:T(8,128)(2,1)}), bf16[128,16,256]{2,0,1:T(8,128)(2,1)}, u32[]{:S(2)}, u32[]{:S(2)}) async-start(bf16[128,16,256]{2,0,1:T(8,128)(2,1)} %fusion.96), calls=%async_computation.4 | async-start | bytes 2097152 | tf_op jit(solution)/shard_map/while/body/eval_jaxpr/all_to_all | solution.py:126
  884.4 22.3 %all-to-all-start.6 = ((bf16[16,2,16384]{2,1,0:T(2,128)(2,1)}), bf16[16,2,16384]{2,1,0:T(2,128)(2,1)}, u32[]{:S(2)}, u32[]{:S(2)}) async-start(bf16[16,2,16384]{2,1,0:T(2,128)(2,1)} %reshape.314), calls=%async_computation.6 | async-start | bytes 2097152 | tf_op jit(solution)/shard_map/while/body/eval_jaxpr/all_to_all | solution.py:143
  891.4 19.7 %copy-start.12 = (bf16[4,512,2,128]{3,2,1,0:T(2,128)(2,1)S(1)}, bf16[4,512,2,128]{3,2,1,0:T(2,128)(2,1)}, u32[]{:S(2)}) copy-start(bf16[4,512,2,128]{3,2,1,0:T(2,128)(2,1)} %get-tuple-element.1017) | copy-start | bytes 3145732 | tf_op jit(solution)/shard_map/while
  906.7 22.3 %all-to-all-start.7 = ((bf16[16,2,16384]{2,1,0:T(2,128)(2,1)}), bf16[16,2,16384]{2,1,0:T(2,128)(2,1)}, u32[]{:S(2)}, u32[]{:S(2)}) async-start(bf16[16,2,16384]{2,1,0:T(2,128)(2,1)} %reshape.316), calls=%async_computation.7 | async-start | bytes 2097152 | tf_op jit(solution)/shard_map/while/body/eval_jaxpr/all_to_all | solution.py:140
  923.7 9.7 copy-start.15
  923.7 10.4 %copy-start.4 = (f32[128,16,1,256]{0,3,1,2:T(8,128)S(1)}, f32[128,16,1,256]{0,3,1,2:T(8,128)}, u32[]{:S(2)}) copy-start(f32[128,16,1,256]{0,3,1,2:T(8,128)} %copy-done.3) | copy-start | bytes 6291460 | tf_op jit(solution)/shard_map/while
  923.7 10.4 %copy-start.6 = (bf16[1,1,128,4096]{2,3,1,0:T(8,128)(2,1)S(1)}, bf16[1,1,128,4096]{2,3,1,0:T(8,128)(2,1)}, u32[]{:S(2)}) copy-start(bf16[1,1,128,4096]{2,3,1,0:T(8,128)(2,1)} %copy-done.5) | copy-start | bytes 3145732 | tf_op jit(solution)/shard_map/while
  929.0 94.4 %all-to-all-start.5 = ((bf16[16,2,16384]{2,1,0:T(2,128)(2,1)}), bf16[16,2,16384]{2,1,0:T(2,128)(2,1)}, u32[]{:S(2)}, u32[]{:S(2)}) async-start(bf16[16,2,16384]{2,1,0:T(2,128)(2,1)} %reshape.312), calls=%async_computation.5 | async-start | bytes 2097152 | tf_op jit(solution)/shard_map/while/body/eval_jaxpr/all_to_all | solution.py:133
  (27 other events, 84.5 us)
where the time goes:
time: 1040 us
  blocking collectives  221 us (21%)
  local copies, waits for them, and re-layouts  218 us (21%)
  matrix products  198 us (19%)
  waiting for transfers between devices  150 us (14%)
  other arithmetic  141 us (14%)
  starting transfers between devices  71.8 us (7%)
  loops' own time  37.6 us (4%)
    psum x2, blocking collectives, one_step(): lax.psum(jnp.sum(grad_gap * mixed_rows, axis=0), 'seq').astype(jnp.bfloat16)  143 us
    psum x2, blocking collectives, log_ratio(): return -lax.psum(partial_sum, 'seq') / (2.0 * entries)  67.8 us
    while x106, local copies, waits for them, and re-layouts  61.7 us
    sub x8, matrix products, one_block(): weights = jnp.exp(scores - row_max)  57.5 us
    dot_general x8, matrix products, one_block(): jnp.einsum('qhd,khd->hqk', rows_grad, heads_value, preferred_element_type...  46.7 us
    dynamic_update_slice x8, other arithmetic, attention_forward(): probabilities, attended = lax.map(one_block, starts)  43.7 us
    dot_general x8, matrix products, one_block(): jnp.einsum('hqk,qhd->khd', grad_scores, rows_query, preferred_element_typ...  40.8 us
    all_to_all x2, waiting for transfers between devices, one_step(): lax.all_to_all(to_heads(grad_out, groups), 'seq', split_axis=1, concat_ax...  31.5 us
  transfers between devices with their start and end apart: 16, of which 14 were waited for; matrix products, arithmetic and copies ran while one was open for 13% of the time, Pallas kernels for 0%

commit v1 on v0

v1 whole, which is shorter than its diff:
```python
import functools

import jax
import jax.numpy as jnp
from jax import lax
from jax.experimental import pallas as pl
from jax.experimental.pallas import tpu as pltpu
from jax.sharding import PartitionSpec as P

HD = 128
GROUPS = 4
SIDE = 16
F32 = jnp.float32
BF16 = jnp.bfloat16
NN = (((1,), (0,)), ((), ()))
NT = (((1,), (1,)), ((), ()))
VMEM_LIMIT = 48 * 1024 * 1024


def step_coef(timesteps):
    fraction = timesteps.astype(F32) / 1000.0
    sigma_level = 0.7 * jnp.sqrt(fraction / (1.0 - fraction))
    return jnp.sqrt(jnp.float32(0.1)) / sigma_level


def dot(left, right, dims=NN):
    return lax.dot_general(left, right, dims, preferred_element_type=F32)


def fold_rows(values, reduce):
    rows, columns = values.shape
    return reduce(values.reshape(rows // 8, 8, columns), axis=0)


def pack_body(
    slot, coef_ref, query_ref, key_ref, value_ref, noise_ref, old_ref, out_ref, misfit_ref
):
    pieces = out_ref.shape[0]
    width = out_ref.shape[3]
    coefficient = coef_ref[slot]

    @pl.when(pl.program_id(0) == 0)
    def _():
        misfit_ref[...] = jnp.zeros_like(misfit_ref)

    total = misfit_ref[...]
    for piece in range(pieces):
        columns = slice(piece * width, (piece + 1) * width)
        out_ref[piece, 0] = query_ref[0, 0, :, columns]
        out_ref[piece, 1] = key_ref[0, 0, :, columns]
        out_ref[piece, 2] = value_ref[0, 0, :, columns]
        noise = noise_ref[0, 0, :, columns].astype(F32)
        shift = coefficient * old_ref[0, 0, :, columns].astype(F32)
        out_ref[piece, 3] = (noise - shift).astype(BF16)
        total = total + fold_rows(shift * (shift - 2.0 * noise), jnp.sum)
    misfit_ref[...] = total


def pack(slot, coefficient, arrays, groups):
    _, _, tokens, full_width = arrays[0].shape
    width = full_width // groups
    pieces = 4
    rows = pl.BlockSpec((1, 1, tokens, pieces * width), lambda i: (0, slot, 0, i))
    return pl.pallas_call(
        functools.partial(pack_body, slot),
        grid=(groups // pieces,),
        out_shape=(
            jax.ShapeDtypeStruct((groups, 4, tokens, width), BF16),
            jax.ShapeDtypeStruct((8, width), F32),
        ),
        in_specs=[pl.BlockSpec(memory_space=pltpu.SMEM)] + [rows] * 5,
        out_specs=(
            pl.BlockSpec((pieces, 4, tokens, width), lambda i: (i, 0, 0, 0)),
            pl.BlockSpec((8, width), lambda i: (0, 0)),
        ),
        compiler_params=pltpu.CompilerParams(vmem_limit_bytes=VMEM_LIMIT),
        cost_estimate=pl.CostEstimate(
            flops=6 * tokens * full_width,
            bytes_accessed=18 * tokens * full_width,
            transcendentals=0,
        ),
    )(coefficient, *arrays)


def attention_body(
    slot,
    block_rows,
    chunk,
    coef_ref,
    query_ref,
    key_ref,
    value_ref,
    field_ref,
    gate_ref,
    misfit_ref,
    out_ref,
    q_rows,
    k_rows,
    v_rows,
    k_cols,
    v_cols,
    field_cols,
    scores,
    weights,
    key_total,
    value_total,
    gate_total,
    misfit_total,
):
    length = q_rows.shape[0]
    pieces = out_ref.shape[0]
    tokens = length // pieces
    scale_factor = HD ** (-0.5)
    log2e = 1.4426950408889634
    coefficient = coef_ref[slot]
    q_rows[...] = query_ref[...].reshape(length, HD)
    k_rows[...] = key_ref[...].reshape(length, HD)
    v_rows[...] = value_ref[...].reshape(length, HD)
    k_cols[...] = k_rows[...].T
    v_cols[...] = v_rows[...].T
    field_cols[...] = field_ref[...].reshape(length, HD).T
    gate = gate_ref[...]
    gate_total[...] = jnp.zeros_like(gate_total)
    misfit_total[...] = jnp.zeros_like(misfit_total)
    chunks = [slice(at, at + chunk) for at in range(0, length, chunk)]

    def one_block(index, _):
        first = index == 0
        start = pl.multiple_of(index * block_rows, block_rows)
        rows_query = q_rows[pl.ds(start, block_rows), :]
        top = jnp.full((8, block_rows), -jnp.inf, F32)
        for part in chunks:
            block_scores = dot(k_rows[part, :], rows_query, NT)
            scores[part, :] = block_scores
            top = jnp.maximum(top, fold_rows(block_scores, jnp.max))
        row_max = jnp.max(top, axis=0, keepdims=True) * (scale_factor * log2e)
        sums = jnp.zeros((8, block_rows), F32)
        mixed = jnp.zeros((HD, block_rows), F32)
        for part in chunks:
            raised = jnp.exp2(scores[part, :] * (scale_factor * log2e) - row_max)
            sums = sums + fold_rows(raised, jnp.sum)
            rounded = raised.astype(BF16)
            weights[part, :] = rounded
            mixed = mixed + dot(v_cols[:, part], rounded)
        inverse = 1.0 / jnp.sum(sums, axis=0, keepdims=True)
        attended = (mixed * inverse).astype(BF16).astype(F32)
        field = field_cols[:, pl.ds(start, block_rows)].astype(F32)
        moved = coefficient * (gate * attended)
        misfit_total[...] += moved * (2.0 * field + moved)
        grad_gap = coefficient * (field + moved)
        gate_total[...] += grad_gap * attended
        grad_cols = (grad_gap * gate * inverse).astype(BF16)
        grad_rows = grad_cols.T
        row_dot = jnp.sum(grad_cols.astype(F32) * attended, axis=0, keepdims=True)
        grad_query = jnp.zeros((HD, block_rows), F32)
        for part in chunks:
            rounded = weights[part, :]
            grad_probs = dot(v_rows[part, :], grad_cols)
            grad_scores = (rounded.astype(F32) * (grad_probs - row_dot)).astype(BF16)
            grad_query = grad_query + dot(k_cols[:, part], grad_scores)
            value_part = dot(rounded, grad_rows)
            key_part = dot(grad_scores, rows_query)
            value_total[part, :] = jnp.where(first, value_part, value_total[part, :] + value_part)
            key_total[part, :] = jnp.where(first, key_part, key_total[part, :] + key_part)
        held = block_rows // tokens
        out_ref[pl.ds(index * held, held), 0:tokens, :] = (
            (grad_query.T * scale_factor).astype(BF16).reshape(held, tokens, HD)
        )
        return 0

    lax.fori_loop(0, length // block_rows, one_block, 0)
    out_ref[:, tokens : 2 * tokens, :] = (
        (key_total[...] * scale_factor).astype(BF16).reshape(pieces, tokens, HD)
    )
    out_ref[:, 2 * tokens : 3 * tokens, :] = (
        value_total[...].astype(BF16).reshape(pieces, tokens, HD)
    )

    def row_of(values):
        total = values[:, 0:HD]
        for at in range(HD, values.shape[1], HD):
            total = total + values[:, at : at + HD]
        return jnp.sum(total.T, axis=0, keepdims=True)

    gate_row = row_of(gate_total[...])
    misfit_row = row_of(misfit_total[...]) + jnp.sum(misfit_ref[...], axis=0, keepdims=True)
    rest = misfit_row
    side = []
    for _ in range(3):
        side.append(rest.astype(BF16).astype(F32))
        rest = rest - side[-1]
    gate_high = gate_row.astype(BF16).astype(F32)
    row_at = lax.broadcasted_iota(jnp.int32, (SIDE, HD), 0)
    rows = jnp.zeros((SIDE, HD), F32)
    for at, row in enumerate([gate_high, gate_row - gate_high] + side):
        rows = jnp.where(row_at == at, row, rows)
    out_ref[:, 3 * tokens :, :] = jnp.broadcast_to(
        rows.astype(BF16)[None], (pieces, SIDE, HD)
    )


def attention(slot, coefficient, arrived, gate_column, misfit):
    groups, _, tokens, width = arrived.shape
    length = groups * tokens
    heads_here = width // HD
    block_rows, chunk = 512, 512

    def field(which):
        return pl.BlockSpec((groups, 1, tokens, HD), lambda h: (0, which, 0, h))

    return pl.pallas_call(
        functools.partial(attention_body, slot, block_rows, chunk),
        grid=(heads_here,),
        out_shape=jax.ShapeDtypeStruct((groups, 3 * tokens + SIDE, width), BF16),
        in_specs=[pl.BlockSpec(memory_space=pltpu.SMEM)]
        + [field(which) for which in range(4)]
        + [
            pl.BlockSpec((HD, 1), lambda h: (h, 0)),
            pl.BlockSpec((8, HD), lambda h: (0, h)),
        ],
        out_specs=pl.BlockSpec((groups, 3 * tokens + SIDE, HD), lambda h: (0, 0, h)),
        scratch_shapes=[pltpu.VMEM((length, HD), BF16)] * 3
        + [pltpu.VMEM((HD, length), BF16)] * 3
        + [
            pltpu.VMEM((length, block_rows), F32),
            pltpu.VMEM((length, block_rows), BF16),
            pltpu.VMEM((length, HD), F32),
            pltpu.VMEM((length, HD), F32),
            pltpu.VMEM((HD, block_rows), F32),
            pltpu.VMEM((HD, block_rows), F32),
        ],
        compiler_params=pltpu.CompilerParams(vmem_limit_bytes=VMEM_LIMIT),
        cost_estimate=pl.CostEstimate(
            flops=heads_here * 24 * length * length * HD,
            bytes_accessed=14 * length * width,
            transcendentals=heads_here * length * length,
        ),
    )(coefficient, arrived, arrived, arrived, arrived, gate_column, misfit)


def unpack_body(slot, entries, weight_ref, main_ref, side_ref, *refs):
    query_ref, key_ref, value_ref, gate_ref, log_ref = refs[-5:]
    pieces = main_ref.shape[0]
    width = main_ref.shape[2]
    tokens = query_ref.shape[2]
    side = side_ref[...].astype(F32)
    misfit = jnp.sum(side[:, 2:5, :])
    ratio_log = jnp.full((1, HD), -misfit / (2.0 * entries), F32)
    log_ref[...] = jnp.broadcast_to(ratio_log, log_ref.shape)
    factor = weight_ref[slot] * jnp.exp(ratio_log)
    factor = jnp.concatenate([factor] * (width // HD), axis=1)
    gate_ref[...] = (side[:, 0, :] + side[:, 1, :]) * factor
    for piece in range(pieces):
        columns = slice(piece * width, (piece + 1) * width)
        for which, out_ref in enumerate((query_ref, key_ref, value_ref)):
            rows = main_ref[piece, which * tokens : (which + 1) * tokens, :].astype(F32)
            out_ref[0, 0, :, columns] = (rows * factor).astype(BF16)


def unpack(slot, slots, weight, returned, previous):
    groups, rows, width = returned.shape
    tokens = (rows - SIDE) // 3
    pieces = 4
    whole = jax.ShapeDtypeStruct((1, slots, tokens, groups * width), BF16)
    part = pl.BlockSpec((1, 1, tokens, pieces * width), lambda i: (0, slot, 0, i))
    held = [] if previous is None else list(previous)
    return pl.pallas_call(
        functools.partial(unpack_body, slot, groups * tokens * groups * width),
        grid=(groups // pieces,),
        out_shape=(
            whole,
            whole,
            whole,
            jax.ShapeDtypeStruct((groups, width), F32),
            jax.ShapeDtypeStruct((8, HD), F32),
        ),
        in_specs=[
            pl.BlockSpec(memory_space=pltpu.SMEM),
            pl.BlockSpec((pieces, 3 * tokens, width), lambda i: (i, 0, 0)),
            pl.BlockSpec((groups, SIDE, width), lambda i: (0, 3 * tokens // SIDE, 0)),
        ]
        + [pl.BlockSpec(memory_space=pl.ANY) for _ in held],
        out_specs=(
            part,
            part,
            part,
            pl.BlockSpec((groups, width), lambda i: (0, 0)),
            pl.BlockSpec((8, HD), lambda i: (0, 0)),
        ),
        input_output_aliases={3 + at: at for at in range(len(held))},
        compiler_params=pltpu.CompilerParams(vmem_limit_bytes=VMEM_LIMIT),
        cost_estimate=pl.CostEstimate(
            flops=3 * tokens * groups * width,
            bytes_accessed=12 * tokens * groups * width,
            transcendentals=0,
        ),
    )(weight, returned, returned, *held)


def exchange(pieces):
    return lax.all_to_all(pieces, "seq", split_axis=0, concat_axis=0, tiled=True)


def sum_over_replicas(values):
    replicas = lax.axis_size("rep")
    total = values
    for shift in range(1, replicas):
        total = total + lax.ppermute(
            values, "rep", [(at, (at + shift) % replicas) for at in range(replicas)]
        )
    return total


def local(
    query_in,
    key_in,
    value_in,
    sample_noise,
    old_velocity,
    gate_scale,
    rewards,
    group_ids,
    timesteps,
    counts,
):
    slots = query_in.shape[1]
    tokens = query_in.shape[2]
    full_width = query_in.shape[3]
    groups = lax.axis_size("seq")
    width = full_width // groups
    expert_at = lax.axis_index("expert")

    def own_expert(both):
        return lax.dynamic_index_in_dim(both, expert_at, 0, keepdims=False)

    coefficient = step_coef(own_expert(timesteps))
    arrays = (query_in, key_in, value_in, sample_noise, old_velocity)
    gate_here = lax.dynamic_slice_in_dim(
        gate_scale[0], lax.axis_index("seq") * width, width, 1
    ).astype(F32)

    kept_mask = (
        jnp.arange(slots, dtype=jnp.int32)[None, :] < counts[:, 0][:, None]
    ).astype(F32)
    choose = (group_ids[..., None] == jnp.arange(GROUPS, dtype=jnp.int32)).astype(F32)
    live_mask = choose * kept_mask[..., None]
    sums = sum_over_replicas(
        jnp.stack(
            (
                jnp.sum(live_mask, axis=(0, 1)),
                jnp.sum(live_mask * rewards[..., None], axis=(0, 1)),
                jnp.sum(live_mask * (rewards * rewards)[..., None], axis=(0, 1)),
            )
        )
    )
    number, reward_sum, square = sums[0], sums[1], sums[2]
    group_mean = reward_sum / jnp.maximum(number, 1.0)
    spread = square / jnp.maximum(number, 1.0) - group_mean * group_mean
    centre = jnp.sum(choose * group_mean, axis=-1)
    group_scale = jnp.sum(choose * jnp.sqrt(jnp.maximum(spread, 1.0)), axis=-1)
    advantage = (rewards - centre) / group_scale
    kept_here = own_expert(kept_mask)
    weight = own_expert(kept_mask * advantage)

    arrived, misfits = [], []
    for slot in range(slots):
        packed, misfit = pack(slot, coefficient, arrays, groups)
        arrived.append(
            exchange(packed.reshape(groups, 4 * tokens, width)).reshape(packed.shape)
        )
        misfits.append(misfit)
    returned = []
    for slot in range(slots):
        returned.append(
            exchange(
                attention(
                    slot, coefficient, arrived[slot], gate_here[slot][:, None], misfits[slot]
                )
            )
        )
    held = None
    gates, logs = [], []
    for slot in range(slots):
        *held, gate_rows, log_rows = unpack(slot, slots, weight, returned[slot], held)
        gates.append(gate_rows.reshape(full_width).astype(BF16))
        logs.append((log_rows[0, 0] * kept_here[slot]).astype(BF16))
    return (
        held[0],
        held[1],
        held[2],
        jnp.stack(gates)[None],
        jnp.stack(logs)[None],
    )


def solution(mesh):
    placed = (
        P("expert", "rep", "seq", None),
        P("expert", "rep", "seq", None),
        P("expert", "rep", "seq", None),
        P("expert", "rep", "seq", None),
        P("expert", "rep", "seq", None),
        P("expert", "rep", None),
        P(None, "rep"),
        P(None, "rep"),
        P(None, "rep"),
        P(None, "rep"),
    )
    return jax.shard_map(
        local,
        mesh=mesh,
        in_specs=placed,
        out_specs=(
            P("expert", "rep", "seq", None),
            P("expert", "rep", "seq", None),
            P("expert", "rep", "seq", None),
            P("expert", "rep", None),
            P("expert", "rep"),
        ),
        check_vma=False,
    )
```

time: 1040 us -> 247 us (0.24)
  blocking collectives: 221 us -> 0 us
  local copies, waits for them, and re-layouts: 218 us -> 13.7 us
  matrix products: 198 us -> 0 us
  other arithmetic: 141 us -> 3.06 us
  Pallas kernels: 0 us -> 90.2 us
  waiting for transfers between devices: 150 us -> 104 us
  starting transfers between devices: 71.8 us -> 31.4 us
  loops' own time: 37.6 us -> 0 us
    psum x5 -> x0, blocking collectives: 221 us -> none  [the longest x2 143 us: one_step(): lax.psum(jnp.sum(grad_gap * mixed_rows, axis=0), 'seq').astype(jnp.bfloat16)]
    dot_general x40 -> x0, matrix products: 140 us -> none  [the longest x8 46.7 us: one_block(): jnp.einsum('qhd,khd->hqk', rows_grad, heads_value, preferred_element_type...]
    pallas_call x0 -> x6, Pallas kernels: none -> 90.2 us  [the longest x2 74.3 us: attention(): pl.pallas_call(functools.partial(attention_body, slot, block_rows, chunk)...]
    while x114 -> x0, local copies, waits for them, and re-layouts: 80 us -> none
    sub x8 -> x0, matrix products: 57.5 us -> none  [one_block(): weights = jnp.exp(scores - row_max)]
    reshape x8 -> x0, other arithmetic: 54.1 us -> none  [the longest x2 25.2 us: one_step(): attended.reshape(length, 1, piece_width)]
    all_to_all x16 -> x4, waiting for transfers between devices: 150 us -> 101 us  [exchange(): lax.all_to_all(pieces, 'seq', split_axis=0, concat_axis=0, tiled=True)]
    dynamic_slice x50 -> x1, local copies, waits for them, and re-layouts: 47.8 us -> 0.01 us  [own_expert(): return lax.dynamic_index_in_dim(both, expert_at, 0, keepdims=False)]
  transfers between devices with their start and end apart: 16 -> 7, of which waited for: 14 -> 6; matrix products, arithmetic and copies ran while one was open for 13% -> 1% of each run, Pallas kernels for 0% -> 34%
where the time goes in v1:
time: 247 us; the launch traced here: 246 us
  waiting for transfers between devices  104 us (42%)
  Pallas kernels  90.2 us (37%)
  starting transfers between devices  31.4 us (13%)
  local copies, waits for them, and re-layouts  13.7 us (6%)
  between operations  3.24 us (1%)
  other arithmetic  3.06 us (1%)
    all_to_all x4, waiting for transfers between devices, exchange(): lax.all_to_all(pieces, 'seq', split_axis=0, concat_axis=0, tiled=True)  101 us
    pallas_call x2, Pallas kernels, attention(): pl.pallas_call(functools.partial(attention_body, slot, block_rows, chunk)...  74.3 us
    all_to_all x4, starting transfers between devices, exchange(): lax.all_to_all(pieces, 'seq', split_axis=0, concat_axis=0, tiled=True)  26.1 us
    unnamed x24, local copies, waits for them, and re-layouts  11.9 us
    pallas_call x2, Pallas kernels, pack(): pl.pallas_call(functools.partial(pack_body, slot), grid=(groups // pieces...  9.45 us
    pallas_call x2, Pallas kernels, unpack(): pl.pallas_call(functools.partial(unpack_body, slot, groups * tokens * gro...  6.4 us
    ppermute x3, starting transfers between devices, sum_over_replicas(): lax.ppermute(values, 'rep', [(at, (at + shift) % replicas) for at in rang...  5.3 us
  transfers between devices with their start and end apart: 7, of which 6 were waited for; matrix products, arithmetic and copies ran while one was open for 1% of the time, Pallas kernels for 34%

profile of v1, /device:TPU:0, one launch (start us, length us, event | category | flops | bytes accessed | tf_op | source)
XLA Modules:
  0.0 245.5 jit_solution(3341688762375688594)
XLA Ops:
  0.6 0.7 fusion.6.coef_ref
  1.3 1.6 copy-done.2
  2.9 1.6 copy-done.4
  4.5 4.7 %shard_map.139 = (bf16[16,4,128,256]{3,2,1,0:T(8,128)(2,1)}, f32[8,256]{1,0:T(8,128)S(1)}) custom-call(f32[2]{0:T(128)S(1)} %fusion.6.coef_ref, bf16[1,2,128,4096]{3,2,1,0:T(8,128)(2,1)S(1)} %copy-done.2, bf16[1,2,128,4096]{3,2,1,0:T(8,128)(2,1)S(1)} %copy-done.4, bf16[1,2,128,4096]{3,2,1,0:T(8,128)(2,1)} %value_ref.3, bf16[1,2,128,4096]{3,2,1,0:T(8,128)(2,1)} %noise_ref.3, ...), custom_call_target="tpu_custom_call" | custom-call | flops 3145728 | bytes 9437184 | tf_op jit(solution)/shard_map/pallas_call | solution.py:64
  9.3 8.0 %all-to-all-start.2 = ((bf16[16,512,256]{2,1,0:T(8,128)(2,1)}), bf16[16,512,256]{2,1,0:T(8,128)(2,1)}, u32[]{:S(2)}, u32[]{:S(2)}) async-start(bf16[16,512,256]{2,1,0:T(8,128)(2,1)} %bitcast.42), calls=%async_computation.2 | async-start | bytes 8388608 | tf_op jit(solution)/shard_map/all_to_all | solution.py:301
  17.3 1.6 copy-done.5
  18.9 4.7 %shard_map.137 = (bf16[16,4,128,256]{3,2,1,0:T(8,128)(2,1)}, f32[8,256]{1,0:T(8,128)S(1)}) custom-call(f32[2]{0:T(128)S(1)} %fusion.6.coef_ref, bf16[1,2,128,4096]{3,2,1,0:T(8,128)(2,1)S(1)} %copy-done.3, bf16[1,2,128,4096]{3,2,1,0:T(8,128)(2,1)S(1)} %copy-done.5, bf16[1,2,128,4096]{3,2,1,0:T(8,128)(2,1)} %value_ref.3, bf16[1,2,128,4096]{3,2,1,0:T(8,128)(2,1)} %noise_ref.3, ...), custom_call_target="tpu_custom_call" | custom-call | flops 3145728 | bytes 9437184 | tf_op jit(solution)/shard_map/pallas_call | solution.py:64
  23.6 50.0 %all-to-all-done.2 = bf16[16,512,256]{2,1,0:T(8,128)(2,1)} async-done(((bf16[16,512,256]{2,1,0:T(8,128)(2,1)}), bf16[16,512,256]{2,1,0:T(8,128)(2,1)}, u32[]{:S(2)}, u32[]{:S(2)}) %all-to-all-start.2) | async-done | bytes 4194336 | tf_op jit(solution)/shard_map/all_to_all | solution.py:301
  73.6 6.1 %all-to-all-start = ((bf16[16,512,256]{2,1,0:T(8,128)(2,1)}), bf16[16,512,256]{2,1,0:T(8,128)(2,1)}, u32[]{:S(2)}, u32[]{:S(2)}) async-start(bf16[16,512,256]{2,1,0:T(8,128)(2,1)} %bitcast.41), calls=%async_computation | async-start | bytes 8388608 | tf_op jit(solution)/shard_map/all_to_all | solution.py:301
  79.8 0.7 dynamic-slice_convert_fusion
  80.6 37.2 %shard_map.140 = bf16[16,400,256]{2,1,0:T(8,128)(2,1)S(1)} custom-call(f32[2]{0:T(128)S(1)} %fusion.6.coef_ref, bf16[16,4,128,256]{3,2,1,0:T(8,128)(2,1)} %bitcast.12.query_ref.key_ref.value_ref.field_ref, bf16[16,4,128,256]{3,2,1,0:T(8,128)(2,1)} %bitcast.12.query_ref.key_ref.value_ref.field_ref, ...), custom_call_target="tpu_custom_call" | custom-call | flops 25769803776 | bytes 7340032 | tf_op jit(solution)/shard_map/pallas_call | solution.py:211
  117.8 1.7 copy-done.7
  119.5 16.6 %all-to-all-done = bf16[16,512,256]{2,1,0:T(8,128)(2,1)} async-done(((bf16[16,512,256]{2,1,0:T(8,128)(2,1)}), bf16[16,512,256]{2,1,0:T(8,128)(2,1)}, u32[]{:S(2)}, u32[]{:S(2)}) %all-to-all-start) | async-done | bytes 4194336 | tf_op jit(solution)/shard_map/all_to_all | solution.py:301
  136.1 6.1 %all-to-all-start.3 = ((bf16[16,400,256]{2,1,0:T(8,128)(2,1)}), bf16[16,400,256]{2,1,0:T(8,128)(2,1)S(1)}, u32[]{:S(2)}, u32[]{:S(2)}) async-start(bf16[16,400,256]{2,1,0:T(8,128)(2,1)} %copy-done.7), calls=%async_computation.3 | async-start | bytes 6553600 | tf_op jit(solution)/shard_map/all_to_all | solution.py:301
  142.4 37.2 %shard_map.138 = bf16[16,400,256]{2,1,0:T(8,128)(2,1)S(1)} custom-call(f32[2]{0:T(128)S(1)} %fusion.6.coef_ref, bf16[16,4,128,256]{3,2,1,0:T(8,128)(2,1)} %bitcast.9.query_ref.key_ref.value_ref.field_ref, bf16[16,4,128,256]{3,2,1,0:T(8,128)(2,1)} %bitcast.9.query_ref.key_ref.value_ref.field_ref, ...), custom_call_target="tpu_custom_call" | custom-call | flops 25769803776 | bytes 7340032 | tf_op jit(solution)/shard_map/pallas_call | solution.py:211
  179.6 1.7 copy-done.6
  181.2 5.2 %all-to-all-done.3.main_ref.side_ref = bf16[16,400,256]{2,1,0:T(8,128)(2,1)S(1)} async-done(((bf16[16,400,256]{2,1,0:T(8,128)(2,1)}), bf16[16,400,256]{2,1,0:T(8,128)(2,1)S(1)}, u32[]{:S(2)}, u32[]{:S(2)}) %all-to-all-start.3) | async-done | bytes 3276832 | tf_op jit(solution)/shard_map/all_to_all | solution.py:301
  186.4 1.7 copy-done
  188.1 5.8 %all-to-all-start.1 = ((bf16[16,400,256]{2,1,0:T(8,128)(2,1)}), bf16[16,400,256]{2,1,0:T(8,128)(2,1)S(1)}, u32[]{:S(2)}, u32[]{:S(2)}) async-start(bf16[16,400,256]{2,1,0:T(8,128)(2,1)} %copy-done.6), calls=%async_computation.1 | async-start | bytes 6553600 | tf_op jit(solution)/shard_map/all_to_all | solution.py:301
  194.2 3.3 %collective-permute-start.1 = (f32[3,4]{1,0:T(4,128)S(1)}, f32[3,4]{1,0:T(4,128)S(1)}, u32[]{:S(2)}, u32[]{:S(2)}) collective-permute-start(f32[3,4]{1,0:T(4,128)S(1)} %pad_maximum_fusion), channel_id=1, source_target_pairs={{0,32},{16,48},{32,0},{48,16},{1,33},{17,49},{33,1},{49,17},{2,34}... | collective-permute-start | bytes 152 | tf_op jit(solution)/shard_map/ppermute | solution.py:308
  197.5 1.1 collective-permute-start.2
  198.5 1.0 collective-permute-start
  199.5 0.6 fusion.15
  200.1 1.0 collective-permute-done.2
  201.0 2.3 collective-permute-done
  203.6 1.9 copy-done.1
  205.5 3.2 %shard_map.141 = (bf16[1,2,128,4096]{3,2,1,0:T(8,128)(2,1)}, bf16[1,2,128,4096]{3,2,1,0:T(8,128)(2,1)}, bf16[1,2,128,4096]{3,2,1,0:T(8,128)(2,1)}, f32[16,256]{1,0:T(8,128)S(1)}, f32[8,128]{1,0:T(8,128)S(1)}) custom-call(f32[2]{0:T(128)S(1)} %fusion.7.weight_ref, bf16[16,400,256]{2,1,0:T(8,128)(2,1)S(1)} %copy-done.1, bf16[16,400,256]{2,1,0:T(8,128)(2,1)S(1)} %copy-done.1), custom_call_target="tpu_custom_call" | custom-call | flops 1572864 | bytes 6291456 | tf_op jit(solution)/shard_map/pallas_call | solution.py:267
  209.2 28.9 %all-to-all-done.1.main_ref.side_ref = bf16[16,400,256]{2,1,0:T(8,128)(2,1)S(1)} async-done(((bf16[16,400,256]{2,1,0:T(8,128)(2,1)}), bf16[16,400,256]{2,1,0:T(8,128)(2,1)S(1)}, u32[]{:S(2)}, u32[]{:S(2)}) %all-to-all-start.1) | async-done | bytes 3276832 | tf_op jit(solution)/shard_map/all_to_all | solution.py:301
  238.1 3.2 %shard_map.142 = (bf16[1,2,128,4096]{3,2,1,0:T(8,128)(2,1)}, bf16[1,2,128,4096]{3,2,1,0:T(8,128)(2,1)}, bf16[1,2,128,4096]{3,2,1,0:T(8,128)(2,1)}, f32[16,256]{1,0:T(8,128)S(1)}, f32[8,128]{1,0:T(8,128)S(1)}) custom-call(f32[2]{0:T(128)S(1)} %fusion.7.weight_ref, ...), custom_call_target="tpu_custom_call", output_to_operand_aliasing={{0}: (3, {}), {1}: (4, {}), {2}: (5, {})} | custom-call | flops 1572864 | bytes 6291456 | tf_op jit(solution)/shard_map/pallas_call | solution.py:267
  241.3 0.5 slice.38
  244.3 0.6 maximum_bitcast_fusion.1
  244.9 0.6 maximum_bitcast_fusion
  (34 shorter events, 1.3 us)
Async XLA Ops:
  1.3 1.6 copy-start.2
  2.9 1.6 copy-start.4
  9.3 8.0 %copy-start.3 = (bf16[1,2,128,4096]{3,2,1,0:T(8,128)(2,1)S(1)}, bf16[1,2,128,4096]{3,2,1,0:T(8,128)(2,1)}, u32[]{:S(2)}) copy-start(bf16[1,2,128,4096]{3,2,1,0:T(8,128)(2,1)} %query_ref.3) | copy-start | bytes 6291460
  9.3 64.3 %all-to-all-start.2 = ((bf16[16,512,256]{2,1,0:T(8,128)(2,1)}), bf16[16,512,256]{2,1,0:T(8,128)(2,1)}, u32[]{:S(2)}, u32[]{:S(2)}) async-start(bf16[16,512,256]{2,1,0:T(8,128)(2,1)} %bitcast.42), calls=%async_computation.2 | async-start | bytes 8388608 | tf_op jit(solution)/shard_map/all_to_all | solution.py:301
  17.3 1.6 copy-start.5
  73.6 62.5 %all-to-all-start = ((bf16[16,512,256]{2,1,0:T(8,128)(2,1)}), bf16[16,512,256]{2,1,0:T(8,128)(2,1)}, u32[]{:S(2)}, u32[]{:S(2)}) async-start(bf16[16,512,256]{2,1,0:T(8,128)(2,1)} %bitcast.41), calls=%async_computation | async-start | bytes 8388608 | tf_op jit(solution)/shard_map/all_to_all | solution.py:301
  117.8 1.7 copy-start.7
  136.1 50.3 %all-to-all-start.3 = ((bf16[16,400,256]{2,1,0:T(8,128)(2,1)}), bf16[16,400,256]{2,1,0:T(8,128)(2,1)S(1)}, u32[]{:S(2)}, u32[]{:S(2)}) async-start(bf16[16,400,256]{2,1,0:T(8,128)(2,1)} %copy-done.7), calls=%async_computation.3 | async-start | bytes 6553600 | tf_op jit(solution)/shard_map/all_to_all | solution.py:301
  179.5 1.7 copy-start.6
  181.2 12.7 %copy-start.8 = (f32[2,2]{1,0:T(2,128)S(1)}, f32[2,2]{1,0:T(2,128)}, u32[]{:S(2)}) copy-start(f32[2,2]{1,0:T(2,128)} %param.16) | copy-start | bytes 52
  181.2 12.8 %copy-start.10 = (s32[2,1]{0,1:T(1,128)S(1)}, s32[2,1]{0,1:T(1,128)}, u32[]{:S(2)}) copy-start(s32[2,1]{0,1:T(1,128)} %param.19) | copy-start | bytes 28
  181.2 12.8 %copy-start.9 = (s32[2,2]{1,0:T(2,128)S(1)}, s32[2,2]{1,0:T(2,128)}, u32[]{:S(2)}) copy-start(s32[2,2]{1,0:T(2,128)} %param.17) | copy-start | bytes 52
  186.4 1.7 copy-start
  188.1 50.0 %all-to-all-start.1 = ((bf16[16,400,256]{2,1,0:T(8,128)(2,1)}), bf16[16,400,256]{2,1,0:T(8,128)(2,1)S(1)}, u32[]{:S(2)}, u32[]{:S(2)}) async-start(bf16[16,400,256]{2,1,0:T(8,128)(2,1)} %copy-done.6), calls=%async_computation.1 | async-start | bytes 6553600 | tf_op jit(solution)/shard_map/all_to_all | solution.py:301
  194.2 5.9 %collective-permute-start.1 = (f32[3,4]{1,0:T(4,128)S(1)}, f32[3,4]{1,0:T(4,128)S(1)}, u32[]{:S(2)}, u32[]{:S(2)}) collective-permute-start(f32[3,4]{1,0:T(4,128)S(1)} %pad_maximum_fusion), channel_id=1, source_target_pairs={{0,32},{16,48},{32,0},{48,16},{1,33},{17,49},{33,1},{49,17},{2,34}... | collective-permute-start | bytes 152 | tf_op jit(solution)/shard_map/ppermute | solution.py:308
  197.5 3.6 %collective-permute-start.2 = (f32[3,4]{1,0:T(4,128)S(1)}, f32[3,4]{1,0:T(4,128)S(1)}, u32[]{:S(2)}, u32[]{:S(2)}) collective-permute-start(f32[3,4]{1,0:T(4,128)S(1)} %pad_maximum_fusion), channel_id=1, source_target_pairs={{0,48},{16,0},{32,16},{48,32},{1,49},{17,1},{33,17},{49,33},{2,50}... | collective-permute-start | bytes 152 | tf_op jit(solution)/shard_map/ppermute | solution.py:308
  198.5 4.8 %collective-permute-start = (f32[3,4]{1,0:T(4,128)S(1)}, f32[3,4]{1,0:T(4,128)S(1)}, u32[]{:S(2)}, u32[]{:S(2)}) collective-permute-start(f32[3,4]{1,0:T(4,128)S(1)} %pad_maximum_fusion), channel_id=1, source_target_pairs={{0,16},{16,32},{32,48},{48,0},{1,17},{17,33},{33,49},{49,1},{2,18}... | collective-permute-start | bytes 152 | tf_op jit(solution)/shard_map/ppermute | solution.py:308
  203.6 1.9 copy-start.1

commit v2 on v1

--- a/solution.py
+++ b/solution.py
@@ -14,7 +14,7 @@
 BF16 = jnp.bfloat16
 NN = (((1,), (0,)), ((), ()))
 NT = (((1,), (1,)), ((), ()))
-VMEM_LIMIT = 48 * 1024 * 1024
+VMEM_LIMIT = 63 * 1024 * 1024
 
 
 def step_coef(timesteps):
@@ -33,11 +33,12 @@
 
 
 def pack_body(
-    slot, coef_ref, query_ref, key_ref, value_ref, noise_ref, old_ref, out_ref, misfit_ref
+    slot, own_ref, coef_ref, query_ref, key_ref, value_ref, noise_ref, old_ref, *refs
 ):
-    pieces = out_ref.shape[0]
-    width = out_ref.shape[3]
-    coefficient = coef_ref[slot]
+    out_ref, misfit_ref = refs[-2:]
+    pieces, _, width = out_ref.shape
+    tokens = query_ref.shape[2]
+    coefficient = coef_ref[own_ref[0], slot]
 
     @pl.when(pl.program_id(0) == 0)
     def _():
@@ -46,31 +47,39 @@
     total = misfit_ref[...]
     for piece in range(pieces):
         columns = slice(piece * width, (piece + 1) * width)
-        out_ref[piece, 0] = query_ref[0, 0, :, columns]
-        out_ref[piece, 1] = key_ref[0, 0, :, columns]
-        out_ref[piece, 2] = value_ref[0, 0, :, columns]
+        out_ref[piece, 0:tokens] = query_ref[0, 0, :, columns]
+        out_ref[piece, tokens : 2 * tokens] = key_ref[0, 0, :, columns]
+        out_ref[piece, 2 * tokens : 3 * tokens] = value_ref[0, 0, :, columns]
         noise = noise_ref[0, 0, :, columns].astype(F32)
         shift = coefficient * old_ref[0, 0, :, columns].astype(F32)
-        out_ref[piece, 3] = (noise - shift).astype(BF16)
+        out_ref[piece, 3 * tokens : 4 * tokens] = (noise - shift).astype(BF16)
         total = total + fold_rows(shift * (shift - 2.0 * noise), jnp.sum)
+        for gate_ref in refs[:-2]:
+            gates = gate_ref[0, :, columns]
+            blank = jnp.zeros((SIDE - gates.shape[0], width), BF16)
+            out_ref[piece, 4 * tokens :] = jnp.concatenate([gates, blank], axis=0)
     misfit_ref[...] = total
 
 
-def pack(slot, coefficient, arrays, groups):
+def pack(slot, own, coefficient, arrays, gate_scale, groups):
     _, _, tokens, full_width = arrays[0].shape
     width = full_width // groups
-    pieces = 4
+    pieces = 8
     rows = pl.BlockSpec((1, 1, tokens, pieces * width), lambda i: (0, slot, 0, i))
+    gates = [] if gate_scale is None else [gate_scale]
+    held = 4 * tokens + SIDE * len(gates)
     return pl.pallas_call(
         functools.partial(pack_body, slot),
         grid=(groups // pieces,),
         out_shape=(
-            jax.ShapeDtypeStruct((groups, 4, tokens, width), BF16),
+            jax.ShapeDtypeStruct((groups, held, width), BF16),
             jax.ShapeDtypeStruct((8, width), F32),
         ),
-        in_specs=[pl.BlockSpec(memory_space=pltpu.SMEM)] + [rows] * 5,
+        in_specs=[pl.BlockSpec(memory_space=pltpu.SMEM)] * 2
+        + [rows] * 5
+        + [pl.BlockSpec((1,) + g.shape[1:2] + (pieces * width,), lambda i: (0, 0, i)) for g in gates],
         out_specs=(
-            pl.BlockSpec((pieces, 4, tokens, width), lambda i: (i, 0, 0, 0)),
+            pl.BlockSpec((pieces, held, width), lambda i: (i, 0, 0)),
             pl.BlockSpec((8, width), lambda i: (0, 0)),
         ),
         compiler_params=pltpu.CompilerParams(vmem_limit_bytes=VMEM_LIMIT),
@@ -79,13 +88,14 @@
             bytes_accessed=18 * tokens * full_width,
             transcendentals=0,
         ),
-    )(coefficient, *arrays)
+    )(own, coefficient, *arrays, *gates)
 
 
 def attention_body(
     slot,
     block_rows,
     chunk,
+    own_ref,
     coef_ref,
     query_ref,
     key_ref,
@@ -108,18 +118,20 @@
     misfit_total,
 ):
     length = q_rows.shape[0]
-    pieces = out_ref.shape[0]
+    pieces = out_ref.shape[1]
     tokens = length // pieces
+    step_set = pl.program_id(0)
     scale_factor = HD ** (-0.5)
     log2e = 1.4426950408889634
-    coefficient = coef_ref[slot]
+    coefficient = coef_ref[step_set, slot]
     q_rows[...] = query_ref[...].reshape(length, HD)
     k_rows[...] = key_ref[...].reshape(length, HD)
     v_rows[...] = value_ref[...].reshape(length, HD)
     k_cols[...] = k_rows[...].T
     v_cols[...] = v_rows[...].T
     field_cols[...] = field_ref[...].reshape(length, HD).T
-    gate = gate_ref[...]
+    gate_row = gate_ref[0, 0, slot : slot + 1, :].astype(F32)
+    gate = jnp.broadcast_to(gate_row, (8, HD)).T[:, 0:1]
     gate_total[...] = jnp.zeros_like(gate_total)
     misfit_total[...] = jnp.zeros_like(misfit_total)
     chunks = [slice(at, at + chunk) for at in range(0, length, chunk)]
@@ -163,16 +175,16 @@
             value_total[part, :] = jnp.where(first, value_part, value_total[part, :] + value_part)
             key_total[part, :] = jnp.where(first, key_part, key_total[part, :] + key_part)
         held = block_rows // tokens
-        out_ref[pl.ds(index * held, held), 0:tokens, :] = (
+        out_ref[0, pl.ds(index * held, held), 0:tokens, :] = (
             (grad_query.T * scale_factor).astype(BF16).reshape(held, tokens, HD)
         )
         return 0
 
     lax.fori_loop(0, length // block_rows, one_block, 0)
-    out_ref[:, tokens : 2 * tokens, :] = (
+    out_ref[0, :, tokens : 2 * tokens, :] = (
         (key_total[...] * scale_factor).astype(BF16).reshape(pieces, tokens, HD)
     )
-    out_ref[:, 2 * tokens : 3 * tokens, :] = (
+    out_ref[0, :, 2 * tokens : 3 * tokens, :] = (
         value_total[...].astype(BF16).reshape(pieces, tokens, HD)
     )
 
@@ -183,7 +195,8 @@
         return jnp.sum(total.T, axis=0, keepdims=True)
 
     gate_row = row_of(gate_total[...])
-    misfit_row = row_of(misfit_total[...]) + jnp.sum(misfit_ref[...], axis=0, keepdims=True)
+    local_row = jnp.sum(misfit_ref[...], axis=0, keepdims=True)
+    misfit_row = row_of(misfit_total[...]) + jnp.where(step_set == own_ref[0], local_row, 0.0)
     rest = misfit_row
     side = []
     for _ in range(3):
@@ -194,31 +207,31 @@
     rows = jnp.zeros((SIDE, HD), F32)
     for at, row in enumerate([gate_high, gate_row - gate_high] + side):
         rows = jnp.where(row_at == at, row, rows)
-    out_ref[:, 3 * tokens :, :] = jnp.broadcast_to(
+    out_ref[0, :, 3 * tokens :, :] = jnp.broadcast_to(
         rows.astype(BF16)[None], (pieces, SIDE, HD)
     )
 
 
-def attention(slot, coefficient, arrived, gate_column, misfit):
-    groups, _, tokens, width = arrived.shape
+def attention(slot, own, coefficient, arrived, gates, misfit):
+    sets, groups, _, width = arrived.shape
+    tokens = arrived.shape[2] // (4 * SIDE) * SIDE
     length = groups * tokens
-    heads_here = width // HD
     block_rows, chunk = 512, 512
 
     def field(which):
-        return pl.BlockSpec((groups, 1, tokens, HD), lambda h: (0, which, 0, h))
+        return pl.BlockSpec((1, groups, tokens, HD), lambda e: (e, 0, which, 0))
 
     return pl.pallas_call(
         functools.partial(attention_body, slot, block_rows, chunk),
-        grid=(heads_here,),
-        out_shape=jax.ShapeDtypeStruct((groups, 3 * tokens + SIDE, width), BF16),
-        in_specs=[pl.BlockSpec(memory_space=pltpu.SMEM)]
+        grid=(sets,),
+        out_shape=jax.ShapeDtypeStruct((sets, groups, 3 * tokens + SIDE, width), BF16),
+        in_specs=[pl.BlockSpec(memory_space=pltpu.SMEM)] * 2
         + [field(which) for which in range(4)]
         + [
-            pl.BlockSpec((HD, 1), lambda h: (h, 0)),
-            pl.BlockSpec((8, HD), lambda h: (0, h)),
+            pl.BlockSpec((1, 1, SIDE, HD), lambda e: (e, 0, 4 * tokens // SIDE, 0)),
+            pl.BlockSpec((8, HD), lambda e: (0, 0)),
         ],
-        out_specs=pl.BlockSpec((groups, 3 * tokens + SIDE, HD), lambda h: (0, 0, h)),
+        out_specs=pl.BlockSpec((1, groups, 3 * tokens + SIDE, HD), lambda e: (e, 0, 0, 0)),
         scratch_shapes=[pltpu.VMEM((length, HD), BF16)] * 3
         + [pltpu.VMEM((HD, length), BF16)] * 3
         + [
@@ -231,74 +244,101 @@
         ],
         compiler_params=pltpu.CompilerParams(vmem_limit_bytes=VMEM_LIMIT),
         cost_estimate=pl.CostEstimate(
-            flops=heads_here * 24 * length * length * HD,
-            bytes_accessed=14 * length * width,
-            transcendentals=heads_here * length * length,
-        ),
-    )(coefficient, arrived, arrived, arrived, arrived, gate_column, misfit)
-
-
-def unpack_body(slot, entries, weight_ref, main_ref, side_ref, *refs):
+            flops=sets * 24 * length * length * HD,
+            bytes_accessed=sets * 14 * length * width,
+            transcendentals=sets * length * length,
+        ),
+    )(own, coefficient, arrived, arrived, arrived, arrived, gates, misfit)
+
+
+def unpack_body(slot, entries, weight_ref, kept_ref, main_ref, side_ref, *refs):
     query_ref, key_ref, value_ref, gate_ref, log_ref = refs[-5:]
+    earlier = refs[:-5]
     pieces = main_ref.shape[0]
     width = main_ref.shape[2]
     tokens = query_ref.shape[2]
-    side = side_ref[...].astype(F32)
-    misfit = jnp.sum(side[:, 2:5, :])
+    misfit = jnp.sum(side_ref[:, 2:5, :].astype(F32))
     ratio_log = jnp.full((1, HD), -misfit / (2.0 * entries), F32)
-    log_ref[...] = jnp.broadcast_to(ratio_log, log_ref.shape)
+    if earlier:
+        gate_ref[0, 0:1, :] = earlier[0][...].astype(BF16)
+        own_log = ratio_log[:, 0:1] * kept_ref[slot]
+        log_ref[...] = jnp.concatenate([earlier[1][:, 0:1], own_log], axis=1).astype(BF16)
+    else:
+        log_ref[...] = ratio_log * kept_ref[slot]
     factor = weight_ref[slot] * jnp.exp(ratio_log)
-    factor = jnp.concatenate([factor] * (width // HD), axis=1)
-    gate_ref[...] = (side[:, 0, :] + side[:, 1, :]) * factor
+    first = pl.program_id(0) * pieces
     for piece in range(pieces):
         columns = slice(piece * width, (piece + 1) * width)
+        parts = side_ref[first + piece, 0:2, :].astype(F32)
+        gate_row = (parts[0:1] + parts[1:2]) * factor
+        if earlier:
+            gate_ref[0, 1:2, columns] = gate_row.astype(BF16)
+        else:
+            gate_ref[:, columns] = gate_row
         for which, out_ref in enumerate((query_ref, key_ref, value_ref)):
             rows = main_ref[piece, which * tokens : (which + 1) * tokens, :].astype(F32)
             out_ref[0, 0, :, columns] = (rows * factor).astype(BF16)
 
 
-def unpack(slot, slots, weight, returned, previous):
-    groups, rows, width = returned.shape
+def unpack(slot, slots, weight, kept, returned, previous):
+    heads, rows, width = returned.shape
     tokens = (rows - SIDE) // 3
-    pieces = 4
-    whole = jax.ShapeDtypeStruct((1, slots, tokens, groups * width), BF16)
+    full_width = heads * width
+    entries = full_width * tokens * lax.axis_size("seq")
+    pieces = 8
+    whole = jax.ShapeDtypeStruct((1, slots, tokens, full_width), BF16)
     part = pl.BlockSpec((1, 1, tokens, pieces * width), lambda i: (0, slot, 0, i))
-    held = [] if previous is None else list(previous)
+    in_specs = [
+        pl.BlockSpec(memory_space=pltpu.SMEM),
+        pl.BlockSpec(memory_space=pltpu.SMEM),
+        pl.BlockSpec((pieces, 3 * tokens, width), lambda i: (i, 0, 0)),
+        pl.BlockSpec((heads, SIDE, width), lambda i: (0, 3 * tokens // SIDE, 0)),
+    ]
+    if previous:
+        in_specs += [pl.BlockSpec(memory_space=pl.ANY)] * 3 + [
+            pl.BlockSpec((1, pieces * width), lambda i: (0, i)),
+            pl.BlockSpec((1, HD), lambda i: (0, 0)),
+        ]
+        small = (
+            jax.ShapeDtypeStruct((1, slots, full_width), BF16),
+            jax.ShapeDtypeStruct((1, slots), BF16),
+        )
+        small_specs = (
+            pl.BlockSpec((1, slots, pieces * width), lambda i: (0, 0, i)),
+            pl.BlockSpec((1, slots), lambda i: (0, 0)),
+        )
+    else:
+        small = (
+            jax.ShapeDtypeStruct((1, full_width), F32),
+            jax.ShapeDtypeStruct((1, HD), F32),
+        )
+        small_specs = (
+            pl.BlockSpec((1, pieces * width), lambda i: (0, i)),
+            pl.BlockSpec((1, HD), lambda i: (0, 0)),
+        )
+
+    def body(weight_ref, kept_ref, main_ref, side_ref, *refs):
+        refs = refs[3:] if previous else refs
+        unpack_body(slot, entries, weight_ref, kept_ref, main_ref, side_ref, *refs)
+
     return pl.pallas_call(
-        functools.partial(unpack_body, slot, groups * tokens * groups * width),
-        grid=(groups // pieces,),
-        out_shape=(
-            whole,
-            whole,
-            whole,
-            jax.ShapeDtypeStruct((groups, width), F32),
-            jax.ShapeDtypeStruct((8, HD), F32),
-        ),
-        in_specs=[
-            pl.BlockSpec(memory_space=pltpu.SMEM),
-            pl.BlockSpec((pieces, 3 * tokens, width), lambda i: (i, 0, 0)),
-            pl.BlockSpec((groups, SIDE, width), lambda i: (0, 3 * tokens // SIDE, 0)),
-        ]
-        + [pl.BlockSpec(memory_space=pl.ANY) for _ in held],
-        out_specs=(
-            part,
-            part,
-            part,
-            pl.BlockSpec((groups, width), lambda i: (0, 0)),
-            pl.BlockSpec((8, HD), lambda i: (0, 0)),
-        ),
-        input_output_aliases={3 + at: at for at in range(len(held))},
+        body,
+        grid=(heads // pieces,),
+        out_shape=(whole, whole, whole) + small,
+        in_specs=in_specs,
+        out_specs=(part, part, part) + small_specs,
+        input_output_aliases={4 + at: at for at in range(3)} if previous else {},
         compiler_params=pltpu.CompilerParams(vmem_limit_bytes=VMEM_LIMIT),
         cost_estimate=pl.CostEstimate(
-            flops=3 * tokens * groups * width,
-            bytes_accessed=12 * tokens * groups * width,
+            flops=3 * tokens * full_width,
+            bytes_accessed=12 * tokens * full_width,
             transcendentals=0,
         ),
-    )(weight, returned, returned, *held)
+    )(weight, kept, returned, returned, *previous)
 
 
 def exchange(pieces):
-    return lax.all_to_all(pieces, "seq", split_axis=0, concat_axis=0, tiled=True)
+    return lax.all_to_all(pieces, ("expert", "seq"), split_axis=0, concat_axis=0, tiled=True)
 
 
 def sum_over_replicas(values):
@@ -327,18 +367,17 @@
     tokens = query_in.shape[2]
     full_width = query_in.shape[3]
     groups = lax.axis_size("seq")
-    width = full_width // groups
+    sets = lax.axis_size("expert")
+    heads = sets * groups
+    width = full_width // heads
     expert_at = lax.axis_index("expert")
+    own = expert_at.astype(jnp.int32)[None]
 
     def own_expert(both):
         return lax.dynamic_index_in_dim(both, expert_at, 0, keepdims=False)
 
-    coefficient = step_coef(own_expert(timesteps))
+    coefficient = step_coef(timesteps)
     arrays = (query_in, key_in, value_in, sample_noise, old_velocity)
-    gate_here = lax.dynamic_slice_in_dim(
-        gate_scale[0], lax.axis_index("seq") * width, width, 1
-    ).astype(F32)
-
     kept_mask = (
         jnp.arange(slots, dtype=jnp.int32)[None, :] < counts[:, 0][:, None]
     ).astype(F32)
@@ -364,33 +403,21 @@
 
     arrived, misfits = [], []
     for slot in range(slots):
-        packed, misfit = pack(slot, coefficient, arrays, groups)
-        arrived.append(
-            exchange(packed.reshape(groups, 4 * tokens, width)).reshape(packed.shape)
-        )
+        packed, misfit = pack(
+            slot, own, coefficient, arrays, gate_scale if slot == 0 else None, heads
+        )
+        arrived.append(exchange(packed).reshape((sets, groups) + packed.shape[1:]))
         misfits.append(misfit)
     returned = []
     for slot in range(slots):
-        returned.append(
-            exchange(
-                attention(
-                    slot, coefficient, arrived[slot], gate_here[slot][:, None], misfits[slot]
-                )
-            )
-        )
-    held = None
-    gates, logs = [], []
+        sent = attention(
+            slot, own, coefficient, arrived[slot], arrived[0], misfits[slot]
+        )
+        returned.append(exchange(sent.reshape(heads, 3 * tokens + SIDE, width)))
+    held = ()
     for slot in range(slots):
-        *held, gate_rows, log_rows = unpack(slot, slots, weight, returned[slot], held)
-        gates.append(gate_rows.reshape(full_width).astype(BF16))
-        logs.append((log_rows[0, 0] * kept_here[slot]).astype(BF16))
-    return (
-        held[0],
-        held[1],
-        held[2],
-        jnp.stack(gates)[None],
-        jnp.stack(logs)[None],
-    )
+        held = unpack(slot, slots, weight, kept_here, returned[slot], held)
+    return held
 
 
 def solution(mesh):

time: 247 us -> 231 us (0.935)
  local copies, waits for them, and re-layouts: 13.7 us -> 0.62 us
  Pallas kernels: 90.2 us -> 96 us
  starting transfers between devices: 31.4 us -> 28.3 us
  between operations: 3.24 us -> 0.71 us
    unnamed x24 -> x6, local copies, waits for them, and re-layouts: 11.9 us -> 0.01 us
    pallas_call x2, Pallas kernels: 6.4 us -> 9.56 us  [unpack(): pl.pallas_call(body, grid=(heads // pieces,), out_shape=(whole, whole, wh...]
    all_to_all x4, starting transfers between devices: 26.1 us -> 23 us  [exchange(): lax.all_to_all(pieces, ('expert', 'seq'), split_axis=0, concat_axis=0, ti...]
  transfers between devices with their start and end apart: 7 -> 7, of which waited for: 6 -> 6; matrix products, arithmetic and copies ran while one was open for 1% -> 0% of each run, Pallas kernels for 34% -> 37%
where the time goes in v2:
time: 231 us
  waiting for transfers between devices  103 us (45%)
  Pallas kernels  96 us (42%)
  starting transfers between devices  28.3 us (12%)
    all_to_all x4, waiting for transfers between devices, exchange(): lax.all_to_all(pieces, ('expert', 'seq'), split_axis=0, concat_axis=0, ti...  99.5 us
    pallas_call x2, Pallas kernels, attention(): pl.pallas_call(functools.partial(attention_body, slot, block_rows, chunk)...  75.7 us
    all_to_all x4, starting transfers between devices, exchange(): lax.all_to_all(pieces, ('expert', 'seq'), split_axis=0, concat_axis=0, ti...  23 us
    pallas_call x2, Pallas kernels, pack(): pl.pallas_call(functools.partial(pack_body, slot), grid=(groups // pieces...  10.7 us
    pallas_call x2, Pallas kernels, unpack(): pl.pallas_call(body, grid=(heads // pieces,), out_shape=(whole, whole, wh...  9.56 us
    ppermute x3, starting transfers between devices, sum_over_replicas(): lax.ppermute(values, 'rep', [(at, (at + shift) % replicas) for at in rang...  5.3 us
  transfers between devices with their start and end apart: 7, of which 6 were waited for; matrix products, arithmetic and copies ran while one was open for 0% of the time, Pallas kernels for 37%

profile of v2, /device:TPU:0, one launch (start us, length us, event | category | flops | bytes accessed | tf_op | source)
XLA Modules:
  0.0 230.6 jit_solution(11597764220949753613)
XLA Ops:
  0.6 1.3 fusion.4.coef_ref
  1.9 5.4 %shard_map.138 = (bf16[32,528,128]{2,1,0:T(8,128)(2,1)}, f32[8,128]{1,0:T(8,128)}) custom-call(s32[1]{0:T(128)} %bitcast.8.own_ref, f32[2,2]{1,0:T(2,128)} %fusion.4.coef_ref, bf16[1,2,128,4096]{3,2,1,0:T(8,128)(2,1)} %query_ref.3, bf16[1,2,128,4096]{3,2,1,0:T(8,128)(2,1)} %key_ref.3, bf16[1,2,128,4096]{3,2,1,0:T(8,128)(2,1)} %value_ref.3, ...), custom_call_target="tpu_custom_call" | custom-call | flops 3145728 | bytes 9437184 | tf_op jit(solution)/shard_map/pallas_call | solution.py:71
  7.3 8.4 %all-to-all-start.1 = ((bf16[32,528,128]{2,1,0:T(8,128)(2,1)}), bf16[32,528,128]{2,1,0:T(8,128)(2,1)}, u32[]{:S(2)}, u32[]{:S(2)}) async-start(bf16[32,528,128]{2,1,0:T(8,128)(2,1)} %get-tuple-element.15), calls=%async_computation.1 | async-start | bytes 8650752 | tf_op jit(solution)/shard_map/all_to_all | solution.py:341
  15.7 5.3 %shard_map.137 = (bf16[32,512,128]{2,1,0:T(8,128)(2,1)}, f32[8,128]{1,0:T(8,128)}) custom-call(s32[1]{0:T(128)} %bitcast.8.own_ref, f32[2,2]{1,0:T(2,128)} %fusion.4.coef_ref, bf16[1,2,128,4096]{3,2,1,0:T(8,128)(2,1)} %query_ref.3, bf16[1,2,128,4096]{3,2,1,0:T(8,128)(2,1)} %key_ref.3, bf16[1,2,128,4096]{3,2,1,0:T(8,128)(2,1)} %value_ref.3, ...), custom_call_target="tpu_custom_call" | custom-call | flops 3145728 | bytes 9437184 | tf_op jit(solution)/shard_map/pallas_call | solution.py:71
  21.0 49.8 %all-to-all-done.1 = bf16[32,528,128]{2,1,0:T(8,128)(2,1)} async-done(((bf16[32,528,128]{2,1,0:T(8,128)(2,1)}), bf16[32,528,128]{2,1,0:T(8,128)(2,1)}, u32[]{:S(2)}, u32[]{:S(2)}) %all-to-all-start.1) | async-done | bytes 4325408 | tf_op jit(solution)/shard_map/all_to_all | solution.py:341
  70.8 4.9 %all-to-all-start = ((bf16[32,512,128]{2,1,0:T(8,128)(2,1)}), bf16[32,512,128]{2,1,0:T(8,128)(2,1)}, u32[]{:S(2)}, u32[]{:S(2)}) async-start(bf16[32,512,128]{2,1,0:T(8,128)(2,1)} %get-tuple-element.14), calls=%async_computation | async-start | bytes 8388608 | tf_op jit(solution)/shard_map/all_to_all | solution.py:341
  75.7 37.9 %shard_map.140 = bf16[2,16,400,128]{3,2,1,0:T(8,128)(2,1)} custom-call(s32[1]{0:T(128)} %bitcast.8.own_ref, f32[2,2]{1,0:T(2,128)} %fusion.4.coef_ref, bf16[2,16,528,128]{3,2,1,0:T(8,128)(2,1)} %bitcast.10.gate_ref.query_ref.key_ref.value_ref.field_ref, bf16[2,16,528,128]{3,2,1,0:T(8,128)(2,1)} %bitcast.10.gate_ref.query_ref.key_ref.value_ref.field_ref, ...), custom_call_target="tpu_custom_call" | custom-call | flops 25769803776 | bytes 7340032 | tf_op jit(solution)/shard_map/pallas_call | solution.py:224
  113.6 15.8 %all-to-all-done = bf16[32,512,128]{2,1,0:T(8,128)(2,1)} async-done(((bf16[32,512,128]{2,1,0:T(8,128)(2,1)}), bf16[32,512,128]{2,1,0:T(8,128)(2,1)}, u32[]{:S(2)}, u32[]{:S(2)}) %all-to-all-start) | async-done | bytes 4194336 | tf_op jit(solution)/shard_map/all_to_all | solution.py:341
  129.4 4.8 %all-to-all-start.3 = ((bf16[32,400,128]{2,1,0:T(8,128)(2,1)}), bf16[32,400,128]{2,1,0:T(8,128)(2,1)}, u32[]{:S(2)}, u32[]{:S(2)}) async-start(bf16[32,400,128]{2,1,0:T(8,128)(2,1)} %bitcast.23), calls=%async_computation.3 | async-start | bytes 6553600 | tf_op jit(solution)/shard_map/all_to_all | solution.py:341
  134.2 37.9 %shard_map.139 = bf16[2,16,400,128]{3,2,1,0:T(8,128)(2,1)} custom-call(s32[1]{0:T(128)} %bitcast.8.own_ref, f32[2,2]{1,0:T(2,128)} %fusion.4.coef_ref, bf16[2,16,512,128]{3,2,1,0:T(8,128)(2,1)} %bitcast.9.query_ref.key_ref.value_ref.field_ref, bf16[2,16,512,128]{3,2,1,0:T(8,128)(2,1)} %bitcast.9.query_ref.key_ref.value_ref.field_ref, ...), custom_call_target="tpu_custom_call" | custom-call | flops 25769803776 | bytes 7340032 | tf_op jit(solution)/shard_map/pallas_call | solution.py:224
  172.1 5.5 %all-to-all-done.3.main_ref.side_ref = bf16[32,400,128]{2,1,0:T(8,128)(2,1)} async-done(((bf16[32,400,128]{2,1,0:T(8,128)(2,1)}), bf16[32,400,128]{2,1,0:T(8,128)(2,1)}, u32[]{:S(2)}, u32[]{:S(2)}) %all-to-all-start.3) | async-done | bytes 3276832 | tf_op jit(solution)/shard_map/all_to_all | solution.py:341
  177.6 0.0 copy-start
  177.6 0.0 copy-start.2
  177.6 0.0 copy-start.1
  177.6 5.0 %all-to-all-start.2 = ((bf16[32,400,128]{2,1,0:T(8,128)(2,1)}), bf16[32,400,128]{2,1,0:T(8,128)(2,1)}, u32[]{:S(2)}, u32[]{:S(2)}) async-start(bf16[32,400,128]{2,1,0:T(8,128)(2,1)} %bitcast.22), calls=%async_computation.2 | async-start | bytes 6553600 | tf_op jit(solution)/shard_map/all_to_all | solution.py:341
  182.5 0.0 copy-done
  182.5 0.0 copy-done.2
  182.6 0.1 fusion.6
  182.6 0.0 copy-done.1
  182.6 0.1 select_reduce_fusion
  182.7 3.3 %collective-permute-start.1 = (f32[3,4]{1,0:T(4,128)S(1)}, f32[3,4]{1,0:T(4,128)S(1)}, u32[]{:S(2)}, u32[]{:S(2)}) collective-permute-start(f32[3,4]{1,0:T(4,128)S(1)} %pad_maximum_fusion), channel_id=1, source_target_pairs={{0,32},{16,48},{32,0},{48,16},{1,33},{17,49},{33,1},{49,17},{2,34}... | collective-permute-start | bytes 152 | tf_op jit(solution)/shard_map/ppermute | solution.py:348
  186.0 1.1 collective-permute-start.2
  187.1 1.0 collective-permute-start
  188.0 0.0 collective-permute-done.1
  188.0 1.6 collective-permute-done.2
  189.6 2.3 collective-permute-done
  191.9 0.2 select_reduce_fusion.2
  192.1 0.1 fusion.5
  192.1 0.6 dynamic-slice_bitcast_fusion
  192.7 4.8 %shard_map.141 = (bf16[1,2,128,4096]{3,2,1,0:T(8,128)(2,1)}, bf16[1,2,128,4096]{3,2,1,0:T(8,128)(2,1)}, bf16[1,2,128,4096]{3,2,1,0:T(8,128)(2,1)}, f32[1,4096]{1,0:T(1,128)}, f32[1,128]{1,0:T(1,128)}) custom-call(f32[2]{0:T(128)} %get-tuple-element.31.weight_ref, f32[2]{0:T(128)} %get-tuple-element.30.kept_ref, ...), custom_call_target="tpu_custom_call" | custom-call | flops 1572864 | bytes 6291456 | tf_op jit(solution)/shard_map/pallas_call | solution.py:324
  197.5 28.4 %all-to-all-done.2.main_ref.side_ref = bf16[32,400,128]{2,1,0:T(8,128)(2,1)} async-done(((bf16[32,400,128]{2,1,0:T(8,128)(2,1)}), bf16[32,400,128]{2,1,0:T(8,128)(2,1)}, u32[]{:S(2)}, u32[]{:S(2)}) %all-to-all-start.2) | async-done | bytes 3276832 | tf_op jit(solution)/shard_map/all_to_all | solution.py:341
  225.8 4.8 %shard_map.142 = (bf16[1,2,128,4096]{3,2,1,0:T(8,128)(2,1)}, bf16[1,2,128,4096]{3,2,1,0:T(8,128)(2,1)}, bf16[1,2,128,4096]{3,2,1,0:T(8,128)(2,1)}, bf16[1,2,4096]{2,1,0:T(2,128)(2,1)}, bf16[1,2]{1,0:T(2,128)(2,1)}) custom-call(f32[2]{0:T(128)} %get-tuple-element.31.weight_ref, ...), custom_call_target="tpu_custom_call", output_to_operand_aliasing={{0}: (4, {}), {1}: (5, {}), {2}: (6, {})} | custom-call | flops 1572864 | bytes 6291456 | tf_op jit(solution)/shard_map/pallas_call | solution.py:324
  (4 shorter events, 0.0 us)
Async XLA Ops:
  7.3 63.5 %all-to-all-start.1 = ((bf16[32,528,128]{2,1,0:T(8,128)(2,1)}), bf16[32,528,128]{2,1,0:T(8,128)(2,1)}, u32[]{:S(2)}, u32[]{:S(2)}) async-start(bf16[32,528,128]{2,1,0:T(8,128)(2,1)} %get-tuple-element.15), calls=%async_computation.1 | async-start | bytes 8650752 | tf_op jit(solution)/shard_map/all_to_all | solution.py:341
  70.8 58.5 %all-to-all-start = ((bf16[32,512,128]{2,1,0:T(8,128)(2,1)}), bf16[32,512,128]{2,1,0:T(8,128)(2,1)}, u32[]{:S(2)}, u32[]{:S(2)}) async-start(bf16[32,512,128]{2,1,0:T(8,128)(2,1)} %get-tuple-element.14), calls=%async_computation | async-start | bytes 8388608 | tf_op jit(solution)/shard_map/all_to_all | solution.py:341
  129.4 48.2 %all-to-all-start.3 = ((bf16[32,400,128]{2,1,0:T(8,128)(2,1)}), bf16[32,400,128]{2,1,0:T(8,128)(2,1)}, u32[]{:S(2)}, u32[]{:S(2)}) async-start(bf16[32,400,128]{2,1,0:T(8,128)(2,1)} %bitcast.23), calls=%async_computation.3 | async-start | bytes 6553600 | tf_op jit(solution)/shard_map/all_to_all | solution.py:341
  177.6 5.0 %copy-start = (f32[2,2]{1,0:T(2,128)S(1)}, f32[2,2]{1,0:T(2,128)}, u32[]{:S(2)}) copy-start(f32[2,2]{1,0:T(2,128)} %param.16) | copy-start | bytes 52
  177.6 5.0 %copy-start.2 = (s32[2,1]{0,1:T(1,128)S(1)}, s32[2,1]{0,1:T(1,128)}, u32[]{:S(2)}) copy-start(s32[2,1]{0,1:T(1,128)} %param.19) | copy-start | bytes 28
  177.6 5.1 %copy-start.1 = (s32[2,2]{1,0:T(2,128)S(1)}, s32[2,2]{1,0:T(2,128)}, u32[]{:S(2)}) copy-start(s32[2,2]{1,0:T(2,128)} %param.17) | copy-start | bytes 52
  177.6 48.3 %all-to-all-start.2 = ((bf16[32,400,128]{2,1,0:T(8,128)(2,1)}), bf16[32,400,128]{2,1,0:T(8,128)(2,1)}, u32[]{:S(2)}, u32[]{:S(2)}) async-start(bf16[32,400,128]{2,1,0:T(8,128)(2,1)} %bitcast.22), calls=%async_computation.2 | async-start | bytes 6553600 | tf_op jit(solution)/shard_map/all_to_all | solution.py:341
  182.7 5.3 %collective-permute-start.1 = (f32[3,4]{1,0:T(4,128)S(1)}, f32[3,4]{1,0:T(4,128)S(1)}, u32[]{:S(2)}, u32[]{:S(2)}) collective-permute-start(f32[3,4]{1,0:T(4,128)S(1)} %pad_maximum_fusion), channel_id=1, source_target_pairs={{0,32},{16,48},{32,0},{48,16},{1,33},{17,49},{33,1},{49,17},{2,34}... | collective-permute-start | bytes 152 | tf_op jit(solution)/shard_map/ppermute | solution.py:348
  186.0 3.6 %collective-permute-start.2 = (f32[3,4]{1,0:T(4,128)S(1)}, f32[3,4]{1,0:T(4,128)S(1)}, u32[]{:S(2)}, u32[]{:S(2)}) collective-permute-start(f32[3,4]{1,0:T(4,128)S(1)} %pad_maximum_fusion), channel_id=1, source_target_pairs={{0,48},{16,0},{32,16},{48,32},{1,49},{17,1},{33,17},{49,33},{2,50}... | collective-permute-start | bytes 152 | tf_op jit(solution)/shard_map/ppermute | solution.py:348
  187.1 4.8 %collective-permute-start = (f32[3,4]{1,0:T(4,128)S(1)}, f32[3,4]{1,0:T(4,128)S(1)}, u32[]{:S(2)}, u32[]{:S(2)}) collective-permute-start(f32[3,4]{1,0:T(4,128)S(1)} %pad_maximum_fusion), channel_id=1, source_target_pairs={{0,16},{16,32},{32,48},{48,0},{1,17},{17,33},{33,49},{49,1},{2,18}... | collective-permute-start | bytes 152 | tf_op jit(solution)/shard_map/ppermute | solution.py:348

commit v3 on v2

--- a/solution.py
+++ b/solution.py
@@ -9,6 +9,7 @@
 
 HD = 128
 GROUPS = 4
+GATE_ROWS = 16
 SIDE = 16
 F32 = jnp.float32
 BF16 = jnp.bfloat16
@@ -17,8 +18,8 @@
 VMEM_LIMIT = 63 * 1024 * 1024
 
 
-def step_coef(timesteps):
-    fraction = timesteps.astype(F32) / 1000.0
+def step_coef(timestep, shape):
+    fraction = jnp.full(shape, timestep.astype(F32)) / 1000.0
     sigma_level = 0.7 * jnp.sqrt(fraction / (1.0 - fraction))
     return jnp.sqrt(jnp.float32(0.1)) / sigma_level
 
@@ -33,12 +34,12 @@
 
 
 def pack_body(
-    slot, own_ref, coef_ref, query_ref, key_ref, value_ref, noise_ref, old_ref, *refs
+    slot, steps_ref, query_ref, key_ref, value_ref, noise_ref, old_ref, *refs
 ):
     out_ref, misfit_ref = refs[-2:]
     pieces, _, width = out_ref.shape
     tokens = query_ref.shape[2]
-    coefficient = coef_ref[own_ref[0], slot]
+    coefficient = step_coef(steps_ref[lax.axis_index("expert"), slot], (8, width))[0:1]
 
     @pl.when(pl.program_id(0) == 0)
     def _():
@@ -56,18 +57,18 @@
         total = total + fold_rows(shift * (shift - 2.0 * noise), jnp.sum)
         for gate_ref in refs[:-2]:
             gates = gate_ref[0, :, columns]
-            blank = jnp.zeros((SIDE - gates.shape[0], width), BF16)
+            blank = jnp.zeros((GATE_ROWS - gates.shape[0], width), BF16)
             out_ref[piece, 4 * tokens :] = jnp.concatenate([gates, blank], axis=0)
     misfit_ref[...] = total
 
 
-def pack(slot, own, coefficient, arrays, gate_scale, groups):
+def pack(slot, timesteps, arrays, gate_scale, groups):
     _, _, tokens, full_width = arrays[0].shape
     width = full_width // groups
-    pieces = 8
+    pieces = 16
     rows = pl.BlockSpec((1, 1, tokens, pieces * width), lambda i: (0, slot, 0, i))
     gates = [] if gate_scale is None else [gate_scale]
-    held = 4 * tokens + SIDE * len(gates)
+    held = 4 * tokens + GATE_ROWS * len(gates)
     return pl.pallas_call(
         functools.partial(pack_body, slot),
         grid=(groups // pieces,),
@@ -75,7 +76,7 @@
             jax.ShapeDtypeStruct((groups, held, width), BF16),
             jax.ShapeDtypeStruct((8, width), F32),
         ),
-        in_specs=[pl.BlockSpec(memory_space=pltpu.SMEM)] * 2
+        in_specs=[pl.BlockSpec(memory_space=pltpu.SMEM)]
         + [rows] * 5
         + [pl.BlockSpec((1,) + g.shape[1:2] + (pieces * width,), lambda i: (0, 0, i)) for g in gates],
         out_specs=(
@@ -88,15 +89,14 @@
             bytes_accessed=18 * tokens * full_width,
             transcendentals=0,
         ),
-    )(own, coefficient, *arrays, *gates)
+    )(timesteps, *arrays, *gates)
 
 
 def attention_body(
     slot,
     block_rows,
     chunk,
-    own_ref,
-    coef_ref,
+    steps_ref,
     query_ref,
     key_ref,
     value_ref,
@@ -123,7 +123,7 @@
     step_set = pl.program_id(0)
     scale_factor = HD ** (-0.5)
     log2e = 1.4426950408889634
-    coefficient = coef_ref[step_set, slot]
+    coefficient = step_coef(steps_ref[step_set, slot], (8, block_rows))[0:1]
     q_rows[...] = query_ref[...].reshape(length, HD)
     k_rows[...] = key_ref[...].reshape(length, HD)
     v_rows[...] = value_ref[...].reshape(length, HD)
@@ -145,11 +145,11 @@
             block_scores = dot(k_rows[part, :], rows_query, NT)
             scores[part, :] = block_scores
             top = jnp.maximum(top, fold_rows(block_scores, jnp.max))
-        row_max = jnp.max(top, axis=0, keepdims=True) * (scale_factor * log2e)
+        row_max = jnp.max(top, axis=0, keepdims=True)
         sums = jnp.zeros((8, block_rows), F32)
         mixed = jnp.zeros((HD, block_rows), F32)
         for part in chunks:
-            raised = jnp.exp2(scores[part, :] * (scale_factor * log2e) - row_max)
+            raised = jnp.exp2((scores[part, :] - row_max) * (scale_factor * log2e))
             sums = sums + fold_rows(raised, jnp.sum)
             rounded = raised.astype(BF16)
             weights[part, :] = rounded
@@ -196,7 +196,7 @@
 
     gate_row = row_of(gate_total[...])
     local_row = jnp.sum(misfit_ref[...], axis=0, keepdims=True)
-    misfit_row = row_of(misfit_total[...]) + jnp.where(step_set == own_ref[0], local_row, 0.0)
+    misfit_row = row_of(misfit_total[...]) + jnp.where(step_set == lax.axis_index("expert"), local_row, 0.0)
     rest = misfit_row
     side = []
     for _ in range(3):
@@ -212,9 +212,9 @@
     )
 
 
-def attention(slot, own, coefficient, arrived, gates, misfit):
+def attention(slot, timesteps, arrived, gates, misfit):
     sets, groups, _, width = arrived.shape
-    tokens = arrived.shape[2] // (4 * SIDE) * SIDE
+    tokens = arrived.shape[2] // (4 * GATE_ROWS) * GATE_ROWS
     length = groups * tokens
     block_rows, chunk = 512, 512
 
@@ -225,10 +225,10 @@
         functools.partial(attention_body, slot, block_rows, chunk),
         grid=(sets,),
         out_shape=jax.ShapeDtypeStruct((sets, groups, 3 * tokens + SIDE, width), BF16),
-        in_specs=[pl.BlockSpec(memory_space=pltpu.SMEM)] * 2
+        in_specs=[pl.BlockSpec(memory_space=pltpu.SMEM)]
         + [field(which) for which in range(4)]
         + [
-            pl.BlockSpec((1, 1, SIDE, HD), lambda e: (e, 0, 4 * tokens // SIDE, 0)),
+            pl.BlockSpec((1, 1, GATE_ROWS, HD), lambda e: (e, 0, 4 * tokens // GATE_ROWS, 0)),
             pl.BlockSpec((8, HD), lambda e: (0, 0)),
         ],
         out_specs=pl.BlockSpec((1, groups, 3 * tokens + SIDE, HD), lambda e: (e, 0, 0, 0)),
@@ -248,7 +248,7 @@
             bytes_accessed=sets * 14 * length * width,
             transcendentals=sets * length * length,
         ),
-    )(own, coefficient, arrived, arrived, arrived, arrived, gates, misfit)
+    )(timesteps, arrived, arrived, arrived, arrived, gates, misfit)
 
 
 def unpack_body(slot, entries, weight_ref, kept_ref, main_ref, side_ref, *refs):
@@ -285,7 +285,7 @@
     tokens = (rows - SIDE) // 3
     full_width = heads * width
     entries = full_width * tokens * lax.axis_size("seq")
-    pieces = 8
+    pieces = 16
     whole = jax.ShapeDtypeStruct((1, slots, tokens, full_width), BF16)
     part = pl.BlockSpec((1, 1, tokens, pieces * width), lambda i: (0, slot, 0, i))
     in_specs = [
@@ -371,12 +371,10 @@
     heads = sets * groups
     width = full_width // heads
     expert_at = lax.axis_index("expert")
-    own = expert_at.astype(jnp.int32)[None]
 
     def own_expert(both):
         return lax.dynamic_index_in_dim(both, expert_at, 0, keepdims=False)
 
-    coefficient = step_coef(timesteps)
     arrays = (query_in, key_in, value_in, sample_noise, old_velocity)
     kept_mask = (
         jnp.arange(slots, dtype=jnp.int32)[None, :] < counts[:, 0][:, None]
@@ -404,14 +402,14 @@
     arrived, misfits = [], []
     for slot in range(slots):
         packed, misfit = pack(
-            slot, own, coefficient, arrays, gate_scale if slot == 0 else None, heads
+            slot, timesteps, arrays, gate_scale if slot == 0 else None, heads
         )
         arrived.append(exchange(packed).reshape((sets, groups) + packed.shape[1:]))
         misfits.append(misfit)
     returned = []
     for slot in range(slots):
         sent = attention(
-            slot, own, coefficient, arrived[slot], arrived[0], misfits[slot]
+            slot, timesteps, arrived[slot], arrived[0], misfits[slot]
         )
         returned.append(exchange(sent.reshape(heads, 3 * tokens + SIDE, width)))
     held = ()

time: 231 us -> 228 us (0.987)
  Pallas kernels: 96 us -> 91.3 us
  waiting for transfers between devices: 103 us -> 106 us
    all_to_all x4, waiting for transfers between devices: 99.5 us -> 102 us  [exchange(): lax.all_to_all(pieces, ('expert', 'seq'), split_axis=0, concat_axis=0, ti...]
where the time goes in v3:
time: 228 us; the launch traced here: 227 us
  waiting for transfers between devices  106 us (46%)
  Pallas kernels  91.3 us (40%)
  starting transfers between devices  28.3 us (12%)
    all_to_all x4, waiting for transfers between devices, exchange(): lax.all_to_all(pieces, ('expert', 'seq'), split_axis=0, concat_axis=0, ti...  102 us
    pallas_call x2, Pallas kernels, attention(): pl.pallas_call(functools.partial(attention_body, slot, block_rows, chunk)...  75.2 us
    all_to_all x4, starting transfers between devices, exchange(): lax.all_to_all(pieces, ('expert', 'seq'), split_axis=0, concat_axis=0, ti...  23 us
    pallas_call x2, Pallas kernels, pack(): pl.pallas_call(functools.partial(pack_body, slot), grid=(groups // pieces...  8.79 us
    pallas_call x2, Pallas kernels, unpack(): pl.pallas_call(body, grid=(heads // pieces,), out_shape=(whole, whole, wh...  7.33 us
    ppermute x3, starting transfers between devices, sum_over_replicas(): lax.ppermute(values, 'rep', [(at, (at + shift) % replicas) for at in rang...  5.3 us
  transfers between devices with their start and end apart: 7, of which 6 were waited for; matrix products, arithmetic and copies ran while one was open for 0% of the time, Pallas kernels for 37%

profile of v3, /device:TPU:0, one launch (start us, length us, event | category | flops | bytes accessed | tf_op | source)
XLA Modules:
  0.0 227.3 jit_solution(14605024119372769211)
XLA Ops:
  0.6 4.4 %shard_map.138 = (bf16[32,528,128]{2,1,0:T(8,128)(2,1)}, f32[8,128]{1,0:T(8,128)}) custom-call(s32[2,2]{1,0:T(2,128)} %steps_ref.7, bf16[1,2,128,4096]{3,2,1,0:T(8,128)(2,1)} %query_ref.3, bf16[1,2,128,4096]{3,2,1,0:T(8,128)(2,1)} %key_ref.3, bf16[1,2,128,4096]{3,2,1,0:T(8,128)(2,1)} %value_ref.3, bf16[1,2,128,4096]{3,2,1,0:T(8,128)(2,1)} %noise_ref.3, ...), custom_call_target="tpu_custom_call" | custom-call | flops 3145728 | bytes 9437184 | tf_op jit(solution)/shard_map/pallas_call | solution.py:72
  5.1 8.4 %all-to-all-start.1 = ((bf16[32,528,128]{2,1,0:T(8,128)(2,1)}), bf16[32,528,128]{2,1,0:T(8,128)(2,1)}, u32[]{:S(2)}, u32[]{:S(2)}) async-start(bf16[32,528,128]{2,1,0:T(8,128)(2,1)} %get-tuple-element.15), calls=%async_computation.1 | async-start | bytes 8650752 | tf_op jit(solution)/shard_map/all_to_all | solution.py:341
  13.4 4.4 %shard_map.137 = (bf16[32,512,128]{2,1,0:T(8,128)(2,1)}, f32[8,128]{1,0:T(8,128)}) custom-call(s32[2,2]{1,0:T(2,128)} %steps_ref.7, bf16[1,2,128,4096]{3,2,1,0:T(8,128)(2,1)} %query_ref.3, bf16[1,2,128,4096]{3,2,1,0:T(8,128)(2,1)} %key_ref.3, bf16[1,2,128,4096]{3,2,1,0:T(8,128)(2,1)} %value_ref.3, bf16[1,2,128,4096]{3,2,1,0:T(8,128)(2,1)} %noise_ref.3, ...), custom_call_target="tpu_custom_call" | custom-call | flops 3145728 | bytes 9437184 | tf_op jit(solution)/shard_map/pallas_call | solution.py:72
  17.8 50.8 %all-to-all-done.1 = bf16[32,528,128]{2,1,0:T(8,128)(2,1)} async-done(((bf16[32,528,128]{2,1,0:T(8,128)(2,1)}), bf16[32,528,128]{2,1,0:T(8,128)(2,1)}, u32[]{:S(2)}, u32[]{:S(2)}) %all-to-all-start.1) | async-done | bytes 4325408 | tf_op jit(solution)/shard_map/all_to_all | solution.py:341
  68.6 4.9 %all-to-all-start = ((bf16[32,512,128]{2,1,0:T(8,128)(2,1)}), bf16[32,512,128]{2,1,0:T(8,128)(2,1)}, u32[]{:S(2)}, u32[]{:S(2)}) async-start(bf16[32,512,128]{2,1,0:T(8,128)(2,1)} %get-tuple-element.14), calls=%async_computation | async-start | bytes 8388608 | tf_op jit(solution)/shard_map/all_to_all | solution.py:341
  73.5 37.6 %shard_map.140 = bf16[2,16,400,128]{3,2,1,0:T(8,128)(2,1)} custom-call(s32[2,2]{1,0:T(2,128)} %steps_ref.7, bf16[2,16,528,128]{3,2,1,0:T(8,128)(2,1)} %bitcast.9.gate_ref.query_ref.key_ref.value_ref.field_ref, bf16[2,16,528,128]{3,2,1,0:T(8,128)(2,1)} %bitcast.9.gate_ref.query_ref.key_ref.value_ref.field_ref, ...), custom_call_target="tpu_custom_call" | custom-call | flops 25769803776 | bytes 7340032 | tf_op jit(solution)/shard_map/pallas_call | solution.py:224
  111.1 16.1 %all-to-all-done = bf16[32,512,128]{2,1,0:T(8,128)(2,1)} async-done(((bf16[32,512,128]{2,1,0:T(8,128)(2,1)}), bf16[32,512,128]{2,1,0:T(8,128)(2,1)}, u32[]{:S(2)}, u32[]{:S(2)}) %all-to-all-start) | async-done | bytes 4194336 | tf_op jit(solution)/shard_map/all_to_all | solution.py:341
  127.1 4.8 %all-to-all-start.3 = ((bf16[32,400,128]{2,1,0:T(8,128)(2,1)}), bf16[32,400,128]{2,1,0:T(8,128)(2,1)}, u32[]{:S(2)}, u32[]{:S(2)}) async-start(bf16[32,400,128]{2,1,0:T(8,128)(2,1)} %bitcast.22), calls=%async_computation.3 | async-start | bytes 6553600 | tf_op jit(solution)/shard_map/all_to_all | solution.py:341
  132.0 37.6 %shard_map.139 = bf16[2,16,400,128]{3,2,1,0:T(8,128)(2,1)} custom-call(s32[2,2]{1,0:T(2,128)} %steps_ref.7, bf16[2,16,512,128]{3,2,1,0:T(8,128)(2,1)} %bitcast.8.query_ref.key_ref.value_ref.field_ref, bf16[2,16,512,128]{3,2,1,0:T(8,128)(2,1)} %bitcast.8.query_ref.key_ref.value_ref.field_ref, ...), custom_call_target="tpu_custom_call" | custom-call | flops 25769803776 | bytes 7340032 | tf_op jit(solution)/shard_map/pallas_call | solution.py:224
  169.6 5.7 %all-to-all-done.3.main_ref.side_ref = bf16[32,400,128]{2,1,0:T(8,128)(2,1)} async-done(((bf16[32,400,128]{2,1,0:T(8,128)(2,1)}), bf16[32,400,128]{2,1,0:T(8,128)(2,1)}, u32[]{:S(2)}, u32[]{:S(2)}) %all-to-all-start.3) | async-done | bytes 3276832 | tf_op jit(solution)/shard_map/all_to_all | solution.py:341
  175.3 0.0 copy-start
  175.3 0.0 copy-start.2
  175.3 0.0 copy-start.1
  175.3 5.0 %all-to-all-start.2 = ((bf16[32,400,128]{2,1,0:T(8,128)(2,1)}), bf16[32,400,128]{2,1,0:T(8,128)(2,1)}, u32[]{:S(2)}, u32[]{:S(2)}) async-start(bf16[32,400,128]{2,1,0:T(8,128)(2,1)} %bitcast.21), calls=%async_computation.2 | async-start | bytes 6553600 | tf_op jit(solution)/shard_map/all_to_all | solution.py:341
  180.3 0.0 copy-done
  180.3 0.0 copy-done.2
  180.3 0.1 fusion.3
  180.4 0.0 copy-done.1
  180.4 0.1 select_reduce_fusion
  180.5 3.3 %collective-permute-start.1 = (f32[3,4]{1,0:T(4,128)S(1)}, f32[3,4]{1,0:T(4,128)S(1)}, u32[]{:S(2)}, u32[]{:S(2)}) collective-permute-start(f32[3,4]{1,0:T(4,128)S(1)} %pad_maximum_fusion), channel_id=1, source_target_pairs={{0,32},{16,48},{32,0},{48,16},{1,33},{17,49},{33,1},{49,17},{2,34}... | collective-permute-start | bytes 152 | tf_op jit(solution)/shard_map/ppermute | solution.py:348
  183.8 1.1 collective-permute-start.2
  184.8 1.0 collective-permute-start
  185.8 0.0 collective-permute-done.1
  185.8 1.6 collective-permute-done.2
  187.4 2.3 collective-permute-done
  189.6 0.2 select_reduce_fusion.2
  189.8 0.1 fusion.2
  189.9 0.6 dynamic-slice_bitcast_fusion
  190.5 3.6 %shard_map.141 = (bf16[1,2,128,4096]{3,2,1,0:T(8,128)(2,1)}, bf16[1,2,128,4096]{3,2,1,0:T(8,128)(2,1)}, bf16[1,2,128,4096]{3,2,1,0:T(8,128)(2,1)}, f32[1,4096]{1,0:T(1,128)}, f32[1,128]{1,0:T(1,128)}) custom-call(f32[2]{0:T(128)} %get-tuple-element.31.weight_ref, f32[2]{0:T(128)} %get-tuple-element.30.kept_ref, ...), custom_call_target="tpu_custom_call" | custom-call | flops 1572864 | bytes 6291456 | tf_op jit(solution)/shard_map/pallas_call | solution.py:324
  194.1 29.5 %all-to-all-done.2.main_ref.side_ref = bf16[32,400,128]{2,1,0:T(8,128)(2,1)} async-done(((bf16[32,400,128]{2,1,0:T(8,128)(2,1)}), bf16[32,400,128]{2,1,0:T(8,128)(2,1)}, u32[]{:S(2)}, u32[]{:S(2)}) %all-to-all-start.2) | async-done | bytes 3276832 | tf_op jit(solution)/shard_map/all_to_all | solution.py:341
  223.6 3.7 %shard_map.142 = (bf16[1,2,128,4096]{3,2,1,0:T(8,128)(2,1)}, bf16[1,2,128,4096]{3,2,1,0:T(8,128)(2,1)}, bf16[1,2,128,4096]{3,2,1,0:T(8,128)(2,1)}, bf16[1,2,4096]{2,1,0:T(2,128)(2,1)}, bf16[1,2]{1,0:T(2,128)(2,1)}) custom-call(f32[2]{0:T(128)} %get-tuple-element.31.weight_ref, ...), custom_call_target="tpu_custom_call", output_to_operand_aliasing={{0}: (4, {}), {1}: (5, {}), {2}: (6, {})} | custom-call | flops 1572864 | bytes 6291456 | tf_op jit(solution)/shard_map/pallas_call | solution.py:324
  (4 shorter events, 0.0 us)
Async XLA Ops:
  5.1 63.5 %all-to-all-start.1 = ((bf16[32,528,128]{2,1,0:T(8,128)(2,1)}), bf16[32,528,128]{2,1,0:T(8,128)(2,1)}, u32[]{:S(2)}, u32[]{:S(2)}) async-start(bf16[32,528,128]{2,1,0:T(8,128)(2,1)} %get-tuple-element.15), calls=%async_computation.1 | async-start | bytes 8650752 | tf_op jit(solution)/shard_map/all_to_all | solution.py:341
  68.6 58.5 %all-to-all-start = ((bf16[32,512,128]{2,1,0:T(8,128)(2,1)}), bf16[32,512,128]{2,1,0:T(8,128)(2,1)}, u32[]{:S(2)}, u32[]{:S(2)}) async-start(bf16[32,512,128]{2,1,0:T(8,128)(2,1)} %get-tuple-element.14), calls=%async_computation | async-start | bytes 8388608 | tf_op jit(solution)/shard_map/all_to_all | solution.py:341
  127.1 48.2 %all-to-all-start.3 = ((bf16[32,400,128]{2,1,0:T(8,128)(2,1)}), bf16[32,400,128]{2,1,0:T(8,128)(2,1)}, u32[]{:S(2)}, u32[]{:S(2)}) async-start(bf16[32,400,128]{2,1,0:T(8,128)(2,1)} %bitcast.22), calls=%async_computation.3 | async-start | bytes 6553600 | tf_op jit(solution)/shard_map/all_to_all | solution.py:341
  175.3 5.0 %copy-start = (f32[2,2]{1,0:T(2,128)S(1)}, f32[2,2]{1,0:T(2,128)}, u32[]{:S(2)}) copy-start(f32[2,2]{1,0:T(2,128)} %param.16) | copy-start | bytes 52
  175.3 5.0 %copy-start.2 = (s32[2,1]{0,1:T(1,128)S(1)}, s32[2,1]{0,1:T(1,128)}, u32[]{:S(2)}) copy-start(s32[2,1]{0,1:T(1,128)} %param.19) | copy-start | bytes 28
  175.3 5.1 %copy-start.1 = (s32[2,2]{1,0:T(2,128)S(1)}, s32[2,2]{1,0:T(2,128)}, u32[]{:S(2)}) copy-start(s32[2,2]{1,0:T(2,128)} %param.17) | copy-start | bytes 52
  175.3 48.3 %all-to-all-start.2 = ((bf16[32,400,128]{2,1,0:T(8,128)(2,1)}), bf16[32,400,128]{2,1,0:T(8,128)(2,1)}, u32[]{:S(2)}, u32[]{:S(2)}) async-start(bf16[32,400,128]{2,1,0:T(8,128)(2,1)} %bitcast.21), calls=%async_computation.2 | async-start | bytes 6553600 | tf_op jit(solution)/shard_map/all_to_all | solution.py:341
  180.5 5.3 %collective-permute-start.1 = (f32[3,4]{1,0:T(4,128)S(1)}, f32[3,4]{1,0:T(4,128)S(1)}, u32[]{:S(2)}, u32[]{:S(2)}) collective-permute-start(f32[3,4]{1,0:T(4,128)S(1)} %pad_maximum_fusion), channel_id=1, source_target_pairs={{0,32},{16,48},{32,0},{48,16},{1,33},{17,49},{33,1},{49,17},{2,34}... | collective-permute-start | bytes 152 | tf_op jit(solution)/shard_map/ppermute | solution.py:348
  183.8 3.6 %collective-permute-start.2 = (f32[3,4]{1,0:T(4,128)S(1)}, f32[3,4]{1,0:T(4,128)S(1)}, u32[]{:S(2)}, u32[]{:S(2)}) collective-permute-start(f32[3,4]{1,0:T(4,128)S(1)} %pad_maximum_fusion), channel_id=1, source_target_pairs={{0,48},{16,0},{32,16},{48,32},{1,49},{17,1},{33,17},{49,33},{2,50}... | collective-permute-start | bytes 152 | tf_op jit(solution)/shard_map/ppermute | solution.py:348
  184.8 4.8 %collective-permute-start = (f32[3,4]{1,0:T(4,128)S(1)}, f32[3,4]{1,0:T(4,128)S(1)}, u32[]{:S(2)}, u32[]{:S(2)}) collective-permute-start(f32[3,4]{1,0:T(4,128)S(1)} %pad_maximum_fusion), channel_id=1, source_target_pairs={{0,16},{16,32},{32,48},{48,0},{1,17},{17,33},{33,49},{49,1},{2,18}... | collective-permute-start | bytes 152 | tf_op jit(solution)/shard_map/ppermute | solution.py:348

commit v4 on v3

--- a/solution.py
+++ b/solution.py
@@ -147,21 +147,23 @@
             top = jnp.maximum(top, fold_rows(block_scores, jnp.max))
         row_max = jnp.max(top, axis=0, keepdims=True)
         sums = jnp.zeros((8, block_rows), F32)
-        mixed = jnp.zeros((HD, block_rows), F32)
         for part in chunks:
             raised = jnp.exp2((scores[part, :] - row_max) * (scale_factor * log2e))
             sums = sums + fold_rows(raised, jnp.sum)
-            rounded = raised.astype(BF16)
+            scores[part, :] = raised
+        inverse = 1.0 / jnp.sum(sums, axis=0, keepdims=True)
+        mixed = jnp.zeros((HD, block_rows), F32)
+        for part in chunks:
+            rounded = (scores[part, :] * inverse).astype(BF16)
             weights[part, :] = rounded
             mixed = mixed + dot(v_cols[:, part], rounded)
-        inverse = 1.0 / jnp.sum(sums, axis=0, keepdims=True)
-        attended = (mixed * inverse).astype(BF16).astype(F32)
+        attended = mixed.astype(BF16).astype(F32)
         field = field_cols[:, pl.ds(start, block_rows)].astype(F32)
         moved = coefficient * (gate * attended)
         misfit_total[...] += moved * (2.0 * field + moved)
         grad_gap = coefficient * (field + moved)
         gate_total[...] += grad_gap * attended
-        grad_cols = (grad_gap * gate * inverse).astype(BF16)
+        grad_cols = (grad_gap * gate).astype(BF16)
         grad_rows = grad_cols.T
         row_dot = jnp.sum(grad_cols.astype(F32) * attended, axis=0, keepdims=True)
         grad_query = jnp.zeros((HD, block_rows), F32)

time: 228 us -> 228 us (level)
  waiting for transfers between devices: 106 us -> 100 us
  Pallas kernels: 91.3 us -> 97 us
    all_to_all x4, waiting for transfers between devices: 102 us -> 96.2 us  [exchange(): lax.all_to_all(pieces, ('expert', 'seq'), split_axis=0, concat_axis=0, ti...]
    pallas_call x2, Pallas kernels: 75.2 us -> 80.9 us  [attention(): pl.pallas_call(functools.partial(attention_body, slot, block_rows, chunk)...]
  transfers between devices with their start and end apart: 7 -> 7, of which waited for: 6 -> 6; matrix products, arithmetic and copies ran while one was open for 0% -> 0% of each run, Pallas kernels for 37% -> 39%
where the time goes in v4:
time: 228 us; the launch traced here: 227 us
  waiting for transfers between devices  100 us (44%)
  Pallas kernels  97 us (43%)
  starting transfers between devices  28.5 us (12%)
    all_to_all x4, waiting for transfers between devices, exchange(): lax.all_to_all(pieces, ('expert', 'seq'), split_axis=0, concat_axis=0, ti...  96.2 us
    pallas_call x2, Pallas kernels, attention(): pl.pallas_call(functools.partial(attention_body, slot, block_rows, chunk)...  80.9 us
    all_to_all x4, starting transfers between devices, exchange(): lax.all_to_all(pieces, ('expert', 'seq'), split_axis=0, concat_axis=0, ti...  23.2 us
    pallas_call x2, Pallas kernels, pack(): pl.pallas_call(functools.partial(pack_body, slot), grid=(groups // pieces...  8.79 us
    pallas_call x2, Pallas kernels, unpack(): pl.pallas_call(body, grid=(heads // pieces,), out_shape=(whole, whole, wh...  7.33 us
    ppermute x3, starting transfers between devices, sum_over_replicas(): lax.ppermute(values, 'rep', [(at, (at + shift) % replicas) for at in rang...  5.3 us
  transfers between devices with their start and end apart: 7, of which 6 were waited for; matrix products, arithmetic and copies ran while one was open for 0% of the time, Pallas kernels for 39%

profile of v4, /device:TPU:0, one launch (start us, length us, event | category | flops | bytes accessed | tf_op | source)
XLA Modules:
  0.0 227.4 jit_solution(15584356306639296634)
XLA Ops:
  0.6 4.4 %shard_map.138 = (bf16[32,528,128]{2,1,0:T(8,128)(2,1)}, f32[8,128]{1,0:T(8,128)}) custom-call(s32[2,2]{1,0:T(2,128)} %steps_ref.7, bf16[1,2,128,4096]{3,2,1,0:T(8,128)(2,1)} %query_ref.3, bf16[1,2,128,4096]{3,2,1,0:T(8,128)(2,1)} %key_ref.3, bf16[1,2,128,4096]{3,2,1,0:T(8,128)(2,1)} %value_ref.3, bf16[1,2,128,4096]{3,2,1,0:T(8,128)(2,1)} %noise_ref.3, ...), custom_call_target="tpu_custom_call" | custom-call | flops 3145728 | bytes 9437184 | tf_op jit(solution)/shard_map/pallas_call | solution.py:72
  5.1 8.4 %all-to-all-start.1 = ((bf16[32,528,128]{2,1,0:T(8,128)(2,1)}), bf16[32,528,128]{2,1,0:T(8,128)(2,1)}, u32[]{:S(2)}, u32[]{:S(2)}) async-start(bf16[32,528,128]{2,1,0:T(8,128)(2,1)} %get-tuple-element.15), calls=%async_computation.1 | async-start | bytes 8650752 | tf_op jit(solution)/shard_map/all_to_all | solution.py:343
  13.4 4.4 %shard_map.137 = (bf16[32,512,128]{2,1,0:T(8,128)(2,1)}, f32[8,128]{1,0:T(8,128)}) custom-call(s32[2,2]{1,0:T(2,128)} %steps_ref.7, bf16[1,2,128,4096]{3,2,1,0:T(8,128)(2,1)} %query_ref.3, bf16[1,2,128,4096]{3,2,1,0:T(8,128)(2,1)} %key_ref.3, bf16[1,2,128,4096]{3,2,1,0:T(8,128)(2,1)} %value_ref.3, bf16[1,2,128,4096]{3,2,1,0:T(8,128)(2,1)} %noise_ref.3, ...), custom_call_target="tpu_custom_call" | custom-call | flops 3145728 | bytes 9437184 | tf_op jit(solution)/shard_map/pallas_call | solution.py:72
  17.8 50.8 %all-to-all-done.1 = bf16[32,528,128]{2,1,0:T(8,128)(2,1)} async-done(((bf16[32,528,128]{2,1,0:T(8,128)(2,1)}), bf16[32,528,128]{2,1,0:T(8,128)(2,1)}, u32[]{:S(2)}, u32[]{:S(2)}) %all-to-all-start.1) | async-done | bytes 4325408 | tf_op jit(solution)/shard_map/all_to_all | solution.py:343
  68.6 4.9 %all-to-all-start = ((bf16[32,512,128]{2,1,0:T(8,128)(2,1)}), bf16[32,512,128]{2,1,0:T(8,128)(2,1)}, u32[]{:S(2)}, u32[]{:S(2)}) async-start(bf16[32,512,128]{2,1,0:T(8,128)(2,1)} %get-tuple-element.14), calls=%async_computation | async-start | bytes 8388608 | tf_op jit(solution)/shard_map/all_to_all | solution.py:343
  73.5 40.4 %shard_map.140 = bf16[2,16,400,128]{3,2,1,0:T(8,128)(2,1)} custom-call(s32[2,2]{1,0:T(2,128)} %steps_ref.7, bf16[2,16,528,128]{3,2,1,0:T(8,128)(2,1)} %bitcast.9.gate_ref.query_ref.key_ref.value_ref.field_ref, bf16[2,16,528,128]{3,2,1,0:T(8,128)(2,1)} %bitcast.9.gate_ref.query_ref.key_ref.value_ref.field_ref, ...), custom_call_target="tpu_custom_call" | custom-call | flops 25769803776 | bytes 7340032 | tf_op jit(solution)/shard_map/pallas_call | solution.py:226
  113.9 13.2 %all-to-all-done = bf16[32,512,128]{2,1,0:T(8,128)(2,1)} async-done(((bf16[32,512,128]{2,1,0:T(8,128)(2,1)}), bf16[32,512,128]{2,1,0:T(8,128)(2,1)}, u32[]{:S(2)}, u32[]{:S(2)}) %all-to-all-start) | async-done | bytes 4194336 | tf_op jit(solution)/shard_map/all_to_all | solution.py:343
  127.1 5.0 %all-to-all-start.3 = ((bf16[32,400,128]{2,1,0:T(8,128)(2,1)}), bf16[32,400,128]{2,1,0:T(8,128)(2,1)}, u32[]{:S(2)}, u32[]{:S(2)}) async-start(bf16[32,400,128]{2,1,0:T(8,128)(2,1)} %bitcast.22), calls=%async_computation.3 | async-start | bytes 6553600 | tf_op jit(solution)/shard_map/all_to_all | solution.py:343
  132.2 40.4 %shard_map.139 = bf16[2,16,400,128]{3,2,1,0:T(8,128)(2,1)} custom-call(s32[2,2]{1,0:T(2,128)} %steps_ref.7, bf16[2,16,512,128]{3,2,1,0:T(8,128)(2,1)} %bitcast.8.query_ref.key_ref.value_ref.field_ref, bf16[2,16,512,128]{3,2,1,0:T(8,128)(2,1)} %bitcast.8.query_ref.key_ref.value_ref.field_ref, ...), custom_call_target="tpu_custom_call" | custom-call | flops 25769803776 | bytes 7340032 | tf_op jit(solution)/shard_map/pallas_call | solution.py:226
  172.6 2.7 %all-to-all-done.3.main_ref.side_ref = bf16[32,400,128]{2,1,0:T(8,128)(2,1)} async-done(((bf16[32,400,128]{2,1,0:T(8,128)(2,1)}), bf16[32,400,128]{2,1,0:T(8,128)(2,1)}, u32[]{:S(2)}, u32[]{:S(2)}) %all-to-all-start.3) | async-done | bytes 3276832 | tf_op jit(solution)/shard_map/all_to_all | solution.py:343
  175.3 0.0 copy-start
  175.3 0.0 copy-start.2
  175.3 0.0 copy-start.1
  175.3 5.0 %all-to-all-start.2 = ((bf16[32,400,128]{2,1,0:T(8,128)(2,1)}), bf16[32,400,128]{2,1,0:T(8,128)(2,1)}, u32[]{:S(2)}, u32[]{:S(2)}) async-start(bf16[32,400,128]{2,1,0:T(8,128)(2,1)} %bitcast.21), calls=%async_computation.2 | async-start | bytes 6553600 | tf_op jit(solution)/shard_map/all_to_all | solution.py:343
  180.3 0.0 copy-done
  180.3 0.0 copy-done.2
  180.3 0.1 fusion.3
  180.4 0.0 copy-done.1
  180.4 0.1 select_reduce_fusion
  180.5 3.3 %collective-permute-start.1 = (f32[3,4]{1,0:T(4,128)S(1)}, f32[3,4]{1,0:T(4,128)S(1)}, u32[]{:S(2)}, u32[]{:S(2)}) collective-permute-start(f32[3,4]{1,0:T(4,128)S(1)} %pad_maximum_fusion), channel_id=1, source_target_pairs={{0,32},{16,48},{32,0},{48,16},{1,33},{17,49},{33,1},{49,17},{2,34}... | collective-permute-start | bytes 152 | tf_op jit(solution)/shard_map/ppermute | solution.py:350
  183.8 1.1 collective-permute-start.2
  184.8 1.0 collective-permute-start
  185.8 0.0 collective-permute-done.1
  185.8 1.6 collective-permute-done.2
  187.4 2.3 collective-permute-done
  189.6 0.2 select_reduce_fusion.2
  189.8 0.1 fusion.2
  189.9 0.6 dynamic-slice_bitcast_fusion
  190.5 3.6 %shard_map.141 = (bf16[1,2,128,4096]{3,2,1,0:T(8,128)(2,1)}, bf16[1,2,128,4096]{3,2,1,0:T(8,128)(2,1)}, bf16[1,2,128,4096]{3,2,1,0:T(8,128)(2,1)}, f32[1,4096]{1,0:T(1,128)}, f32[1,128]{1,0:T(1,128)}) custom-call(f32[2]{0:T(128)} %get-tuple-element.31.weight_ref, f32[2]{0:T(128)} %get-tuple-element.30.kept_ref, ...), custom_call_target="tpu_custom_call" | custom-call | flops 1572864 | bytes 6291456 | tf_op jit(solution)/shard_map/pallas_call | solution.py:326
  194.1 29.5 %all-to-all-done.2.main_ref.side_ref = bf16[32,400,128]{2,1,0:T(8,128)(2,1)} async-done(((bf16[32,400,128]{2,1,0:T(8,128)(2,1)}), bf16[32,400,128]{2,1,0:T(8,128)(2,1)}, u32[]{:S(2)}, u32[]{:S(2)}) %all-to-all-start.2) | async-done | bytes 3276832 | tf_op jit(solution)/shard_map/all_to_all | solution.py:343
  223.6 3.7 %shard_map.142 = (bf16[1,2,128,4096]{3,2,1,0:T(8,128)(2,1)}, bf16[1,2,128,4096]{3,2,1,0:T(8,128)(2,1)}, bf16[1,2,128,4096]{3,2,1,0:T(8,128)(2,1)}, bf16[1,2,4096]{2,1,0:T(2,128)(2,1)}, bf16[1,2]{1,0:T(2,128)(2,1)}) custom-call(f32[2]{0:T(128)} %get-tuple-element.31.weight_ref, ...), custom_call_target="tpu_custom_call", output_to_operand_aliasing={{0}: (4, {}), {1}: (5, {}), {2}: (6, {})} | custom-call | flops 1572864 | bytes 6291456 | tf_op jit(solution)/shard_map/pallas_call | solution.py:326
  (4 shorter events, 0.0 us)
Async XLA Ops:
  5.1 63.5 %all-to-all-start.1 = ((bf16[32,528,128]{2,1,0:T(8,128)(2,1)}), bf16[32,528,128]{2,1,0:T(8,128)(2,1)}, u32[]{:S(2)}, u32[]{:S(2)}) async-start(bf16[32,528,128]{2,1,0:T(8,128)(2,1)} %get-tuple-element.15), calls=%async_computation.1 | async-start | bytes 8650752 | tf_op jit(solution)/shard_map/all_to_all | solution.py:343
  68.6 58.5 %all-to-all-start = ((bf16[32,512,128]{2,1,0:T(8,128)(2,1)}), bf16[32,512,128]{2,1,0:T(8,128)(2,1)}, u32[]{:S(2)}, u32[]{:S(2)}) async-start(bf16[32,512,128]{2,1,0:T(8,128)(2,1)} %get-tuple-element.14), calls=%async_computation | async-start | bytes 8388608 | tf_op jit(solution)/shard_map/all_to_all | solution.py:343
  127.1 48.2 %all-to-all-start.3 = ((bf16[32,400,128]{2,1,0:T(8,128)(2,1)}), bf16[32,400,128]{2,1,0:T(8,128)(2,1)}, u32[]{:S(2)}, u32[]{:S(2)}) async-start(bf16[32,400,128]{2,1,0:T(8,128)(2,1)} %bitcast.22), calls=%async_computation.3 | async-start | bytes 6553600 | tf_op jit(solution)/shard_map/all_to_all | solution.py:343
  175.3 5.0 %copy-start = (f32[2,2]{1,0:T(2,128)S(1)}, f32[2,2]{1,0:T(2,128)}, u32[]{:S(2)}) copy-start(f32[2,2]{1,0:T(2,128)} %param.16) | copy-start | bytes 52
  175.3 5.0 %copy-start.2 = (s32[2,1]{0,1:T(1,128)S(1)}, s32[2,1]{0,1:T(1,128)}, u32[]{:S(2)}) copy-start(s32[2,1]{0,1:T(1,128)} %param.19) | copy-start | bytes 28
  175.3 5.1 %copy-start.1 = (s32[2,2]{1,0:T(2,128)S(1)}, s32[2,2]{1,0:T(2,128)}, u32[]{:S(2)}) copy-start(s32[2,2]{1,0:T(2,128)} %param.17) | copy-start | bytes 52
  175.3 48.3 %all-to-all-start.2 = ((bf16[32,400,128]{2,1,0:T(8,128)(2,1)}), bf16[32,400,128]{2,1,0:T(8,128)(2,1)}, u32[]{:S(2)}, u32[]{:S(2)}) async-start(bf16[32,400,128]{2,1,0:T(8,128)(2,1)} %bitcast.21), calls=%async_computation.2 | async-start | bytes 6553600 | tf_op jit(solution)/shard_map/all_to_all | solution.py:343
  180.5 5.3 %collective-permute-start.1 = (f32[3,4]{1,0:T(4,128)S(1)}, f32[3,4]{1,0:T(4,128)S(1)}, u32[]{:S(2)}, u32[]{:S(2)}) collective-permute-start(f32[3,4]{1,0:T(4,128)S(1)} %pad_maximum_fusion), channel_id=1, source_target_pairs={{0,32},{16,48},{32,0},{48,16},{1,33},{17,49},{33,1},{49,17},{2,34}... | collective-permute-start | bytes 152 | tf_op jit(solution)/shard_map/ppermute | solution.py:350
  183.8 3.6 %collective-permute-start.2 = (f32[3,4]{1,0:T(4,128)S(1)}, f32[3,4]{1,0:T(4,128)S(1)}, u32[]{:S(2)}, u32[]{:S(2)}) collective-permute-start(f32[3,4]{1,0:T(4,128)S(1)} %pad_maximum_fusion), channel_id=1, source_target_pairs={{0,48},{16,0},{32,16},{48,32},{1,49},{17,1},{33,17},{49,33},{2,50}... | collective-permute-start | bytes 152 | tf_op jit(solution)/shard_map/ppermute | solution.py:350
  184.8 4.8 %collective-permute-start = (f32[3,4]{1,0:T(4,128)S(1)}, f32[3,4]{1,0:T(4,128)S(1)}, u32[]{:S(2)}, u32[]{:S(2)}) collective-permute-start(f32[3,4]{1,0:T(4,128)S(1)} %pad_maximum_fusion), channel_id=1, source_target_pairs={{0,16},{16,32},{32,48},{48,0},{1,17},{17,33},{33,49},{49,1},{2,18}... | collective-permute-start | bytes 152 | tf_op jit(solution)/shard_map/ppermute | solution.py:350

commit v5 on v4

--- a/solution.py
+++ b/solution.py
@@ -9,7 +9,6 @@
 
 HD = 128
 GROUPS = 4
-GATE_ROWS = 16
 SIDE = 16
 F32 = jnp.float32
 BF16 = jnp.bfloat16
@@ -34,9 +33,8 @@
 
 
 def pack_body(
-    slot, steps_ref, query_ref, key_ref, value_ref, noise_ref, old_ref, *refs
+    slot, steps_ref, query_ref, key_ref, value_ref, noise_ref, old_ref, out_ref, misfit_ref
 ):
-    out_ref, misfit_ref = refs[-2:]
     pieces, _, width = out_ref.shape
     tokens = query_ref.shape[2]
     coefficient = step_coef(steps_ref[lax.axis_index("expert"), slot], (8, width))[0:1]
@@ -55,20 +53,15 @@
         shift = coefficient * old_ref[0, 0, :, columns].astype(F32)
         out_ref[piece, 3 * tokens : 4 * tokens] = (noise - shift).astype(BF16)
         total = total + fold_rows(shift * (shift - 2.0 * noise), jnp.sum)
-        for gate_ref in refs[:-2]:
-            gates = gate_ref[0, :, columns]
-            blank = jnp.zeros((GATE_ROWS - gates.shape[0], width), BF16)
-            out_ref[piece, 4 * tokens :] = jnp.concatenate([gates, blank], axis=0)
     misfit_ref[...] = total
 
 
-def pack(slot, timesteps, arrays, gate_scale, groups):
+def pack(slot, timesteps, arrays, groups):
     _, _, tokens, full_width = arrays[0].shape
     width = full_width // groups
     pieces = 16
     rows = pl.BlockSpec((1, 1, tokens, pieces * width), lambda i: (0, slot, 0, i))
-    gates = [] if gate_scale is None else [gate_scale]
-    held = 4 * tokens + GATE_ROWS * len(gates)
+    held = 4 * tokens
     return pl.pallas_call(
         functools.partial(pack_body, slot),
         grid=(groups // pieces,),
@@ -76,9 +69,7 @@
             jax.ShapeDtypeStruct((groups, held, width), BF16),
             jax.ShapeDtypeStruct((8, width), F32),
         ),
-        in_specs=[pl.BlockSpec(memory_space=pltpu.SMEM)]
-        + [rows] * 5
-        + [pl.BlockSpec((1,) + g.shape[1:2] + (pieces * width,), lambda i: (0, 0, i)) for g in gates],
+        in_specs=[pl.BlockSpec(memory_space=pltpu.SMEM)] + [rows] * 5,
         out_specs=(
             pl.BlockSpec((pieces, held, width), lambda i: (i, 0, 0)),
             pl.BlockSpec((8, width), lambda i: (0, 0)),
@@ -89,7 +80,7 @@
             bytes_accessed=18 * tokens * full_width,
             transcendentals=0,
         ),
-    )(timesteps, *arrays, *gates)
+    )(timesteps, *arrays)
 
 
 def attention_body(
@@ -130,7 +121,7 @@
     k_cols[...] = k_rows[...].T
     v_cols[...] = v_rows[...].T
     field_cols[...] = field_ref[...].reshape(length, HD).T
-    gate_row = gate_ref[0, 0, slot : slot + 1, :].astype(F32)
+    gate_row = gate_ref[0, slot : slot + 1, :].astype(F32)
     gate = jnp.broadcast_to(gate_row, (8, HD)).T[:, 0:1]
     gate_total[...] = jnp.zeros_like(gate_total)
     misfit_total[...] = jnp.zeros_like(misfit_total)
@@ -216,7 +207,7 @@
 
 def attention(slot, timesteps, arrived, gates, misfit):
     sets, groups, _, width = arrived.shape
-    tokens = arrived.shape[2] // (4 * GATE_ROWS) * GATE_ROWS
+    tokens = arrived.shape[2] // 4
     length = groups * tokens
     block_rows, chunk = 512, 512
 
@@ -230,7 +221,7 @@
         in_specs=[pl.BlockSpec(memory_space=pltpu.SMEM)]
         + [field(which) for which in range(4)]
         + [
-            pl.BlockSpec((1, 1, GATE_ROWS, HD), lambda e: (e, 0, 4 * tokens // GATE_ROWS, 0)),
+            pl.BlockSpec((1,) + gates.shape[1:], lambda e: (e, 0, 0)),
             pl.BlockSpec((8, HD), lambda e: (0, 0)),
         ],
         out_specs=pl.BlockSpec((1, groups, 3 * tokens + SIDE, HD), lambda e: (e, 0, 0, 0)),
@@ -401,17 +392,24 @@
     kept_here = own_expert(kept_mask)
     weight = own_expert(kept_mask * advantage)
 
+    gate_own = gate_scale[0]
+    gate_other = lax.ppermute(gate_own, "expert", [(0, 1), (1, 0)])
     arrived, misfits = [], []
     for slot in range(slots):
-        packed, misfit = pack(
-            slot, timesteps, arrays, gate_scale if slot == 0 else None, heads
-        )
+        packed, misfit = pack(slot, timesteps, arrays, heads)
+        if slot == 1:
+            packed, gate_other = lax.optimization_barrier((packed, gate_other))
         arrived.append(exchange(packed).reshape((sets, groups) + packed.shape[1:]))
         misfits.append(misfit)
+    gates = jnp.where(
+        expert_at == 0, jnp.stack([gate_own, gate_other]), jnp.stack([gate_other, gate_own])
+    )
+    head_at = expert_at * groups + lax.axis_index("seq")
+    gates = lax.dynamic_slice_in_dim(gates, head_at * width, width, 2)
     returned = []
     for slot in range(slots):
         sent = attention(
-            slot, timesteps, arrived[slot], arrived[0], misfits[slot]
+            slot, timesteps, arrived[slot], gates, misfits[slot]
         )
         returned.append(exchange(sent.reshape(heads, 3 * tokens + SIDE, width)))
     held = ()

time: 228 us -> 226 us (level)
  waiting for transfers between devices: 100 us -> 96.1 us
    all_to_all x4, waiting for transfers between devices: 96.2 us -> 52.8 us  [exchange(): lax.all_to_all(pieces, ('expert', 'seq'), split_axis=0, concat_axis=0, ti...]
    ppermute x0 -> x1, waiting for transfers between devices: none -> 39.5 us  [local(): gate_other = lax.ppermute(gate_own, 'expert', [(0, 1), (1, 0)])]
  transfers between devices with their start and end apart: 7 -> 8, of which waited for: 6 -> 7; matrix products, arithmetic and copies ran while one was open for 0% -> 1% of each run, Pallas kernels for 39% -> 39%
where the time goes in v5:
time: 226 us
  Pallas kernels  96.9 us (43%)
  waiting for transfers between devices  96.1 us (43%)
  starting transfers between devices  30.4 us (13%)
    pallas_call x2, Pallas kernels, attention(): pl.pallas_call(functools.partial(attention_body, slot, block_rows, chunk)...  80.9 us
    all_to_all x4, waiting for transfers between devices, exchange(): lax.all_to_all(pieces, ('expert', 'seq'), split_axis=0, concat_axis=0, ti...  52.8 us
    ppermute x1, waiting for transfers between devices, local(): gate_other = lax.ppermute(gate_own, 'expert', [(0, 1), (1, 0)])  39.5 us
    all_to_all x4, starting transfers between devices, exchange(): lax.all_to_all(pieces, ('expert', 'seq'), split_axis=0, concat_axis=0, ti...  23.3 us
    pallas_call x2, Pallas kernels, pack(): pl.pallas_call(functools.partial(pack_body, slot), grid=(groups // pieces...  8.66 us
    pallas_call x2, Pallas kernels, unpack(): pl.pallas_call(body, grid=(heads // pieces,), out_shape=(whole, whole, wh...  7.35 us
    ppermute x3, starting transfers between devices, sum_over_replicas(): lax.ppermute(values, 'rep', [(at, (at + shift) % replicas) for at in rang...  5.3 us
  transfers between devices with their start and end apart: 8, of which 7 were waited for; matrix products, arithmetic and copies ran while one was open for 1% of the time, Pallas kernels for 39%

profile of v5, /device:TPU:0, one launch (start us, length us, event | category | flops | bytes accessed | tf_op | source)
XLA Modules:
  0.0 225.9 jit_solution(16051278082360219569)
XLA Ops:
  0.6 4.3 %shard_map.139 = (bf16[32,512,128]{2,1,0:T(8,128)(2,1)}, f32[8,128]{1,0:T(8,128)}) custom-call(s32[2,2]{1,0:T(2,128)} %steps_ref.7, bf16[1,2,128,4096]{3,2,1,0:T(8,128)(2,1)} %query_ref.3, bf16[1,2,128,4096]{3,2,1,0:T(8,128)(2,1)} %key_ref.3, bf16[1,2,128,4096]{3,2,1,0:T(8,128)(2,1)} %value_ref.3, bf16[1,2,128,4096]{3,2,1,0:T(8,128)(2,1)} %noise_ref.3, ...), custom_call_target="tpu_custom_call" | custom-call | flops 3145728 | bytes 9437184 | tf_op jit(solution)/shard_map/pallas_call | solution.py:65
  5.0 8.5 %all-to-all-start.2 = ((bf16[32,512,128]{2,1,0:T(8,128)(2,1)}), bf16[32,512,128]{2,1,0:T(8,128)(2,1)}, u32[]{:S(2)}, u32[]{:S(2)}) async-start(bf16[32,512,128]{2,1,0:T(8,128)(2,1)} %get-tuple-element.20), calls=%async_computation.2 | async-start | bytes 8388608 | tf_op jit(solution)/shard_map/all_to_all | solution.py:334
  13.5 0.0 copy-done
  13.5 1.8 collective-permute-start.3
  15.3 4.3 %shard_map.137 = (bf16[32,512,128]{2,1,0:T(8,128)(2,1)}, f32[8,128]{1,0:T(8,128)}) custom-call(s32[2,2]{1,0:T(2,128)} %steps_ref.7, bf16[1,2,128,4096]{3,2,1,0:T(8,128)(2,1)} %query_ref.3, bf16[1,2,128,4096]{3,2,1,0:T(8,128)(2,1)} %key_ref.3, bf16[1,2,128,4096]{3,2,1,0:T(8,128)(2,1)} %value_ref.3, bf16[1,2,128,4096]{3,2,1,0:T(8,128)(2,1)} %noise_ref.3, ...), custom_call_target="tpu_custom_call" | custom-call | flops 3145728 | bytes 9437184 | tf_op jit(solution)/shard_map/pallas_call | solution.py:65
  19.6 39.5 %collective-permute-done.3 = bf16[2,4096]{1,0:T(2,128)(2,1)S(1)} collective-permute-done((bf16[2,4096]{1,0:T(2,128)(2,1)S(1)}, bf16[2,4096]{1,0:T(2,128)(2,1)S(1)}, u32[]{:S(2)}, u32[]{:S(2)}) %collective-permute-start.3) | collective-permute-done | bytes 16416 | tf_op jit(solution)/shard_map/ppermute | solution.py:396
  59.1 8.0 %all-to-all-done.2 = bf16[32,512,128]{2,1,0:T(8,128)(2,1)} async-done(((bf16[32,512,128]{2,1,0:T(8,128)(2,1)}), bf16[32,512,128]{2,1,0:T(8,128)(2,1)}, u32[]{:S(2)}, u32[]{:S(2)}) %all-to-all-start.2) | async-done | bytes 4194336 | tf_op jit(solution)/shard_map/all_to_all | solution.py:334
  67.1 4.9 %all-to-all-start = ((bf16[32,512,128]{2,1,0:T(8,128)(2,1)}), bf16[32,512,128]{2,1,0:T(8,128)(2,1)}, u32[]{:S(2)}, u32[]{:S(2)}) async-start(bf16[32,512,128]{2,1,0:T(8,128)(2,1)} %get-tuple-element.17), calls=%async_computation | async-start | bytes 8388608 | tf_op jit(solution)/shard_map/all_to_all | solution.py:334
  71.9 0.6 broadcast_select_fusion.gate_ref
  72.5 40.4 %shard_map.140 = bf16[2,16,400,128]{3,2,1,0:T(8,128)(2,1)} custom-call(s32[2,2]{1,0:T(2,128)} %steps_ref.7, bf16[2,16,512,128]{3,2,1,0:T(8,128)(2,1)} %bitcast.12.query_ref.key_ref.value_ref.field_ref, bf16[2,16,512,128]{3,2,1,0:T(8,128)(2,1)} %bitcast.12.query_ref.key_ref.value_ref.field_ref, ...), custom_call_target="tpu_custom_call" | custom-call | flops 25769803776 | bytes 7340032 | tf_op jit(solution)/shard_map/pallas_call | solution.py:217
  112.9 12.7 %all-to-all-done = bf16[32,512,128]{2,1,0:T(8,128)(2,1)} async-done(((bf16[32,512,128]{2,1,0:T(8,128)(2,1)}), bf16[32,512,128]{2,1,0:T(8,128)(2,1)}, u32[]{:S(2)}, u32[]{:S(2)}) %all-to-all-start) | async-done | bytes 4194336 | tf_op jit(solution)/shard_map/all_to_all | solution.py:334
  125.6 5.0 %all-to-all-start.3 = ((bf16[32,400,128]{2,1,0:T(8,128)(2,1)}), bf16[32,400,128]{2,1,0:T(8,128)(2,1)}, u32[]{:S(2)}, u32[]{:S(2)}) async-start(bf16[32,400,128]{2,1,0:T(8,128)(2,1)} %bitcast.24), calls=%async_computation.3 | async-start | bytes 6553600 | tf_op jit(solution)/shard_map/all_to_all | solution.py:334
  130.6 40.5 %shard_map.138 = bf16[2,16,400,128]{3,2,1,0:T(8,128)(2,1)} custom-call(s32[2,2]{1,0:T(2,128)} %steps_ref.7, bf16[2,16,512,128]{3,2,1,0:T(8,128)(2,1)} %bitcast.9.query_ref.key_ref.value_ref.field_ref, bf16[2,16,512,128]{3,2,1,0:T(8,128)(2,1)} %bitcast.9.query_ref.key_ref.value_ref.field_ref, ...), custom_call_target="tpu_custom_call" | custom-call | flops 25769803776 | bytes 7340032 | tf_op jit(solution)/shard_map/pallas_call | solution.py:217
  171.1 2.7 %all-to-all-done.3.main_ref.side_ref = bf16[32,400,128]{2,1,0:T(8,128)(2,1)} async-done(((bf16[32,400,128]{2,1,0:T(8,128)(2,1)}), bf16[32,400,128]{2,1,0:T(8,128)(2,1)}, u32[]{:S(2)}, u32[]{:S(2)}) %all-to-all-start.3) | async-done | bytes 3276832 | tf_op jit(solution)/shard_map/all_to_all | solution.py:334
  173.8 4.9 %all-to-all-start.1 = ((bf16[32,400,128]{2,1,0:T(8,128)(2,1)}), bf16[32,400,128]{2,1,0:T(8,128)(2,1)}, u32[]{:S(2)}, u32[]{:S(2)}) async-start(bf16[32,400,128]{2,1,0:T(8,128)(2,1)} %bitcast.23), calls=%async_computation.1 | async-start | bytes 6553600 | tf_op jit(solution)/shard_map/all_to_all | solution.py:334
  178.7 0.0 copy-done.1
  178.7 0.0 copy-done.3
  178.7 0.1 fusion.5
  178.8 0.0 copy-done.2
  178.8 0.1 select_reduce_fusion
  178.9 3.3 %collective-permute-start.1 = (f32[3,4]{1,0:T(4,128)S(1)}, f32[3,4]{1,0:T(4,128)S(1)}, u32[]{:S(2)}, u32[]{:S(2)}) collective-permute-start(f32[3,4]{1,0:T(4,128)S(1)} %pad_maximum_fusion), channel_id=1, source_target_pairs={{0,32},{16,48},{32,0},{48,16},{1,33},{17,49},{33,1},{49,17},{2,34}... | collective-permute-start | bytes 152 | tf_op jit(solution)/shard_map/ppermute | solution.py:341
  182.2 1.1 collective-permute-start.2
  183.3 1.0 collective-permute-start
  184.2 0.0 collective-permute-done.1
  184.2 1.6 collective-permute-done.2
  185.8 2.3 %collective-permute-done = f32[3,4]{1,0:T(4,128)S(1)} collective-permute-done((f32[3,4]{1,0:T(4,128)S(1)}, f32[3,4]{1,0:T(4,128)S(1)}, u32[]{:S(2)}, u32[]{:S(2)}) %collective-permute-start) | collective-permute-done | bytes 80 | tf_op jit(solution)/shard_map/ppermute | solution.py:341
  188.1 0.2 select_reduce_fusion.2
  188.2 0.1 fusion.4
  188.3 0.6 fusion.6
  188.9 3.7 %shard_map.141 = (bf16[1,2,128,4096]{3,2,1,0:T(8,128)(2,1)}, bf16[1,2,128,4096]{3,2,1,0:T(8,128)(2,1)}, bf16[1,2,128,4096]{3,2,1,0:T(8,128)(2,1)}, f32[1,4096]{1,0:T(1,128)}, f32[1,128]{1,0:T(1,128)}) custom-call(f32[2]{0:T(128)} %get-tuple-element.34.weight_ref, f32[2]{0:T(128)} %get-tuple-element.35.kept_ref, ...), custom_call_target="tpu_custom_call" | custom-call | flops 1572864 | bytes 6291456 | tf_op jit(solution)/shard_map/pallas_call | solution.py:317
  192.6 29.4 %all-to-all-done.1.main_ref.side_ref = bf16[32,400,128]{2,1,0:T(8,128)(2,1)} async-done(((bf16[32,400,128]{2,1,0:T(8,128)(2,1)}), bf16[32,400,128]{2,1,0:T(8,128)(2,1)}, u32[]{:S(2)}, u32[]{:S(2)}) %all-to-all-start.1) | async-done | bytes 3276832 | tf_op jit(solution)/shard_map/all_to_all | solution.py:334
  222.0 3.7 %shard_map.142 = (bf16[1,2,128,4096]{3,2,1,0:T(8,128)(2,1)}, bf16[1,2,128,4096]{3,2,1,0:T(8,128)(2,1)}, bf16[1,2,128,4096]{3,2,1,0:T(8,128)(2,1)}, bf16[1,2,4096]{2,1,0:T(2,128)(2,1)}, bf16[1,2]{1,0:T(2,128)(2,1)}) custom-call(f32[2]{0:T(128)} %get-tuple-element.34.weight_ref, ...), custom_call_target="tpu_custom_call", output_to_operand_aliasing={{0}: (4, {}), {1}: (5, {}), {2}: (6, {})} | custom-call | flops 1572864 | bytes 6291456 | tf_op jit(solution)/shard_map/pallas_call | solution.py:317
  (8 shorter events, 0.1 us)
Async XLA Ops:
  5.0 8.5 %copy-start = (bf16[1,2,4096]{2,1,0:T(2,128)(2,1)S(1)}, bf16[1,2,4096]{2,1,0:T(2,128)(2,1)}, u32[]{:S(2)}) copy-start(bf16[1,2,4096]{2,1,0:T(2,128)(2,1)} %param.15) | copy-start | bytes 49156
  5.0 62.1 %all-to-all-start.2 = ((bf16[32,512,128]{2,1,0:T(8,128)(2,1)}), bf16[32,512,128]{2,1,0:T(8,128)(2,1)}, u32[]{:S(2)}, u32[]{:S(2)}) async-start(bf16[32,512,128]{2,1,0:T(8,128)(2,1)} %get-tuple-element.20), calls=%async_computation.2 | async-start | bytes 8388608 | tf_op jit(solution)/shard_map/all_to_all | solution.py:334
  13.5 45.6 %collective-permute-start.3 = (bf16[2,4096]{1,0:T(2,128)(2,1)S(1)}, bf16[2,4096]{1,0:T(2,128)(2,1)S(1)}, u32[]{:S(2)}, u32[]{:S(2)}) collective-permute-start(bf16[2,4096]{1,0:T(2,128)(2,1)S(1)} %bitcast.25), channel_id=1, source_target_pairs={{0,64},{64,0},{1,65},{65,1},{2,66},{66,2},{3,67},{67,3},{4,68},{68... | collective-permute-start | bytes 49160 | tf_op jit(solution)/shard_map/ppermute | solution.py:396
  67.1 58.5 %all-to-all-start = ((bf16[32,512,128]{2,1,0:T(8,128)(2,1)}), bf16[32,512,128]{2,1,0:T(8,128)(2,1)}, u32[]{:S(2)}, u32[]{:S(2)}) async-start(bf16[32,512,128]{2,1,0:T(8,128)(2,1)} %get-tuple-element.17), calls=%async_computation | async-start | bytes 8388608 | tf_op jit(solution)/shard_map/all_to_all | solution.py:334
  125.6 48.1 %all-to-all-start.3 = ((bf16[32,400,128]{2,1,0:T(8,128)(2,1)}), bf16[32,400,128]{2,1,0:T(8,128)(2,1)}, u32[]{:S(2)}, u32[]{:S(2)}) async-start(bf16[32,400,128]{2,1,0:T(8,128)(2,1)} %bitcast.24), calls=%async_computation.3 | async-start | bytes 6553600 | tf_op jit(solution)/shard_map/all_to_all | solution.py:334
  173.8 5.0 %copy-start.1 = (f32[2,2]{1,0:T(2,128)S(1)}, f32[2,2]{1,0:T(2,128)}, u32[]{:S(2)}) copy-start(f32[2,2]{1,0:T(2,128)} %param.16) | copy-start | bytes 52
  173.8 5.0 %copy-start.3 = (s32[2,1]{0,1:T(1,128)S(1)}, s32[2,1]{0,1:T(1,128)}, u32[]{:S(2)}) copy-start(s32[2,1]{0,1:T(1,128)} %param.19) | copy-start | bytes 28
  173.8 5.1 %copy-start.2 = (s32[2,2]{1,0:T(2,128)S(1)}, s32[2,2]{1,0:T(2,128)}, u32[]{:S(2)}) copy-start(s32[2,2]{1,0:T(2,128)} %param.17) | copy-start | bytes 52
  173.8 48.3 %all-to-all-start.1 = ((bf16[32,400,128]{2,1,0:T(8,128)(2,1)}), bf16[32,400,128]{2,1,0:T(8,128)(2,1)}, u32[]{:S(2)}, u32[]{:S(2)}) async-start(bf16[32,400,128]{2,1,0:T(8,128)(2,1)} %bitcast.23), calls=%async_computation.1 | async-start | bytes 6553600 | tf_op jit(solution)/shard_map/all_to_all | solution.py:334
  178.9 5.3 %collective-permute-start.1 = (f32[3,4]{1,0:T(4,128)S(1)}, f32[3,4]{1,0:T(4,128)S(1)}, u32[]{:S(2)}, u32[]{:S(2)}) collective-permute-start(f32[3,4]{1,0:T(4,128)S(1)} %pad_maximum_fusion), channel_id=1, source_target_pairs={{0,32},{16,48},{32,0},{48,16},{1,33},{17,49},{33,1},{49,17},{2,34}... | collective-permute-start | bytes 152 | tf_op jit(solution)/shard_map/ppermute | solution.py:341
  182.2 3.6 %collective-permute-start.2 = (f32[3,4]{1,0:T(4,128)S(1)}, f32[3,4]{1,0:T(4,128)S(1)}, u32[]{:S(2)}, u32[]{:S(2)}) collective-permute-start(f32[3,4]{1,0:T(4,128)S(1)} %pad_maximum_fusion), channel_id=1, source_target_pairs={{0,48},{16,0},{32,16},{48,32},{1,49},{17,1},{33,17},{49,33},{2,50}... | collective-permute-start | bytes 152 | tf_op jit(solution)/shard_map/ppermute | solution.py:341
  183.3 4.8 %collective-permute-start = (f32[3,4]{1,0:T(4,128)S(1)}, f32[3,4]{1,0:T(4,128)S(1)}, u32[]{:S(2)}, u32[]{:S(2)}) collective-permute-start(f32[3,4]{1,0:T(4,128)S(1)} %pad_maximum_fusion), channel_id=1, source_target_pairs={{0,16},{16,32},{32,48},{48,0},{1,17},{17,33},{33,49},{49,1},{2,18}... | collective-permute-start | bytes 152 | tf_op jit(solution)/shard_map/ppermute | solution.py:341

commit v6 on v5

--- a/solution.py
+++ b/solution.py
@@ -15,6 +15,7 @@
 NN = (((1,), (0,)), ((), ()))
 NT = (((1,), (1,)), ((), ()))
 VMEM_LIMIT = 63 * 1024 * 1024
+UNPACK_LIMIT = 24 * 1024 * 1024
 
 
 def step_coef(timestep, shape):
@@ -321,7 +322,7 @@
         in_specs=in_specs,
         out_specs=(part, part, part) + small_specs,
         input_output_aliases={4 + at: at for at in range(3)} if previous else {},
-        compiler_params=pltpu.CompilerParams(vmem_limit_bytes=VMEM_LIMIT),
+        compiler_params=pltpu.CompilerParams(vmem_limit_bytes=UNPACK_LIMIT),
         cost_estimate=pl.CostEstimate(
             flops=3 * tokens * full_width,
             bytes_accessed=12 * tokens * full_width,

time: 226 us -> 225 us (level)
  transfers between devices with their start and end apart: 8 -> 8, of which waited for: 7 -> 7; matrix products, arithmetic and copies ran while one was open for 1% -> 0% of each run, Pallas kernels for 39% -> 40%
where the time goes in v6:
time: 225 us
  waiting for transfers between devices  96.7 us (43%)
  Pallas kernels  96.1 us (43%)
  starting transfers between devices  30 us (13%)
    pallas_call x2, Pallas kernels, attention(): pl.pallas_call(functools.partial(attention_body, slot, block_rows, chunk)...  80.9 us
    all_to_all x4, waiting for transfers between devices, exchange(): lax.all_to_all(pieces, ('expert', 'seq'), split_axis=0, concat_axis=0, ti...  53.4 us
    ppermute x1, waiting for transfers between devices, local(): gate_other = lax.ppermute(gate_own, 'expert', [(0, 1), (1, 0)])  39.5 us
    all_to_all x4, starting transfers between devices, exchange(): lax.all_to_all(pieces, ('expert', 'seq'), split_axis=0, concat_axis=0, ti...  22.9 us
    pallas_call x2, Pallas kernels, pack(): pl.pallas_call(functools.partial(pack_body, slot), grid=(groups // pieces...  8.66 us
    pallas_call x2, Pallas kernels, unpack(): pl.pallas_call(body, grid=(heads // pieces,), out_shape=(whole, whole, wh...  6.58 us
    ppermute x3, starting transfers between devices, sum_over_replicas(): lax.ppermute(values, 'rep', [(at, (at + shift) % replicas) for at in rang...  5.3 us
  transfers between devices with their start and end apart: 8, of which 7 were waited for; matrix products, arithmetic and copies ran while one was open for 0% of the time, Pallas kernels for 40%

profile of v6, /device:TPU:0, one launch (start us, length us, event | category | flops | bytes accessed | tf_op | source)
XLA Modules:
  0.0 224.6 jit_solution(1880455397822683661)
XLA Ops:
  0.6 4.3 %shard_map.139 = (bf16[32,512,128]{2,1,0:T(8,128)(2,1)}, f32[8,128]{1,0:T(8,128)}) custom-call(s32[2,2]{1,0:T(2,128)} %steps_ref.7, bf16[1,2,128,4096]{3,2,1,0:T(8,128)(2,1)} %query_ref.3, bf16[1,2,128,4096]{3,2,1,0:T(8,128)(2,1)} %key_ref.3, bf16[1,2,128,4096]{3,2,1,0:T(8,128)(2,1)} %value_ref.3, bf16[1,2,128,4096]{3,2,1,0:T(8,128)(2,1)} %noise_ref.3, ...), custom_call_target="tpu_custom_call" | custom-call | flops 3145728 | bytes 9437184 | tf_op jit(solution)/shard_map/pallas_call | solution.py:66
  5.0 0.0 copy-start
  5.0 8.5 %all-to-all-start.2 = ((bf16[32,512,128]{2,1,0:T(8,128)(2,1)}), bf16[32,512,128]{2,1,0:T(8,128)(2,1)}, u32[]{:S(2)}, u32[]{:S(2)}) async-start(bf16[32,512,128]{2,1,0:T(8,128)(2,1)} %get-tuple-element.20), calls=%async_computation.2 | async-start | bytes 8388608 | tf_op jit(solution)/shard_map/all_to_all | solution.py:335
  13.5 0.0 copy-done
  13.5 1.8 collective-permute-start.3
  15.3 4.3 %shard_map.137 = (bf16[32,512,128]{2,1,0:T(8,128)(2,1)}, f32[8,128]{1,0:T(8,128)}) custom-call(s32[2,2]{1,0:T(2,128)} %steps_ref.7, bf16[1,2,128,4096]{3,2,1,0:T(8,128)(2,1)} %query_ref.3, bf16[1,2,128,4096]{3,2,1,0:T(8,128)(2,1)} %key_ref.3, bf16[1,2,128,4096]{3,2,1,0:T(8,128)(2,1)} %value_ref.3, bf16[1,2,128,4096]{3,2,1,0:T(8,128)(2,1)} %noise_ref.3, ...), custom_call_target="tpu_custom_call" | custom-call | flops 3145728 | bytes 9437184 | tf_op jit(solution)/shard_map/pallas_call | solution.py:66
  19.6 39.5 %collective-permute-done.3 = bf16[2,4096]{1,0:T(2,128)(2,1)S(1)} collective-permute-done((bf16[2,4096]{1,0:T(2,128)(2,1)S(1)}, bf16[2,4096]{1,0:T(2,128)(2,1)S(1)}, u32[]{:S(2)}, u32[]{:S(2)}) %collective-permute-start.3) | collective-permute-done | bytes 16416 | tf_op jit(solution)/shard_map/ppermute | solution.py:397
  59.1 8.0 %all-to-all-done.2 = bf16[32,512,128]{2,1,0:T(8,128)(2,1)} async-done(((bf16[32,512,128]{2,1,0:T(8,128)(2,1)}), bf16[32,512,128]{2,1,0:T(8,128)(2,1)}, u32[]{:S(2)}, u32[]{:S(2)}) %all-to-all-start.2) | async-done | bytes 4194336 | tf_op jit(solution)/shard_map/all_to_all | solution.py:335
  67.1 4.9 %all-to-all-start = ((bf16[32,512,128]{2,1,0:T(8,128)(2,1)}), bf16[32,512,128]{2,1,0:T(8,128)(2,1)}, u32[]{:S(2)}, u32[]{:S(2)}) async-start(bf16[32,512,128]{2,1,0:T(8,128)(2,1)} %get-tuple-element.17), calls=%async_computation | async-start | bytes 8388608 | tf_op jit(solution)/shard_map/all_to_all | solution.py:335
  71.9 0.6 broadcast_select_fusion.gate_ref
  72.5 40.4 %shard_map.140 = bf16[2,16,400,128]{3,2,1,0:T(8,128)(2,1)} custom-call(s32[2,2]{1,0:T(2,128)} %steps_ref.7, bf16[2,16,512,128]{3,2,1,0:T(8,128)(2,1)} %bitcast.12.query_ref.key_ref.value_ref.field_ref, bf16[2,16,512,128]{3,2,1,0:T(8,128)(2,1)} %bitcast.12.query_ref.key_ref.value_ref.field_ref, ...), custom_call_target="tpu_custom_call" | custom-call | flops 25769803776 | bytes 7340032 | tf_op jit(solution)/shard_map/pallas_call | solution.py:218
  112.9 12.7 %all-to-all-done = bf16[32,512,128]{2,1,0:T(8,128)(2,1)} async-done(((bf16[32,512,128]{2,1,0:T(8,128)(2,1)}), bf16[32,512,128]{2,1,0:T(8,128)(2,1)}, u32[]{:S(2)}, u32[]{:S(2)}) %all-to-all-start) | async-done | bytes 4194336 | tf_op jit(solution)/shard_map/all_to_all | solution.py:335
  125.6 5.0 %all-to-all-start.3 = ((bf16[32,400,128]{2,1,0:T(8,128)(2,1)}), bf16[32,400,128]{2,1,0:T(8,128)(2,1)}, u32[]{:S(2)}, u32[]{:S(2)}) async-start(bf16[32,400,128]{2,1,0:T(8,128)(2,1)} %bitcast.24), calls=%async_computation.3 | async-start | bytes 6553600 | tf_op jit(solution)/shard_map/all_to_all | solution.py:335
  130.6 40.5 %shard_map.138 = bf16[2,16,400,128]{3,2,1,0:T(8,128)(2,1)} custom-call(s32[2,2]{1,0:T(2,128)} %steps_ref.7, bf16[2,16,512,128]{3,2,1,0:T(8,128)(2,1)} %bitcast.9.query_ref.key_ref.value_ref.field_ref, bf16[2,16,512,128]{3,2,1,0:T(8,128)(2,1)} %bitcast.9.query_ref.key_ref.value_ref.field_ref, ...), custom_call_target="tpu_custom_call" | custom-call | flops 25769803776 | bytes 7340032 | tf_op jit(solution)/shard_map/pallas_call | solution.py:218
  171.1 2.7 %all-to-all-done.3.main_ref.side_ref = bf16[32,400,128]{2,1,0:T(8,128)(2,1)} async-done(((bf16[32,400,128]{2,1,0:T(8,128)(2,1)}), bf16[32,400,128]{2,1,0:T(8,128)(2,1)}, u32[]{:S(2)}, u32[]{:S(2)}) %all-to-all-start.3) | async-done | bytes 3276832 | tf_op jit(solution)/shard_map/all_to_all | solution.py:335
  173.8 4.6 %all-to-all-start.1 = ((bf16[32,400,128]{2,1,0:T(8,128)(2,1)}), bf16[32,400,128]{2,1,0:T(8,128)(2,1)S(1)}, u32[]{:S(2)}, u32[]{:S(2)}) async-start(bf16[32,400,128]{2,1,0:T(8,128)(2,1)} %bitcast.23), calls=%async_computation.1 | async-start | bytes 6553600 | tf_op jit(solution)/shard_map/all_to_all | solution.py:335
  178.3 0.0 copy-done.1
  178.4 0.0 copy-done.3
  178.4 0.1 fusion.5
  178.4 0.0 copy-done.2
  178.4 0.1 select_reduce_fusion
  178.6 3.3 %collective-permute-start.1 = (f32[3,4]{1,0:T(4,128)S(1)}, f32[3,4]{1,0:T(4,128)S(1)}, u32[]{:S(2)}, u32[]{:S(2)}) collective-permute-start(f32[3,4]{1,0:T(4,128)S(1)} %pad_maximum_fusion), channel_id=1, source_target_pairs={{0,32},{16,48},{32,0},{48,16},{1,33},{17,49},{33,1},{49,17},{2,34}... | collective-permute-start | bytes 152 | tf_op jit(solution)/shard_map/ppermute | solution.py:342
  181.8 1.1 collective-permute-start.2
  182.9 1.0 collective-permute-start
  183.9 0.0 collective-permute-done.1
  183.9 1.6 collective-permute-done.2
  185.4 2.3 %collective-permute-done = f32[3,4]{1,0:T(4,128)S(1)} collective-permute-done((f32[3,4]{1,0:T(4,128)S(1)}, f32[3,4]{1,0:T(4,128)S(1)}, u32[]{:S(2)}, u32[]{:S(2)}) %collective-permute-start) | collective-permute-done | bytes 80 | tf_op jit(solution)/shard_map/ppermute | solution.py:342
  187.7 0.2 select_reduce_fusion.2
  187.9 0.1 fusion.4
  187.9 3.7 %shard_map.141 = (bf16[1,2,128,4096]{3,2,1,0:T(8,128)(2,1)}, bf16[1,2,128,4096]{3,2,1,0:T(8,128)(2,1)}, bf16[1,2,128,4096]{3,2,1,0:T(8,128)(2,1)}, f32[1,4096]{1,0:T(1,128)S(1)}, f32[1,128]{1,0:T(1,128)S(1)}) custom-call(f32[2]{0:T(128)S(1)} %get-tuple-element.34.weight_ref, f32[2]{0:T(128)S(1)} %get-tuple-element.35.kept_ref, ...), custom_call_target="tpu_custom_call" | custom-call | flops 1572864 | bytes 6291456 | tf_op jit(solution)/shard_map/pallas_call | solution.py:318
  191.6 30.1 %all-to-all-done.1.main_ref.side_ref = bf16[32,400,128]{2,1,0:T(8,128)(2,1)S(1)} async-done(((bf16[32,400,128]{2,1,0:T(8,128)(2,1)}), bf16[32,400,128]{2,1,0:T(8,128)(2,1)S(1)}, u32[]{:S(2)}, u32[]{:S(2)}) %all-to-all-start.1) | async-done | bytes 3276832 | tf_op jit(solution)/shard_map/all_to_all | solution.py:335
  221.7 2.9 %shard_map.142 = (bf16[1,2,128,4096]{3,2,1,0:T(8,128)(2,1)}, bf16[1,2,128,4096]{3,2,1,0:T(8,128)(2,1)}, bf16[1,2,128,4096]{3,2,1,0:T(8,128)(2,1)}, bf16[1,2,4096]{2,1,0:T(2,128)(2,1)}, bf16[1,2]{1,0:T(2,128)(2,1)}) custom-call(f32[2]{0:T(128)S(1)} %get-tuple-element.34.weight_ref, ...), custom_call_target="tpu_custom_call", output_to_operand_aliasing={{0}: (4, {}), {1}: (5, {}), {2}: (6, {})} | custom-call | flops 1572864 | bytes 6291456 | tf_op jit(solution)/shard_map/pallas_call | solution.py:318
  (8 shorter events, 0.1 us)
Async XLA Ops:
  5.0 8.5 %copy-start = (bf16[1,2,4096]{2,1,0:T(2,128)(2,1)S(1)}, bf16[1,2,4096]{2,1,0:T(2,128)(2,1)}, u32[]{:S(2)}) copy-start(bf16[1,2,4096]{2,1,0:T(2,128)(2,1)} %param.15) | copy-start | bytes 49156
  5.0 62.1 %all-to-all-start.2 = ((bf16[32,512,128]{2,1,0:T(8,128)(2,1)}), bf16[32,512,128]{2,1,0:T(8,128)(2,1)}, u32[]{:S(2)}, u32[]{:S(2)}) async-start(bf16[32,512,128]{2,1,0:T(8,128)(2,1)} %get-tuple-element.20), calls=%async_computation.2 | async-start | bytes 8388608 | tf_op jit(solution)/shard_map/all_to_all | solution.py:335
  13.5 45.6 %collective-permute-start.3 = (bf16[2,4096]{1,0:T(2,128)(2,1)S(1)}, bf16[2,4096]{1,0:T(2,128)(2,1)S(1)}, u32[]{:S(2)}, u32[]{:S(2)}) collective-permute-start(bf16[2,4096]{1,0:T(2,128)(2,1)S(1)} %bitcast.25), channel_id=1, source_target_pairs={{0,64},{64,0},{1,65},{65,1},{2,66},{66,2},{3,67},{67,3},{4,68},{68... | collective-permute-start | bytes 49160 | tf_op jit(solution)/shard_map/ppermute | solution.py:397
  67.1 58.5 %all-to-all-start = ((bf16[32,512,128]{2,1,0:T(8,128)(2,1)}), bf16[32,512,128]{2,1,0:T(8,128)(2,1)}, u32[]{:S(2)}, u32[]{:S(2)}) async-start(bf16[32,512,128]{2,1,0:T(8,128)(2,1)} %get-tuple-element.17), calls=%async_computation | async-start | bytes 8388608 | tf_op jit(solution)/shard_map/all_to_all | solution.py:335
  125.6 48.1 %all-to-all-start.3 = ((bf16[32,400,128]{2,1,0:T(8,128)(2,1)}), bf16[32,400,128]{2,1,0:T(8,128)(2,1)}, u32[]{:S(2)}, u32[]{:S(2)}) async-start(bf16[32,400,128]{2,1,0:T(8,128)(2,1)} %bitcast.24), calls=%async_computation.3 | async-start | bytes 6553600 | tf_op jit(solution)/shard_map/all_to_all | solution.py:335
  173.8 4.6 %copy-start.1 = (f32[2,2]{1,0:T(2,128)S(1)}, f32[2,2]{1,0:T(2,128)}, u32[]{:S(2)}) copy-start(f32[2,2]{1,0:T(2,128)} %param.16) | copy-start | bytes 52
  173.8 4.6 %copy-start.3 = (s32[2,1]{0,1:T(1,128)S(1)}, s32[2,1]{0,1:T(1,128)}, u32[]{:S(2)}) copy-start(s32[2,1]{0,1:T(1,128)} %param.19) | copy-start | bytes 28
  173.8 4.7 %copy-start.2 = (s32[2,2]{1,0:T(2,128)S(1)}, s32[2,2]{1,0:T(2,128)}, u32[]{:S(2)}) copy-start(s32[2,2]{1,0:T(2,128)} %param.17) | copy-start | bytes 52
  173.8 47.9 %all-to-all-start.1 = ((bf16[32,400,128]{2,1,0:T(8,128)(2,1)}), bf16[32,400,128]{2,1,0:T(8,128)(2,1)S(1)}, u32[]{:S(2)}, u32[]{:S(2)}) async-start(bf16[32,400,128]{2,1,0:T(8,128)(2,1)} %bitcast.23), calls=%async_computation.1 | async-start | bytes 6553600 | tf_op jit(solution)/shard_map/all_to_all | solution.py:335
  178.6 5.3 %collective-permute-start.1 = (f32[3,4]{1,0:T(4,128)S(1)}, f32[3,4]{1,0:T(4,128)S(1)}, u32[]{:S(2)}, u32[]{:S(2)}) collective-permute-start(f32[3,4]{1,0:T(4,128)S(1)} %pad_maximum_fusion), channel_id=1, source_target_pairs={{0,32},{16,48},{32,0},{48,16},{1,33},{17,49},{33,1},{49,17},{2,34}... | collective-permute-start | bytes 152 | tf_op jit(solution)/shard_map/ppermute | solution.py:342
  181.8 3.6 %collective-permute-start.2 = (f32[3,4]{1,0:T(4,128)S(1)}, f32[3,4]{1,0:T(4,128)S(1)}, u32[]{:S(2)}, u32[]{:S(2)}) collective-permute-start(f32[3,4]{1,0:T(4,128)S(1)} %pad_maximum_fusion), channel_id=1, source_target_pairs={{0,48},{16,0},{32,16},{48,32},{1,49},{17,1},{33,17},{49,33},{2,50}... | collective-permute-start | bytes 152 | tf_op jit(solution)/shard_map/ppermute | solution.py:342
  182.9 4.8 %collective-permute-start = (f32[3,4]{1,0:T(4,128)S(1)}, f32[3,4]{1,0:T(4,128)S(1)}, u32[]{:S(2)}, u32[]{:S(2)}) collective-permute-start(f32[3,4]{1,0:T(4,128)S(1)} %pad_maximum_fusion), channel_id=1, source_target_pairs={{0,16},{16,32},{32,48},{48,0},{1,17},{17,33},{33,49},{49,1},{2,18}... | collective-permute-start | bytes 152 | tf_op jit(solution)/shard_map/ppermute | solution.py:342

commit v7 on v6

--- a/solution.py
+++ b/solution.py
@@ -15,6 +15,7 @@
 NN = (((1,), (0,)), ((), ()))
 NT = (((1,), (1,)), ((), ()))
 VMEM_LIMIT = 63 * 1024 * 1024
+ATTENTION_LIMIT = 56 * 1024 * 1024
 UNPACK_LIMIT = 24 * 1024 * 1024
 
 
@@ -236,7 +237,7 @@
             pltpu.VMEM((HD, block_rows), F32),
             pltpu.VMEM((HD, block_rows), F32),
         ],
-        compiler_params=pltpu.CompilerParams(vmem_limit_bytes=VMEM_LIMIT),
+        compiler_params=pltpu.CompilerParams(vmem_limit_bytes=ATTENTION_LIMIT),
         cost_estimate=pl.CostEstimate(
             flops=sets * 24 * length * length * HD,
             bytes_accessed=sets * 14 * length * width,

time: 225 us -> 225 us (level)
  transfers between devices with their start and end apart: 8 -> 8, of which waited for: 7 -> 7; matrix products, arithmetic and copies ran while one was open for 0% -> 0% of each run, Pallas kernels for 40% -> 39%
where the time goes in v7:
time: 225 us
  waiting for transfers between devices  97.4 us (43%)
  Pallas kernels  96.1 us (43%)
  starting transfers between devices  29.7 us (13%)
    pallas_call x2, Pallas kernels, attention(): pl.pallas_call(functools.partial(attention_body, slot, block_rows, chunk)...  80.9 us
    all_to_all x4, waiting for transfers between devices, exchange(): lax.all_to_all(pieces, ('expert', 'seq'), split_axis=0, concat_axis=0, ti...  54.2 us
    ppermute x1, waiting for transfers between devices, local(): gate_other = lax.ppermute(gate_own, 'expert', [(0, 1), (1, 0)])  39.5 us
    all_to_all x4, starting transfers between devices, exchange(): lax.all_to_all(pieces, ('expert', 'seq'), split_axis=0, concat_axis=0, ti...  22.6 us
    pallas_call x2, Pallas kernels, pack(): pl.pallas_call(functools.partial(pack_body, slot), grid=(groups // pieces...  8.66 us
    pallas_call x2, Pallas kernels, unpack(): pl.pallas_call(body, grid=(heads // pieces,), out_shape=(whole, whole, wh...  6.57 us
    ppermute x3, starting transfers between devices, sum_over_replicas(): lax.ppermute(values, 'rep', [(at, (at + shift) % replicas) for at in rang...  5.3 us
  transfers between devices with their start and end apart: 8, of which 7 were waited for; matrix products, arithmetic and copies ran while one was open for 0% of the time, Pallas kernels for 39%

profile of v7, /device:TPU:0, one launch (start us, length us, event | category | flops | bytes accessed | tf_op | source)
XLA Modules:
  0.0 225.0 jit_solution(17272732512877384270)
XLA Ops:
  0.6 4.3 %shard_map.139 = (bf16[32,512,128]{2,1,0:T(8,128)(2,1)}, f32[8,128]{1,0:T(8,128)}) custom-call(s32[2,2]{1,0:T(2,128)} %steps_ref.7, bf16[1,2,128,4096]{3,2,1,0:T(8,128)(2,1)} %query_ref.3, bf16[1,2,128,4096]{3,2,1,0:T(8,128)(2,1)} %key_ref.3, bf16[1,2,128,4096]{3,2,1,0:T(8,128)(2,1)} %value_ref.3, bf16[1,2,128,4096]{3,2,1,0:T(8,128)(2,1)} %noise_ref.3, ...), custom_call_target="tpu_custom_call" | custom-call | flops 3145728 | bytes 9437184 | tf_op jit(solution)/shard_map/pallas_call | solution.py:67
  5.0 0.0 copy-start
  5.0 8.5 %all-to-all-start.2 = ((bf16[32,512,128]{2,1,0:T(8,128)(2,1)}), bf16[32,512,128]{2,1,0:T(8,128)(2,1)}, u32[]{:S(2)}, u32[]{:S(2)}) async-start(bf16[32,512,128]{2,1,0:T(8,128)(2,1)} %get-tuple-element.20), calls=%async_computation.2 | async-start | bytes 8388608 | tf_op jit(solution)/shard_map/all_to_all | solution.py:336
  13.5 0.0 copy-done
  13.5 1.8 collective-permute-start.3
  15.3 4.3 %shard_map.137 = (bf16[32,512,128]{2,1,0:T(8,128)(2,1)}, f32[8,128]{1,0:T(8,128)}) custom-call(s32[2,2]{1,0:T(2,128)} %steps_ref.7, bf16[1,2,128,4096]{3,2,1,0:T(8,128)(2,1)} %query_ref.3, bf16[1,2,128,4096]{3,2,1,0:T(8,128)(2,1)} %key_ref.3, bf16[1,2,128,4096]{3,2,1,0:T(8,128)(2,1)} %value_ref.3, bf16[1,2,128,4096]{3,2,1,0:T(8,128)(2,1)} %noise_ref.3, ...), custom_call_target="tpu_custom_call" | custom-call | flops 3145728 | bytes 9437184 | tf_op jit(solution)/shard_map/pallas_call | solution.py:67
  19.6 39.5 %collective-permute-done.3 = bf16[2,4096]{1,0:T(2,128)(2,1)S(1)} collective-permute-done((bf16[2,4096]{1,0:T(2,128)(2,1)S(1)}, bf16[2,4096]{1,0:T(2,128)(2,1)S(1)}, u32[]{:S(2)}, u32[]{:S(2)}) %collective-permute-start.3) | collective-permute-done | bytes 16416 | tf_op jit(solution)/shard_map/ppermute | solution.py:398
  59.1 8.0 %all-to-all-done.2 = bf16[32,512,128]{2,1,0:T(8,128)(2,1)} async-done(((bf16[32,512,128]{2,1,0:T(8,128)(2,1)}), bf16[32,512,128]{2,1,0:T(8,128)(2,1)}, u32[]{:S(2)}, u32[]{:S(2)}) %all-to-all-start.2) | async-done | bytes 4194336 | tf_op jit(solution)/shard_map/all_to_all | solution.py:336
  67.1 4.9 %all-to-all-start = ((bf16[32,512,128]{2,1,0:T(8,128)(2,1)}), bf16[32,512,128]{2,1,0:T(8,128)(2,1)}, u32[]{:S(2)}, u32[]{:S(2)}) async-start(bf16[32,512,128]{2,1,0:T(8,128)(2,1)} %get-tuple-element.17), calls=%async_computation | async-start | bytes 8388608 | tf_op jit(solution)/shard_map/all_to_all | solution.py:336
  71.9 0.6 broadcast_select_fusion.gate_ref
  72.5 40.4 %shard_map.140 = bf16[2,16,400,128]{3,2,1,0:T(8,128)(2,1)} custom-call(s32[2,2]{1,0:T(2,128)} %steps_ref.7, bf16[2,16,512,128]{3,2,1,0:T(8,128)(2,1)} %bitcast.12.query_ref.key_ref.value_ref.field_ref, bf16[2,16,512,128]{3,2,1,0:T(8,128)(2,1)} %bitcast.12.query_ref.key_ref.value_ref.field_ref, ...), custom_call_target="tpu_custom_call" | custom-call | flops 25769803776 | bytes 7340032 | tf_op jit(solution)/shard_map/pallas_call | solution.py:219
  112.9 12.7 %all-to-all-done = bf16[32,512,128]{2,1,0:T(8,128)(2,1)} async-done(((bf16[32,512,128]{2,1,0:T(8,128)(2,1)}), bf16[32,512,128]{2,1,0:T(8,128)(2,1)}, u32[]{:S(2)}, u32[]{:S(2)}) %all-to-all-start) | async-done | bytes 4194336 | tf_op jit(solution)/shard_map/all_to_all | solution.py:336
  125.6 4.2 %all-to-all-start.3 = ((bf16[32,400,128]{2,1,0:T(8,128)(2,1)}), bf16[32,400,128]{2,1,0:T(8,128)(2,1)S(1)}, u32[]{:S(2)}, u32[]{:S(2)}) async-start(bf16[32,400,128]{2,1,0:T(8,128)(2,1)} %bitcast.24), calls=%async_computation.3 | async-start | bytes 6553600 | tf_op jit(solution)/shard_map/all_to_all | solution.py:336
  129.9 40.5 %shard_map.138 = bf16[2,16,400,128]{3,2,1,0:T(8,128)(2,1)} custom-call(s32[2,2]{1,0:T(2,128)} %steps_ref.7, bf16[2,16,512,128]{3,2,1,0:T(8,128)(2,1)} %bitcast.9.query_ref.key_ref.value_ref.field_ref, bf16[2,16,512,128]{3,2,1,0:T(8,128)(2,1)} %bitcast.9.query_ref.key_ref.value_ref.field_ref, ...), custom_call_target="tpu_custom_call" | custom-call | flops 25769803776 | bytes 7340032 | tf_op jit(solution)/shard_map/pallas_call | solution.py:219
  170.3 2.7 %all-to-all-done.3.main_ref.side_ref = bf16[32,400,128]{2,1,0:T(8,128)(2,1)S(1)} async-done(((bf16[32,400,128]{2,1,0:T(8,128)(2,1)}), bf16[32,400,128]{2,1,0:T(8,128)(2,1)S(1)}, u32[]{:S(2)}, u32[]{:S(2)}) %all-to-all-start.3) | async-done | bytes 3276832 | tf_op jit(solution)/shard_map/all_to_all | solution.py:336
  173.0 4.9 %all-to-all-start.1 = ((bf16[32,400,128]{2,1,0:T(8,128)(2,1)}), bf16[32,400,128]{2,1,0:T(8,128)(2,1)}, u32[]{:S(2)}, u32[]{:S(2)}) async-start(bf16[32,400,128]{2,1,0:T(8,128)(2,1)} %bitcast.23), calls=%async_computation.1 | async-start | bytes 6553600 | tf_op jit(solution)/shard_map/all_to_all | solution.py:336
  178.0 0.0 copy-done.1
  178.0 0.0 copy-done.3
  178.0 0.1 fusion.5
  178.1 0.0 copy-done.2
  178.1 0.1 select_reduce_fusion
  178.2 3.3 %collective-permute-start.1 = (f32[3,4]{1,0:T(4,128)S(1)}, f32[3,4]{1,0:T(4,128)S(1)}, u32[]{:S(2)}, u32[]{:S(2)}) collective-permute-start(f32[3,4]{1,0:T(4,128)S(1)} %pad_maximum_fusion), channel_id=1, source_target_pairs={{0,32},{16,48},{32,0},{48,16},{1,33},{17,49},{33,1},{49,17},{2,34}... | collective-permute-start | bytes 152 | tf_op jit(solution)/shard_map/ppermute | solution.py:343
  181.5 1.1 collective-permute-start.2
  182.5 1.0 collective-permute-start
  183.5 0.0 collective-permute-done.1
  183.5 1.6 collective-permute-done.2
  185.1 2.3 %collective-permute-done = f32[3,4]{1,0:T(4,128)S(1)} collective-permute-done((f32[3,4]{1,0:T(4,128)S(1)}, f32[3,4]{1,0:T(4,128)S(1)}, u32[]{:S(2)}, u32[]{:S(2)}) %collective-permute-start) | collective-permute-done | bytes 80 | tf_op jit(solution)/shard_map/ppermute | solution.py:343
  187.3 0.2 select_reduce_fusion.2
  187.5 0.1 fusion.4
  187.6 2.9 %shard_map.141 = (bf16[1,2,128,4096]{3,2,1,0:T(8,128)(2,1)}, bf16[1,2,128,4096]{3,2,1,0:T(8,128)(2,1)}, bf16[1,2,128,4096]{3,2,1,0:T(8,128)(2,1)}, f32[1,4096]{1,0:T(1,128)S(1)}, f32[1,128]{1,0:T(1,128)S(1)}) custom-call(f32[2]{0:T(128)S(1)} %get-tuple-element.34.weight_ref, f32[2]{0:T(128)S(1)} %get-tuple-element.35.kept_ref, ...), custom_call_target="tpu_custom_call" | custom-call | flops 1572864 | bytes 6291456 | tf_op jit(solution)/shard_map/pallas_call | solution.py:319
  190.5 30.8 %all-to-all-done.1.main_ref.side_ref = bf16[32,400,128]{2,1,0:T(8,128)(2,1)} async-done(((bf16[32,400,128]{2,1,0:T(8,128)(2,1)}), bf16[32,400,128]{2,1,0:T(8,128)(2,1)}, u32[]{:S(2)}, u32[]{:S(2)}) %all-to-all-start.1) | async-done | bytes 3276832 | tf_op jit(solution)/shard_map/all_to_all | solution.py:336
  221.3 3.7 %shard_map.142 = (bf16[1,2,128,4096]{3,2,1,0:T(8,128)(2,1)}, bf16[1,2,128,4096]{3,2,1,0:T(8,128)(2,1)}, bf16[1,2,128,4096]{3,2,1,0:T(8,128)(2,1)}, bf16[1,2,4096]{2,1,0:T(2,128)(2,1)}, bf16[1,2]{1,0:T(2,128)(2,1)}) custom-call(f32[2]{0:T(128)S(1)} %get-tuple-element.34.weight_ref, ...), custom_call_target="tpu_custom_call", output_to_operand_aliasing={{0}: (4, {}), {1}: (5, {}), {2}: (6, {})} | custom-call | flops 1572864 | bytes 6291456 | tf_op jit(solution)/shard_map/pallas_call | solution.py:319
  (8 shorter events, 0.1 us)
Async XLA Ops:
  5.0 8.5 %copy-start = (bf16[1,2,4096]{2,1,0:T(2,128)(2,1)S(1)}, bf16[1,2,4096]{2,1,0:T(2,128)(2,1)}, u32[]{:S(2)}) copy-start(bf16[1,2,4096]{2,1,0:T(2,128)(2,1)} %param.15) | copy-start | bytes 49156
  5.0 62.1 %all-to-all-start.2 = ((bf16[32,512,128]{2,1,0:T(8,128)(2,1)}), bf16[32,512,128]{2,1,0:T(8,128)(2,1)}, u32[]{:S(2)}, u32[]{:S(2)}) async-start(bf16[32,512,128]{2,1,0:T(8,128)(2,1)} %get-tuple-element.20), calls=%async_computation.2 | async-start | bytes 8388608 | tf_op jit(solution)/shard_map/all_to_all | solution.py:336
  13.5 45.6 %collective-permute-start.3 = (bf16[2,4096]{1,0:T(2,128)(2,1)S(1)}, bf16[2,4096]{1,0:T(2,128)(2,1)S(1)}, u32[]{:S(2)}, u32[]{:S(2)}) collective-permute-start(bf16[2,4096]{1,0:T(2,128)(2,1)S(1)} %bitcast.25), channel_id=1, source_target_pairs={{0,64},{64,0},{1,65},{65,1},{2,66},{66,2},{3,67},{67,3},{4,68},{68... | collective-permute-start | bytes 49160 | tf_op jit(solution)/shard_map/ppermute | solution.py:398
  67.1 58.5 %all-to-all-start = ((bf16[32,512,128]{2,1,0:T(8,128)(2,1)}), bf16[32,512,128]{2,1,0:T(8,128)(2,1)}, u32[]{:S(2)}, u32[]{:S(2)}) async-start(bf16[32,512,128]{2,1,0:T(8,128)(2,1)} %get-tuple-element.17), calls=%async_computation | async-start | bytes 8388608 | tf_op jit(solution)/shard_map/all_to_all | solution.py:336
  125.6 47.4 %all-to-all-start.3 = ((bf16[32,400,128]{2,1,0:T(8,128)(2,1)}), bf16[32,400,128]{2,1,0:T(8,128)(2,1)S(1)}, u32[]{:S(2)}, u32[]{:S(2)}) async-start(bf16[32,400,128]{2,1,0:T(8,128)(2,1)} %bitcast.24), calls=%async_computation.3 | async-start | bytes 6553600 | tf_op jit(solution)/shard_map/all_to_all | solution.py:336
  173.0 5.0 %copy-start.1 = (f32[2,2]{1,0:T(2,128)S(1)}, f32[2,2]{1,0:T(2,128)}, u32[]{:S(2)}) copy-start(f32[2,2]{1,0:T(2,128)} %param.16) | copy-start | bytes 52
  173.0 5.0 %copy-start.3 = (s32[2,1]{0,1:T(1,128)S(1)}, s32[2,1]{0,1:T(1,128)}, u32[]{:S(2)}) copy-start(s32[2,1]{0,1:T(1,128)} %param.19) | copy-start | bytes 28
  173.0 5.1 %copy-start.2 = (s32[2,2]{1,0:T(2,128)S(1)}, s32[2,2]{1,0:T(2,128)}, u32[]{:S(2)}) copy-start(s32[2,2]{1,0:T(2,128)} %param.17) | copy-start | bytes 52
  173.0 48.3 %all-to-all-start.1 = ((bf16[32,400,128]{2,1,0:T(8,128)(2,1)}), bf16[32,400,128]{2,1,0:T(8,128)(2,1)}, u32[]{:S(2)}, u32[]{:S(2)}) async-start(bf16[32,400,128]{2,1,0:T(8,128)(2,1)} %bitcast.23), calls=%async_computation.1 | async-start | bytes 6553600 | tf_op jit(solution)/shard_map/all_to_all | solution.py:336
  178.2 5.3 %collective-permute-start.1 = (f32[3,4]{1,0:T(4,128)S(1)}, f32[3,4]{1,0:T(4,128)S(1)}, u32[]{:S(2)}, u32[]{:S(2)}) collective-permute-start(f32[3,4]{1,0:T(4,128)S(1)} %pad_maximum_fusion), channel_id=1, source_target_pairs={{0,32},{16,48},{32,0},{48,16},{1,33},{17,49},{33,1},{49,17},{2,34}... | collective-permute-start | bytes 152 | tf_op jit(solution)/shard_map/ppermute | solution.py:343
  181.5 3.6 %collective-permute-start.2 = (f32[3,4]{1,0:T(4,128)S(1)}, f32[3,4]{1,0:T(4,128)S(1)}, u32[]{:S(2)}, u32[]{:S(2)}) collective-permute-start(f32[3,4]{1,0:T(4,128)S(1)} %pad_maximum_fusion), channel_id=1, source_target_pairs={{0,48},{16,0},{32,16},{48,32},{1,49},{17,1},{33,17},{49,33},{2,50}... | collective-permute-start | bytes 152 | tf_op jit(solution)/shard_map/ppermute | solution.py:343
  182.5 4.8 %collective-permute-start = (f32[3,4]{1,0:T(4,128)S(1)}, f32[3,4]{1,0:T(4,128)S(1)}, u32[]{:S(2)}, u32[]{:S(2)}) collective-permute-start(f32[3,4]{1,0:T(4,128)S(1)} %pad_maximum_fusion), channel_id=1, source_target_pairs={{0,16},{16,32},{32,48},{48,0},{1,17},{17,33},{33,49},{49,1},{2,18}... | collective-permute-start | bytes 152 | tf_op jit(solution)/shard_map/ppermute | solution.py:343
